TPU v7x, 128 devices: a whole 4x4x4 slice. The times are simulated.
128 devices in a mesh: row: 16 (over z, x), col: 8 (over y, core).
Axes of the slice: x: 4, y: 4, z: 4, core: 2. Of those that a mesh axis runs over, the one named last changes fastest.
Arguments:
- template_pair: bfloat16 [4, 64, 1024, 1024], P(None, None, 'row', 'col'), may hold values from -6 to 6
- template_feat: bfloat16 [128, 64, 128], P(('row', 'col')), may hold values from -6 to 6
- block_map: int32 [4, 8], replicated, may hold values from 0 to 127
- block_count: int32 [4, 8], replicated, may hold values from 1 to 128
- residue_mask: int32 [4, 1024], replicated, may hold values 0 or 1
- row_embed: bfloat16 [64, 64], replicated, may hold values from -0.75 to 0.75
- col_embed: bfloat16 [64, 64], replicated, may hold values from -0.75 to 0.75
- norm_gain: bfloat16 [64], replicated, may hold values from 0.25 to 1.75
- left_proj: bfloat16 [64, 64], replicated, may hold values from -0.75 to 0.75
- right_proj: bfloat16 [64, 64], replicated, may hold values from -0.75 to 0.75
- gate_proj: bfloat16 [64, 64], replicated, may hold values from -0.75 to 0.75
- out_proj: bfloat16 [64, 64], replicated, may hold values from -0.75 to 0.75
- embed_grad: bfloat16 [64, 1024, 1024], P(None, 'row', 'col'), may hold values from -0.29882812 to 0.29882812
Outputs:
- embedding: bfloat16 [64, 1024, 1024], P(None, 'row', 'col')
- feat_grad: float32 [128, 64, 128], P(('row', 'col'))
All inputs are finite; a program needn't handle non-finite values.
Results may differ from a plain program's by a relative error of at most 0.013.
Values may be sent and summed in bfloat16 or wider, within the bound.
No kernel may reach another device: no remote copies, remote signals or barrier semaphores. Data moves between devices by JAX's collectives and lax.ppermute only.
A program may use at most 192 MiB of HBM per device.

v0:
```python
import jax
import jax.numpy as jnp
from jax import lax
from jax.sharding import PartitionSpec as P

EPS = 1e-05
HIGHEST = lax.Precision.HIGHEST


def normalize(values, axis):
    center = jnp.mean(values, axis=axis, keepdims=True)
    shifted = values - center
    inverse = lax.rsqrt(jnp.mean(shifted * shifted, axis=axis, keepdims=True) + EPS)
    return (shifted * inverse, inverse)


def normalize_back(grad_hat, normed, inverse, axis):
    first_mean = jnp.mean(grad_hat, axis=axis, keepdims=True)
    second_mean = jnp.mean(grad_hat * normed, axis=axis, keepdims=True)
    return (grad_hat - first_mean - normed * second_mean) * inverse


def project(weight, values):
    return jnp.einsum("dc,tdij->tcij", weight, values, preferred_element_type=jnp.float32)


def project_back(weight, values):
    return jnp.einsum("dc,tcij->tdij", weight, values, preferred_element_type=jnp.float32)


def spread_pairs(values, row_count, col_count):
    slices, _, height_dev, width_dev = values.shape
    shaped = values.reshape(slices, row_count, col_count, height_dev, width_dev)
    return shaped.transpose(0, 1, 3, 2, 4).reshape(
        slices, row_count * height_dev, col_count * width_dev
    )


def split_pairs(values, row_count, col_count):
    slices, height_all, width_all = values.shape
    shaped = values.reshape(
        slices, row_count, height_all // row_count, col_count, width_all // col_count
    )
    return shaped.transpose(1, 3, 0, 2, 4).reshape(
        row_count * col_count, slices, height_all // row_count, width_all // col_count
    )


def pick_rows(shard_part, block_ids, offsets):
    block_total = shard_part.shape[0]
    choose = (block_ids[:, :, None] == jnp.arange(block_total, dtype=jnp.int32)).astype(
        shard_part.dtype
    )
    columns = jnp.take(shard_part, offsets, axis=2)
    return jnp.einsum("tlb,bfl->tfl", choose, columns, preferred_element_type=jnp.float32)


def scatter_terms(block_total, block_ids, offsets, grads, block_width):
    choose = (block_ids[:, :, None] == jnp.arange(block_total, dtype=jnp.int32)).astype(jnp.float32)
    placing = (offsets[:, None] == jnp.arange(block_width, dtype=jnp.int32)[None, :]).astype(
        jnp.float32
    )
    gathered = jnp.einsum("tlb,tfl->bfl", choose, grads, precision=HIGHEST)
    return jnp.einsum("bfl,lp->bfp", gathered, placing, precision=HIGHEST)


def per_device(
    template_pair,
    template_feat,
    block_map,
    block_count,
    residue_mask,
    row_embed,
    col_embed,
    norm_gain,
    left_proj,
    right_proj,
    gate_proj,
    out_proj,
    embed_grad,
):
    row_count = lax.axis_size("row")
    col_count = lax.axis_size("col")
    templates, channels, height_dev, width_dev = template_pair.shape
    block_width = template_feat.shape[2]
    slice_total = templates * channels
    row_ids = lax.axis_index("row") * height_dev + jnp.arange(height_dev, dtype=jnp.int32)
    col_ids = lax.axis_index("col") * width_dev + jnp.arange(width_dev, dtype=jnp.int32)

    def residue_info(residues):
        query_block = residues // block_width
        offsets = residues % block_width
        block_ids = jnp.take(block_map, query_block, axis=1)
        limits = jnp.take(block_count, query_block, axis=1)
        marks = jnp.take(residue_mask, residues, axis=1)
        valid = ((offsets[None, :] < limits) & (marks == 1)).astype(jnp.float32)
        return (block_ids, offsets, valid)

    row_blocks, row_offsets, row_valid = residue_info(row_ids)
    col_blocks, col_offsets, col_valid = residue_info(col_ids)
    shard_part = lax.all_gather(template_feat, ("row", "col"), axis=0, tiled=True)
    fetched_rows = pick_rows(shard_part, row_blocks, row_offsets)
    fetched_cols = pick_rows(shard_part, col_blocks, col_offsets)
    feat_rows = (fetched_rows * row_valid[:, None, :]).astype(jnp.bfloat16)
    feat_cols = (fetched_cols * col_valid[:, None, :]).astype(jnp.bfloat16)
    left_terms = jnp.einsum("fc,tfi->tci", row_embed, feat_rows, preferred_element_type=jnp.float32)
    right_terms = jnp.einsum(
        "fc,tfj->tcj", col_embed, feat_cols, preferred_element_type=jnp.float32
    )
    pair = (
        template_pair.astype(jnp.float32) + left_terms[:, :, :, None] + right_terms[:, :, None, :]
    )
    normed, inverse = normalize(pair, 1)
    gain = norm_gain.astype(jnp.float32)[None, :, None, None]
    scaled = (normed * gain).astype(jnp.bfloat16)
    left_pair = project(left_proj, scaled).astype(jnp.bfloat16)
    right_pair = project(right_proj, scaled).astype(jnp.bfloat16)
    gate = jax.nn.sigmoid(project(gate_proj, scaled))
    flat_left = left_pair.reshape(slice_total, height_dev, width_dev)
    flat_right = right_pair.reshape(slice_total, height_dev, width_dev)
    sent_left, sent_right = (
        lax.all_to_all(flat_left[:, None], ("row", "col"), split_axis=0, concat_axis=1, tiled=True),
        lax.all_to_all(
            flat_right[:, None], ("row", "col"), split_axis=0, concat_axis=1, tiled=True
        ),
    )
    wide_left = spread_pairs(sent_left, row_count, col_count)
    wide_right = spread_pairs(sent_right, row_count, col_count)
    wide_product = jnp.einsum(
        "sik,sjk->sij", wide_left, wide_right, preferred_element_type=jnp.float32
    ).astype(jnp.bfloat16)
    returned = lax.all_to_all(
        split_pairs(wide_product, row_count, col_count),
        ("row", "col"),
        split_axis=0,
        concat_axis=1,
        tiled=True,
    )
    product = returned.reshape(slice_total, height_dev, width_dev)
    product = product.reshape(templates, channels, height_dev, width_dev)
    prod_norm, prod_inv = normalize(product.astype(jnp.float32), 1)
    projected = project(out_proj, prod_norm.astype(jnp.bfloat16))
    output_sum = jnp.sum(pair + gate * projected, axis=0)
    embedding = (output_sum / templates).astype(jnp.bfloat16)
    grad_out = embed_grad.astype(jnp.float32)[None] / templates
    grad_proj = (grad_out * gate).astype(jnp.bfloat16)
    grad_gate = (grad_out * projected * gate * (1.0 - gate)).astype(jnp.bfloat16)
    grad_norm = project_back(out_proj, grad_proj)
    grad_prod = normalize_back(grad_norm, prod_norm, prod_inv, 1).astype(jnp.bfloat16)
    flat_grad = grad_prod.reshape(slice_total, height_dev, width_dev)
    sent_grad = lax.all_to_all(
        flat_grad[:, None], ("row", "col"), split_axis=0, concat_axis=1, tiled=True
    )
    wide_grad = spread_pairs(sent_grad, row_count, col_count)
    wide_gleft = jnp.einsum(
        "sij,sjk->sik", wide_grad, wide_right, preferred_element_type=jnp.float32
    ).astype(jnp.bfloat16)
    wide_gright = jnp.einsum(
        "sij,sik->sjk", wide_grad, wide_left, preferred_element_type=jnp.float32
    ).astype(jnp.bfloat16)
    back_left, back_right = (
        lax.all_to_all(
            split_pairs(wide_gleft, row_count, col_count),
            ("row", "col"),
            split_axis=0,
            concat_axis=1,
            tiled=True,
        ),
        lax.all_to_all(
            split_pairs(wide_gright, row_count, col_count),
            ("row", "col"),
            split_axis=0,
            concat_axis=1,
            tiled=True,
        ),
    )
    grad_left = back_left.reshape(slice_total, height_dev, width_dev)
    grad_right = back_right.reshape(slice_total, height_dev, width_dev)
    grad_left = grad_left.reshape(templates, channels, height_dev, width_dev)
    grad_right = grad_right.reshape(templates, channels, height_dev, width_dev)
    grad_scaled = (
        project_back(left_proj, grad_left)
        + project_back(right_proj, grad_right)
        + project_back(gate_proj, grad_gate)
    )
    grad_pair = grad_out + normalize_back(grad_scaled * gain, normed, inverse, 1)
    row_sums = jnp.sum(grad_pair, axis=3)
    col_sums = jnp.sum(grad_pair, axis=2)
    row_weight = row_embed.astype(jnp.float32)
    col_weight = col_embed.astype(jnp.float32)
    grad_rows = (
        jnp.einsum("fc,tci->tfi", row_weight, row_sums, precision=HIGHEST) * row_valid[:, None, :]
    )
    grad_cols = (
        jnp.einsum("fc,tcj->tfj", col_weight, col_sums, precision=HIGHEST) * col_valid[:, None, :]
    )
    block_total = lax.axis_size(("row", "col")) * template_feat.shape[0]
    feat_grad = lax.psum_scatter(
        scatter_terms(block_total, row_blocks, row_offsets, grad_rows, block_width)
        + scatter_terms(block_total, col_blocks, col_offsets, grad_cols, block_width),
        ("row", "col"),
        scatter_dimension=0,
        tiled=True,
    )
    return (embedding, feat_grad)


def solution(mesh):
    return jax.shard_map(
        per_device,
        mesh=mesh,
        in_specs=(
            P(None, None, "row", "col"),
            P(("row", "col"), None, None),
            P(),
            P(),
            P(),
            P(),
            P(),
            P(),
            P(),
            P(),
            P(),
            P(),
            P(None, "row", "col"),
        ),
        out_specs=(P(None, "row", "col"), P(("row", "col"), None, None)),
        check_vma=False,
    )
```

profile of v0, /device:TPU:1, one launch (start us, length us, event | category | flops | bytes accessed | tf_op | source)
XLA Modules:
  0.0 1279.9 jit_solution(8572631330061487603)
XLA Ops:
  15.7 64.5 %all-gather.2.cloned.1.call-done = bf16[128,64,128]{2,1,0:T(8,128)(2,1)} async-done(((bf16[1,64,128]{2,1,0:T(8,128)(2,1)}), bf16[128,64,128]{2,1,0:T(8,128)(2,1)}) %all-gather.2.cloned.1.call-update) | async-done | bytes 2097168 | tf_op jit(solution)/shard_map/all_gather | solution.py:101
  91.0 5.6 fusion.16
  100.3 10.7 convert_bitcast_fusion
  115.6 16.0 %all-to-all-start.1 = ((bf16[256,1,64,128]{3,2,1,0:T(8,128)(2,1)}), bf16[256,1,64,128]{3,2,1,0:T(8,128)(2,1)}, u32[]{:S(2)}, u32[]{:S(2)}) async-start(bf16[256,1,64,128]{3,2,1,0:T(8,128)(2,1)} %bitcast.256), calls=%async_computation.1 | async-start | bytes 8388608 | tf_op jit(solution)/shard_map/all_to_all | solution.py:123
  131.7 6.0 convert_bitcast_fusion.1
  142.4 41.9 %all-to-all-done.1 = bf16[256,1,64,128]{3,2,1,0:T(8,128)(2,1)} async-done(((bf16[256,1,64,128]{3,2,1,0:T(8,128)(2,1)}), bf16[256,1,64,128]{3,2,1,0:T(8,128)(2,1)}, u32[]{:S(2)}, u32[]{:S(2)}) %all-to-all-start.1) | async-done | bytes 4194336 | tf_op jit(solution)/shard_map/all_to_all | solution.py:123
  189.7 12.2 copy.229
  202.0 7.5 reshape.295
  209.5 33.2 %all-to-all-done = bf16[256,1,64,128]{3,2,1,0:T(8,128)(2,1)} async-done(((bf16[256,1,64,128]{3,2,1,0:T(8,128)(2,1)}), bf16[256,1,64,128]{3,2,1,0:T(8,128)(2,1)}, u32[]{:S(2)}, u32[]{:S(2)}) %all-to-all-start) | async-done | bytes 4194336 | tf_op jit(solution)/shard_map/all_to_all | solution.py:122
  242.7 12.3 copy.224
  255.0 7.7 reshape.293
  262.6 8.0 convolution_convert_fusion.2
  274.9 5.7 all-to-all-start.2
  282.7 8.7 add_divide_fusion
  291.4 42.1 %all-to-all-done.2 = bf16[128,2,64,128]{3,2,1,0:T(8,128)(2,1)} async-done(((bf16[128,2,64,128]{3,2,1,0:T(8,128)(2,1)}), bf16[128,2,64,128]{3,2,1,0:T(8,128)(2,1)}, u32[]{:S(2)}, u32[]{:S(2)}) %all-to-all-start.2) | async-done | bytes 4194336 | tf_op jit(solution)/shard_map/all_to_all | solution.py:132
  348.1 15.7 %bitcast_reduce_fusion.1 = (f32[4,64,128]{2,1,0:T(8,128)S(1)}, f32[4,64,128]{2,1,0:T(8,128)}, f32[4,64,128,64]{2,3,1,0:T(8,128)}) fusion(f32[4,64,128]{2,1,0:T(8,128)S(1)} %add_rsqrt_fusion, f32[4,64,128]{2,1,0:T(8,128)S(1)} %broadcast_multiply_fusion.4, f32[4,64,64,128]{3,2,1,0:T(8,128)S(1)} %bitcast_convert_fusion, f32[4,64,128,64]{2,3,1,0:T(8,128)S(1)} %bitcast.251, ...), kind=kOutput, calls=%fused_computation.17 | convolution fusion | flops 283049984 | bytes 27795456 | tf_op jit(solution)/shard_map/dc,tcij->tdij/dot_general | solution.py:28
  364.7 8.7 fusion.6
  376.1 57.3 %all_to_all.72 = bf16[256,1,64,128]{3,2,1,0:T(8,128)(2,1)S(1)} all-to-all(bf16[256,1,64,128]{3,2,1,0:T(8,128)(2,1)S(1)} %bitcast.259), channel_id=1, replica_groups=mesh['row'=16,'col'=8] {'row','col'}, dimensions={0} | all-to-all | bytes 8388608 | tf_op jit(solution)/shard_map/all_to_all | solution.py:151
  433.5 10.1 copy.237
  443.6 7.4 reshape.299
  451.0 8.0 convolution_convert_fusion
  468.8 8.0 convolution_convert_fusion.1
  481.0 40.7 %all-to-all-done.5 = bf16[128,2,64,128]{3,2,1,0:T(8,128)(2,1)} async-done(((bf16[128,2,64,128]{3,2,1,0:T(8,128)(2,1)}), bf16[128,2,64,128]{3,2,1,0:T(8,128)(2,1)}, u32[]{:S(2)}, u32[]{:S(2)}) %all-to-all-start.5) | async-done | bytes 4194336 | tf_op jit(solution)/shard_map/all_to_all | solution.py:169
  527.4 9.2 fusion.19
  536.6 11.5 fusion.23
  548.2 8.7 fusion.27
  556.9 23.4 %all-to-all-done.4 = bf16[128,2,64,128]{3,2,1,0:T(8,128)(2,1)} async-done(((bf16[128,2,64,128]{3,2,1,0:T(8,128)(2,1)}), bf16[128,2,64,128]{3,2,1,0:T(8,128)(2,1)}, u32[]{:S(2)}, u32[]{:S(2)}) %all-to-all-start.4) | async-done | bytes 4194336 | tf_op jit(solution)/shard_map/all_to_all | solution.py:162
  580.3 21.6 %bitcast_reduce_fusion = (f32[4,64,128]{2,1,0:T(8,128)S(1)}, f32[4,64,128]{2,1,0:T(8,128)S(1)}, f32[64,64,128]{2,0,1:T(8,128)}, f32[4,64,128,64]{2,3,1,0:T(8,128)S(1)}) fusion(f32[4,64,128]{2,1,0:T(8,128)S(1)} %add_rsqrt_fusion.1, f32[4,64,128]{2,1,0:T(8,128)S(1)} %broadcast_multiply_fusion.5, f32[4,64,128]{2,1,0:T(8,128)S(1)} %convolution_bitcast_fusion.3, ...), kind=kOutput, calls=%fused_computation.10 | convolution fusion | flops 297205760 | bytes 53158144 | tf_op jit(solution)/shard_map/dc,tcij->tdij/dot_general | solution.py:28
  602.0 14.1 %fusion.98 = (f32[4,64,128]{2,1,0:T(8,128)S(1)}, f32[4,64,64]{1,2,0:T(8,128)S(1)}) fusion(f32[4,64,128]{2,1,0:T(8,128)S(1)} %broadcast_multiply_fusion, f32[4,64,128]{2,1,0:T(8,128)S(1)} %add_rsqrt_fusion.1, f32[4,64,128]{2,1,0:T(8,128)S(1)} %broadcast_multiply_fusion.5, f32[4,64,128]{2,1,0:T(8,128)S(1)} %convolution_bitcast_fusion.3, ...), kind=kLoop, calls=%fused_computation.191 | loop fusion | flops 25116672 | bytes 15597568 | tf_op jit(solution)/shard_map/reduce_sum | solution.py:188
  618.3 6.2 fusion.43
  628.6 8.5 fusion.38
  643.4 629.5 %reduce-scatter.2.cloned.1.call-done = f32[1,64,128]{2,1,0:T(8,128)} async-done(((f32[128,64,128]{2,1,0:T(8,128)}), f32[1,64,128]{2,1,0:T(8,128)}) %reduce-scatter.2.cloned.1.call-update) | async-done | bytes 32784 | tf_op jit(solution)/shard_map/reduce_scatter | solution.py:198
  (142 shorter events, 93.8 us)
Async XLA Ops:
  7.2 124.5 %copy-start = (bf16[64,64]{1,0:T(8,128)(2,1)S(1)}, bf16[64,64]{1,0:T(8,128)(2,1)}, u32[]{:S(2)}) copy-start(bf16[64,64]{1,0:T(8,128)(2,1)} %param.25) | copy-start | bytes 24580
  7.2 73.0 %all-gather.2.cloned.1.call-start = ((), (), s32[]{:S(2)}) async-start(), calls=%async_computation.7 | async-start | bytes 2113536 | tf_op jit(solution)/shard_map/all_gather | solution.py:101
  9.4 80.4 %copy-start.23 = (s32[128]{0:T(128)}, s32[128]{0:T(128)S(1)}, u32[]{:S(2)}) copy-start(s32[128]{0:T(128)S(1)} %get-tuple-element.26) | copy-start | bytes 1540
  10.8 4.6 copy-start.25
  14.6 71.6 %copy-start.19 = (f32[4,64]{1,0:T(4,128)}, f32[4,64]{1,0:T(4,128)S(1)}, u32[]{:S(2)}) copy-start(f32[4,64]{1,0:T(4,128)S(1)} %fusion.85) | copy-start | bytes 3076
  15.5 75.3 %copy-start.17 = (f32[4,128]{1,0:T(4,128)}, f32[4,128]{1,0:T(4,128)S(1)}, u32[]{:S(2)}) copy-start(f32[4,128]{1,0:T(4,128)S(1)} %fusion.88) | copy-start | bytes 6148
  15.5 74.4 %copy-start.10 = (s32[4,64]{0,1:T(8,128)}, s32[4,64]{0,1:T(8,128)S(1)}, u32[]{:S(2)}) copy-start(s32[4,64]{0,1:T(8,128)S(1)} %select_bitcast_fusion.1) | copy-start | bytes 3076
  15.6 73.3 %copy-start.8 = (s32[4,128]{0,1:T(8,128)}, s32[4,128]{0,1:T(8,128)S(1)}, u32[]{:S(2)}) copy-start(s32[4,128]{0,1:T(8,128)S(1)} %select_bitcast_fusion) | copy-start | bytes 6148
  84.0 6.7 copy-start.14
  84.0 6.8 copy-start.12
  89.1 11.1 copy-start.22
  89.9 6.8 copy-start.3
  115.6 68.7 %all-to-all-start.1 = ((bf16[256,1,64,128]{3,2,1,0:T(8,128)(2,1)}), bf16[256,1,64,128]{3,2,1,0:T(8,128)(2,1)}, u32[]{:S(2)}, u32[]{:S(2)}) async-start(bf16[256,1,64,128]{3,2,1,0:T(8,128)(2,1)} %bitcast.256), calls=%async_computation.1 | async-start | bytes 8388608 | tf_op jit(solution)/shard_map/all_to_all | solution.py:123
  184.3 58.3 %all-to-all-start = ((bf16[256,1,64,128]{3,2,1,0:T(8,128)(2,1)}), bf16[256,1,64,128]{3,2,1,0:T(8,128)(2,1)}, u32[]{:S(2)}, u32[]{:S(2)}) async-start(bf16[256,1,64,128]{3,2,1,0:T(8,128)(2,1)} %bitcast.254), calls=%async_computation | async-start | bytes 8388608 | tf_op jit(solution)/shard_map/all_to_all | solution.py:122
  271.7 9.0 copy-start.7
  271.8 11.0 copy-start.21
  274.9 58.5 %all-to-all-start.2 = ((bf16[128,2,64,128]{3,2,1,0:T(8,128)(2,1)}), bf16[128,2,64,128]{3,2,1,0:T(8,128)(2,1)}, u32[]{:S(2)}, u32[]{:S(2)}) async-start(bf16[128,2,64,128]{3,2,1,0:T(8,128)(2,1)} %bitcast.257), calls=%async_computation.2 | async-start | bytes 8388608 | tf_op jit(solution)/shard_map/all_to_all | solution.py:132
  348.1 16.6 %copy-start.1 = (f32[4,64,64,128]{3,2,1,0:T(8,128)}, f32[4,64,64,128]{3,2,1,0:T(8,128)S(1)}, u32[]{:S(2)}) copy-start(f32[4,64,64,128]{3,2,1,0:T(8,128)S(1)} %bitcast_convert_fusion) | copy-start | bytes 25165828
  463.4 58.3 %all-to-all-start.5 = ((bf16[128,2,64,128]{3,2,1,0:T(8,128)(2,1)}), bf16[128,2,64,128]{3,2,1,0:T(8,128)(2,1)}, u32[]{:S(2)}, u32[]{:S(2)}) async-start(bf16[128,2,64,128]{3,2,1,0:T(8,128)(2,1)} %bitcast.255), calls=%async_computation.5 | async-start | bytes 8388608 | tf_op jit(solution)/shard_map/all_to_all | solution.py:169
  521.7 58.6 %all-to-all-start.4 = ((bf16[128,2,64,128]{3,2,1,0:T(8,128)(2,1)}), bf16[128,2,64,128]{3,2,1,0:T(8,128)(2,1)}, u32[]{:S(2)}, u32[]{:S(2)}) async-start(bf16[128,2,64,128]{3,2,1,0:T(8,128)(2,1)} %bitcast.253), calls=%async_computation.4 | async-start | bytes 8388608 | tf_op jit(solution)/shard_map/all_to_all | solution.py:162
  527.3 9.3 copy-start.5
  527.3 745.6 %reduce-scatter.2.cloned.1.call-start = ((), (), s32[]{:S(2)}) async-start(), calls=%async_computation.8 | async-start | bytes 4227072 | tf_op jit(solution)/shard_map/reduce_scatter | solution.py:198
  536.6 11.5 copy-start.2
  580.3 21.6 %copy-start.4 = (bf16[4,64,64,128]{3,2,1,0:T(8,128)(2,1)S(1)}, bf16[4,64,64,128]{3,2,1,0:T(8,128)(2,1)}, u32[]{:S(2)}) copy-start(bf16[4,64,64,128]{3,2,1,0:T(8,128)(2,1)} %param.17) | copy-start | bytes 12582916
  601.9 14.2 %copy-start.15 = (bf16[64,64]{1,0:T(8,128)(2,1)S(1)}, bf16[64,64]{1,0:T(8,128)(2,1)}, u32[]{:S(2)}) copy-start(bf16[64,64]{1,0:T(8,128)(2,1)} %param.22) | copy-start | bytes 24580
  601.9 14.2 %copy-start.20 = (f32[4,64]{1,0:T(4,128)S(1)}, f32[4,64]{1,0:T(4,128)}, u32[]{:S(2)}) copy-start(f32[4,64]{1,0:T(4,128)} %copy-done.19) | copy-start | bytes 3076
  601.9 14.5 %copy-start.11 = (s32[4,64]{0,1:T(8,128)S(1)}, s32[4,64]{0,1:T(8,128)}, u32[]{:S(2)}) copy-start(s32[4,64]{0,1:T(8,128)} %copy-done.10) | copy-start | bytes 3076
  601.9 16.3 %copy-start.26 = (s32[64]{0:T(128)S(1)}, s32[64]{0:T(128)}, u32[]{:S(2)}) copy-start(s32[64]{0:T(128)} %copy-done.25) | copy-start | bytes 772
  601.9 22.6 %copy-start.13 = (bf16[64,64]{1,0:T(8,128)(2,1)S(1)}, bf16[64,64]{1,0:T(8,128)(2,1)}, u32[]{:S(2)}) copy-start(bf16[64,64]{1,0:T(8,128)(2,1)} %param.23) | copy-start | bytes 24580
  602.0 22.6 %copy-start.18 = (f32[4,128]{1,0:T(4,128)S(1)}, f32[4,128]{1,0:T(4,128)}, u32[]{:S(2)}) copy-start(f32[4,128]{1,0:T(4,128)} %copy-done.17) | copy-start | bytes 6148
  616.1 8.8 copy-start.9
  616.1 12.4 copy-start.24
  (4 other events, 16.4 us)
Sparse Core Ops, SparseCore 0:
  11.2 68.9 all-gather.1
  641.6 631.2 reduce-scatter.1
where the time goes:
time: 1300 us; the launch traced here: 1280 us
  waiting for transfers between devices  876 us (67%)
  matrix products  141 us (11%)
  local copies, waits for them, and re-layouts  103 us (8%)
  blocking collectives  57.3 us (4%)
  other arithmetic  49.2 us (4%)
  starting transfers between devices  38.2 us (3%)
  between operations  15.1 us (1%)
    reduce_scatter x1, waiting for transfers between devices, per_device(): lax.psum_scatter(scatter_terms(block_total, row_blocks, row_offsets, grad...  630 us
    all_gather x1, waiting for transfers between devices, per_device(): lax.all_gather(template_feat, ('row', 'col'), axis=0, tiled=True)  64.5 us
    dot_general x4, matrix products, project_back(): jnp.einsum('dc,tcij->tdij', weight, values, preferred_element_type=jnp.fl...  57.5 us
    all_to_all x1, blocking collectives, per_device(): lax.all_to_all(flat_grad[:, None], ('row', 'col'), split_axis=0, concat_a...  57.3 us
    all_to_all x1, waiting for transfers between devices, per_device(): lax.all_to_all(split_pairs(wide_product, row_count, col_count), ('row', '...  42.1 us
    all_to_all x1, waiting for transfers between devices, per_device(): lax.all_to_all(flat_right[:, None], ('row', 'col'), split_axis=0, concat_...  41.9 us
    all_to_all x1, waiting for transfers between devices, per_device(): lax.all_to_all(split_pairs(wide_gright, row_count, col_count), ('row', 'c...  40.7 us
    dot_general x4, matrix products, project(): jnp.einsum('dc,tdij->tcij', weight, values, preferred_element_type=jnp.fl...  34.7 us
  transfers between devices with their start and end apart: 7, of which 7 were waited for; matrix products, arithmetic and copies ran while one was open for 7% of the time, Pallas kernels for 0%

commit v1 on v0

v1 whole, which is shorter than its diff:
```python
import jax
import jax.numpy as jnp
import numpy as np
from jax import lax
from jax.experimental import pallas as pl
from jax.experimental.pallas import tpu as pltpu
from jax.sharding import PartitionSpec as P

EPS = 1e-05
HIGHEST = lax.Precision.HIGHEST
F32 = jnp.float32
BF = jnp.bfloat16
AXES = ("row", "col")
VMEM = 60 * 2**20

C = 64
T = 4
H = 64
W = 128
N = 1024
K8 = C * 8
ROWS = 288


def params():
    return pltpu.CompilerParams(vmem_limit_bytes=VMEM)


def stack_rows(top, bottom):
    return jnp.concatenate([top.reshape(K8, W), bottom.reshape(K8, W)], axis=1)


def unstack_rows(wide):
    return wide[:, :W].reshape(C, 8, W), wide[:, W:].reshape(C, 8, W)


def join_rows(top, bottom):
    return jnp.concatenate([top, bottom], axis=1)


def norm_kernel(
    pair_ref, left_ref, right_ref, gain_ref, kl_ref, kr_ref, pay_ref, scaled_ref, inv_ref, sum_ref
):
    step = pl.program_id(0)
    right = right_ref[0]
    for g in range(4):
        rows = slice(g * 16, g * 16 + 16)
        pairs, scaleds, invs = [], [], []
        for part in range(2):
            first = g * 16 + part * 8
            raw = pair_ref[0, :, rows, :].astype(F32)[:, part * 8 : part * 8 + 8, :]
            lane = 2 * g + part
            left = jnp.broadcast_to(left_ref[0, :, lane : lane + 1], (K8, W)).reshape(C, 8, W)
            pair = raw + left + right
            center = jnp.sum(pair, axis=0, keepdims=True) * (1.0 / C)
            shifted = pair - center
            inverse = lax.rsqrt(
                jnp.sum(shifted * shifted, axis=0, keepdims=True) * (1.0 / C) + EPS
            )
            inv_ref[0, first : first + 8, :] = inverse[0]
            scaleds.append(shifted * inverse * gain_ref[...])
            invs.append(inverse[0])
            where = (slice(None), slice(first, first + 8), slice(None))

            @pl.when(step == 0)
            def _():
                sum_ref[where] = pair

            @pl.when(step > 0)
            def _():
                sum_ref[where] += pair

        scaled_ref[0, :, rows, :] = join_rows(*scaleds).astype(BF)
        wide = stack_rows(*scaleds).astype(BF)
        for k, weight in enumerate((kl_ref, kr_ref)):
            out = jnp.dot(weight[...], wide, preferred_element_type=F32)
            out = join_rows(*unstack_rows(out)).astype(BF).reshape(C // 2, 2, 16, W)
            for s in range(2):
                first = k * 128 + s * 64 + g * 16
                pay_ref[0, :, first : first + 16, :] = out[:, s]
        both = jnp.concatenate(invs, axis=0).astype(BF)
        first = 256 + (g % 2) * 16
        for q in range(g // 2, C // 2, 2):
            pay_ref[0, q, first : first + 16, :] = both


def run_norm(pair, left, right, gain, kl, kr):
    whole = lambda *shape: pl.BlockSpec(shape, lambda t: (0,) * len(shape))
    return pl.pallas_call(
        norm_kernel,
        grid=(T,),
        in_specs=[
            pl.BlockSpec((1, C, H, W), lambda t: (t, 0, 0, 0)),
            pl.BlockSpec((1, K8, 8), lambda t: (t, 0, 0)),
            pl.BlockSpec((1, C, 8, W), lambda t: (t, 0, 0, 0)),
            whole(C, 8, W),
            whole(K8, K8),
            whole(K8, K8),
        ],
        out_specs=[
            pl.BlockSpec((1, C // 2, ROWS, W), lambda t: (t, 0, 0, 0)),
            pl.BlockSpec((1, C, H, W), lambda t: (t, 0, 0, 0)),
            pl.BlockSpec((1, H, W), lambda t: (t, 0, 0)),
            whole(C, H, W),
        ],
        out_shape=[
            jax.ShapeDtypeStruct((T, C // 2, ROWS, W), BF),
            jax.ShapeDtypeStruct((T, C, H, W), BF),
            jax.ShapeDtypeStruct((T, H, W), F32),
            jax.ShapeDtypeStruct((C, H, W), F32),
        ],
        compiler_params=params(),
        name="pair_norm",
    )(pair, left, right, gain, kl, kr)


def spread(blocks_ref, full_ref):
    @pl.loop(0, 16)
    def _(r):
        for c in range(8):
            full_ref[pl.ds(r * H, H), c * W : (c + 1) * W] = blocks_ref[r * 8 + c]


def product_kernel(left_ref, right_ref, out_ref, left, right):
    spread(left_ref, left)
    spread(right_ref, right)

    @pl.loop(0, 4)
    def _(b):
        out = lax.dot_general(
            left[pl.ds(b * 256, 256), :],
            right[...],
            (((1,), (1,)), ((), ())),
            preferred_element_type=F32,
        ).astype(BF)
        for r in range(4):
            for c in range(8):
                out_ref[(b * 4 + r) * 8 + c] = out[r * H : (r + 1) * H, c * W : (c + 1) * W]


def run_product(factors):
    spec = lambda first: pl.BlockSpec((128, H, W), lambda s: (0, first + s, 0))
    return pl.pallas_call(
        product_kernel,
        grid=(2,),
        in_specs=[spec(0), spec(2)],
        out_specs=pl.BlockSpec((128, H, W), lambda s: (0, s, 0)),
        out_shape=jax.ShapeDtypeStruct((128, 2 * H, W), BF),
        scratch_shapes=[pltpu.VMEM((N, N), BF), pltpu.VMEM((N, N), BF)],
        compiler_params=params(),
        name="triangle_product",
    )(factors, factors)


def gate_kernel(
    prod_ref, scaled_ref, grad_ref, sum_ref, inv_ref, kg_ref, ko_ref, kb_ref, pick_ref,
    emb_ref, out_ref, mean_ref, rows_ref, cols_ref, grows_ref, gcols_ref, total,
):
    step = pl.program_id(0)
    halves = lambda v: (v[:, :8, :], v[:, 8:, :])
    row_sums = jnp.zeros((K8, W), F32)
    col_sums = jnp.zeros((C, 8, W), F32)
    for g in range(4):
        rows = slice(g * 16, g * 16 + 16)
        scaled = stack_rows(*halves(scaled_ref[0, :, rows, :].astype(F32))).astype(BF)
        opened = unstack_rows(jnp.dot(kg_ref[...], scaled, preferred_element_type=F32))
        normed, prod_invs = [], []
        for product in halves(prod_ref[0, :, rows, :].astype(F32)):
            center = jnp.sum(product, axis=0, keepdims=True) * (1.0 / C)
            shifted = product - center
            inverse = lax.rsqrt(
                jnp.sum(shifted * shifted, axis=0, keepdims=True) * (1.0 / C) + EPS
            )
            normed.append(shifted * inverse)
            prod_invs.append(inverse)
        projected = unstack_rows(
            jnp.dot(ko_ref[...], stack_rows(*normed).astype(BF), preferred_element_type=F32)
        )
        grads = halves(grad_ref[:, rows, :].astype(F32))
        grad_projs, weighted = [], []
        for part in range(2):
            first = g * 16 + part * 8
            where = (slice(None), slice(first, first + 8), slice(None))
            gate = jax.nn.sigmoid(opened[part])
            gated = gate * projected[part]

            @pl.when(step == 0)
            def _():
                total[where] = sum_ref[where] + gated

            @pl.when(step > 0)
            def _():
                total[where] += gated

            grad_out = grads[part] * (1.0 / T)
            grad_projs.append(grad_out * gate)
            grad_gate = grad_out * gated * (1.0 - gate)
            mean_ref[0, first : first + 8, :] = jnp.sum(grad_gate * opened[part], axis=0)
            term = grad_gate * inv_ref[0, first : first + 8, :][None]
            col_sums = col_sums + term
            weighted.append(term)
        row_sums = row_sums + jnp.dot(
            stack_rows(*weighted).astype(BF), pick_ref[g], preferred_element_type=F32
        )
        grad_norms = unstack_rows(
            jnp.dot(kb_ref[...], stack_rows(*grad_projs).astype(BF), preferred_element_type=F32)
        )
        outs = []
        for part in range(2):
            grad_norm = grad_norms[part]
            first_mean = jnp.sum(grad_norm, axis=0, keepdims=True) * (1.0 / C)
            second_mean = jnp.sum(grad_norm * normed[part], axis=0, keepdims=True) * (1.0 / C)
            outs.append((grad_norm - first_mean - normed[part] * second_mean) * prod_invs[part])
        out_ref[0, :, rows, :] = join_rows(*outs).astype(BF)
    rows_ref[0] = row_sums
    cols_ref[0] = col_sums.reshape(K8, W)

    @pl.when(step == 0)
    def _():
        grad_rows = jnp.zeros((K8, W), F32)
        grad_cols = jnp.zeros((C, 8, W), F32)
        for g in range(4):
            top, bottom = halves(grad_ref[:, g * 16 : g * 16 + 16, :].astype(F32))
            grad_cols = grad_cols + top + bottom
            grad_rows = grad_rows + jnp.dot(
                stack_rows(top, bottom).astype(BF), pick_ref[g], preferred_element_type=F32
            )
        grows_ref[...] = grad_rows
        gcols_ref[...] = grad_cols.reshape(K8, W)

    @pl.when(step == T - 1)
    def _():
        emb_ref[...] = (total[...] * (1.0 / T)).astype(BF)


def run_gate(prod, scaled, grad, pair_sum, inv, kg, ko, kb, pick):
    whole = lambda *shape: pl.BlockSpec(shape, lambda t: (0,) * len(shape))
    each = lambda *shape: pl.BlockSpec((1, *shape), lambda t: (t,) + (0,) * len(shape))
    return pl.pallas_call(
        gate_kernel,
        grid=(T,),
        in_specs=[
            each(C, H, W), each(C, H, W), whole(C, H, W), whole(C, H, W), each(H, W),
            whole(K8, K8), whole(K8, K8), whole(K8, K8), whole(4, 2 * W, W),
        ],
        out_specs=[
            whole(C, H, W), each(C, H, W), each(H, W), each(K8, W), each(K8, W),
            whole(K8, W), whole(K8, W),
        ],
        out_shape=[
            jax.ShapeDtypeStruct((C, H, W), BF),
            jax.ShapeDtypeStruct((T, C, H, W), BF),
            jax.ShapeDtypeStruct((T, H, W), F32),
            jax.ShapeDtypeStruct((T, K8, W), F32),
            jax.ShapeDtypeStruct((T, K8, W), F32),
            jax.ShapeDtypeStruct((K8, W), F32),
            jax.ShapeDtypeStruct((K8, W), F32),
        ],
        scratch_shapes=[pltpu.VMEM((C, H, W), F32)],
        compiler_params=params(),
        name="gate_and_grad",
    )(prod, scaled, grad, pair_sum, inv, kg, ko, kb, pick)


def factor_kernel(
    left_ref, right_ref, grad_ref, inv_ref, out_ref, sums_ref, left, right, grad, inv, mean
):
    step = pl.program_id(0)
    spread(left_ref, left)
    spread(right_ref, right)
    spread(grad_ref, grad)

    @pl.when(step == 0)
    def _():
        spread(inv_ref, inv)
        mean[...] = jnp.zeros_like(mean)

    sums_ref[...] = jnp.zeros_like(sums_ref)
    ones = jnp.full((8, W), 0.125, F32)

    def finish(value, rows, factor, kind):
        mean[rows, :] += value * factor[rows, :].astype(F32)
        term = value * inv[rows, :].astype(F32)
        sums_ref[0, 2 * kind + 1] += jnp.sum(term.reshape(32, 8, N), axis=0)
        lanes = term[:, :W]
        for c in range(1, 8):
            lanes = lanes + term[:, c * W : (c + 1) * W]
        sums_ref[0, 2 * kind, :, rows] = lax.dot_general(
            ones, lanes, (((1,), (1,)), ((), ())), precision=HIGHEST, preferred_element_type=F32
        )

    for b in range(4):
        rows = slice(b * 256, b * 256 + 256)
        value = jnp.dot(grad[rows, :], right[...], preferred_element_type=F32)
        finish(value, rows, left, 0)
    for b in range(4):
        rows = slice(b * 256, b * 256 + 256)
        value = lax.dot_general(
            grad[:, rows], left[...], (((0,), (0,)), ((), ())), preferred_element_type=F32
        )
        finish(value, rows, right, 1)

    @pl.when(step == 1)
    def _():
        @pl.loop(0, 16)
        def _(r):
            for c in range(8):
                out_ref[r * 8 + c] = mean[pl.ds(r * H, H), c * W : (c + 1) * W].astype(BF)


def run_factor(factors, grad, inv):
    spec = lambda first: pl.BlockSpec((128, H, W), lambda s: (0, first + s, 0))
    return pl.pallas_call(
        factor_kernel,
        grid=(2,),
        in_specs=[spec(0), spec(2), spec(0), pl.BlockSpec((128, H, W), lambda s: (0, 0, 0))],
        out_specs=[
            pl.BlockSpec((128, H, W), lambda s: (0, 0, 0)),
            pl.BlockSpec((1, 4, 8, N), lambda s: (s, 0, 0, 0)),
        ],
        out_shape=[
            jax.ShapeDtypeStruct((128, H, W), BF),
            jax.ShapeDtypeStruct((2, 4, 8, N), F32),
        ],
        scratch_shapes=[
            pltpu.VMEM((N, N), BF),
            pltpu.VMEM((N, N), BF),
            pltpu.VMEM((N, N), BF),
            pltpu.VMEM((N, N), BF),
            pltpu.VMEM((N, N), F32),
        ],
        compiler_params=params(),
        name="factor_grads",
    )(factors, factors, grad, inv)


def close_kernel(recv_ref, mean_ref, inv_ref, scaled_ref, pick_ref, rows_ref, cols_ref):
    got = recv_ref[0].astype(F32)
    total = got[0]
    for k in range(1, 16):
        total = total + got[k]
    weight = (total.reshape(H, W) + mean_ref[0]) * inv_ref[0] * (1.0 / C)
    row_sums = jnp.zeros((K8, W), F32)
    col_sums = jnp.zeros((C, 8, W), F32)
    for g in range(4):
        scaled = scaled_ref[0, :, g * 16 : g * 16 + 16, :].astype(F32)
        terms = []
        for part in range(2):
            first = g * 16 + part * 8
            term = scaled[:, part * 8 : part * 8 + 8, :] * weight[first : first + 8, :][None]
            col_sums = col_sums + term
            terms.append(term)
        row_sums = row_sums + jnp.dot(
            stack_rows(*terms).astype(BF), pick_ref[g], preferred_element_type=F32
        )
    rows_ref[0] = row_sums
    cols_ref[0] = col_sums.reshape(K8, W)


def run_close(recv, mean, inv, scaled, pick):
    each = lambda *shape: pl.BlockSpec((1, *shape), lambda t: (t,) + (0,) * len(shape))
    return pl.pallas_call(
        close_kernel,
        grid=(T,),
        in_specs=[
            each(16, 2, H // 2, W), each(H, W), each(H, W), each(C, H, W),
            pl.BlockSpec((4, 2 * W, W), lambda t: (0, 0, 0)),
        ],
        out_specs=[each(K8, W), each(K8, W)],
        out_shape=[jax.ShapeDtypeStruct((T, K8, W), F32)] * 2,
        compiler_params=params(),
        name="close_sums",
    )(recv, mean, inv, scaled, pick)


def swap_cores(value):
    return lax.ppermute(value, "col", [(i, i ^ 1) for i in range(8)])


def exchange(value):
    return lax.all_to_all(value, AXES, split_axis=0, concat_axis=0, tiled=True)


def in_order(core, mine, other, axis):
    first = jnp.where(core == 0, mine, other)
    second = jnp.where(core == 0, other, mine)
    return jnp.concatenate([first, second], axis=axis)


def lane_rows(sums):
    lead = sums.shape[:-2]
    cut = sums[..., :8].reshape(*lead, C, 8, 8)
    return jnp.swapaxes(cut, -1, -2).reshape(*lead, C, H)


def lane_cols(sums):
    lead = sums.shape[:-2]
    return jnp.sum(sums.reshape(*lead, C, 8, W), axis=-2)


def expand(weights):
    to = jnp.asarray(np.kron(np.eye(C), np.ones((8, 1))), BF)
    tall = jnp.einsum("ac,ncd->nad", to, weights, preferred_element_type=F32).astype(BF)
    wide = jnp.einsum("nad,bd->nab", tall, to, preferred_element_type=F32)
    index = jnp.arange(K8, dtype=jnp.int32) % 8
    return jnp.where(index[:, None] == index[None, :], wide, 0.0).astype(BF)


def per_device(
    template_pair,
    template_feat,
    block_map,
    block_count,
    residue_mask,
    row_embed,
    col_embed,
    norm_gain,
    left_proj,
    right_proj,
    gate_proj,
    out_proj,
    embed_grad,
):
    row = lax.axis_index("row")
    col = lax.axis_index("col")
    core = col % 2
    me = row * 8 + col
    own = me // 32
    pair_at = me % 32
    blocks = jnp.arange(128, dtype=jnp.int32)
    half = row % 2
    row_block = row // 2

    feat_halves = jnp.stack([template_feat[0, :32], template_feat[0, 32:]])
    sent_feat = jnp.broadcast_to(feat_halves[None], (64, 2, 32, W)).reshape(128, 32, W)
    pool = exchange(sent_feat)
    column_ids = lambda m, at: lax.dynamic_index_in_dim(m, at, axis=1, keepdims=False)
    row_ids = column_ids(block_map, row_block)
    col_ids = column_ids(block_map, col)
    other_ids = column_ids(block_map, col ^ 1)
    wanted = jnp.concatenate([col_ids, row_ids, other_ids, row_ids])
    choose = (wanted[:, None] == blocks[None, :]).astype(BF)
    picked = jnp.einsum(
        "eb,bx->ex", choose, pool.reshape(128, 32 * W), preferred_element_type=F32
    ).astype(BF)
    picked = picked.reshape(16, 32, W)
    arrived = swap_cores(picked[8:])
    feats = in_order(core, picked[:8], arrived, 1).astype(F32)

    offsets = jnp.arange(W, dtype=jnp.int32)
    col_marks = lax.dynamic_slice_in_dim(residue_mask, col * W, W, axis=1)
    col_valid = (
        (offsets[None, :] < column_ids(block_count, col)[:, None]) & (col_marks == 1)
    ).astype(F32)
    row_offsets = half * H + jnp.arange(H, dtype=jnp.int32)
    row_marks = lax.dynamic_slice_in_dim(residue_mask, row * H, H, axis=1)
    row_valid = (
        (row_offsets[None, :] < column_ids(block_count, row_block)[:, None]) & (row_marks == 1)
    ).astype(F32)
    feat_cols = (feats[:4] * col_valid[:, None, :]).astype(BF)
    feat_rows = jnp.where(half == 0, feats[4:, :, :H], feats[4:, :, H:])
    feat_rows = (feat_rows * row_valid[:, None, :]).astype(BF)
    left_terms = jnp.einsum("fc,tfi->tci", row_embed, feat_rows, preferred_element_type=F32)
    right_terms = jnp.einsum("fc,tfj->tcj", col_embed, feat_cols, preferred_element_type=F32)
    left_cut = left_terms.reshape(T, C, 8, 8).transpose(0, 1, 3, 2).reshape(T, K8, 8)
    right_wide = jnp.broadcast_to(right_terms[:, :, None, :], (T, C, 8, W))
    gain = norm_gain.astype(F32)
    gain_wide = jnp.broadcast_to(gain[:, None, None], (C, 8, W))
    kl, kr, kg, ko, kb = expand(
        jnp.stack([left_proj.T, right_proj.T, gate_proj.T, out_proj.T, out_proj])
    )
    pick = jnp.asarray(
        np.arange(W)[None, None, :]
        == 2 * np.arange(4)[:, None, None] + (np.arange(2 * W) // W)[None, :, None],
        BF,
    )

    sent, scaled, inv, pair_sum = run_norm(template_pair, left_cut, right_wide, gain_wide, kl, kr)
    factors = exchange(sent.reshape(128, ROWS, W))
    my_inv = factors[:, 256:]
    inv_all = in_order(core, my_inv, swap_cores(my_inv), 1)
    prod = exchange(run_product(factors)).reshape(T, C, H, W)
    embedding, grad_prod, gate_mean, gate_rows, gate_cols, out_rows, out_cols = run_gate(
        prod, scaled, embed_grad, pair_sum, inv, kg, ko, kb, pick
    )
    grads = exchange(grad_prod.reshape(128, 2 * H, W))
    part_mean, sums = run_factor(factors, grads, inv_all)
    kept = jnp.where(core == 0, part_mean[:, :32], part_mean[:, 32:])
    given = jnp.where(core == 0, part_mean[:, 32:], part_mean[:, :32])
    mean_half = (kept.astype(F32) + swap_cores(given).astype(F32)).astype(BF)
    recv = exchange(mean_half).reshape(T, 16, 2, H // 2, W)
    close_rows, close_cols = run_close(recv, gate_mean, inv, scaled, pick)

    def center(weights):
        scaled_weights = gain[:, None] * weights.astype(F32)
        return scaled_weights - jnp.mean(scaled_weights, axis=0, keepdims=True)

    embeds = jnp.stack([row_embed, col_embed]).astype(F32)
    mixed = jnp.einsum(
        "efd,kdc->kefc",
        embeds,
        jnp.stack([center(left_proj), center(right_proj), center(gate_proj)]),
        precision=HIGHEST,
    )
    closing = -embeds / gain[None, None, :]
    opening = embeds * (1.0 / T)

    def finish(side, gated, closed, out, valid):
        total = jnp.einsum("fc,tci->tfi", mixed[2, side], gated, precision=HIGHEST)
        total = total + jnp.einsum("fc,tci->tfi", closing[side], closed, precision=HIGHEST)
        total = total + jnp.einsum("fc,ci->fi", opening[side], out, precision=HIGHEST)[None]
        return total * valid[:, None, :]

    grad_rows = finish(
        0, lane_rows(gate_rows), lane_rows(close_rows), lane_rows(out_rows), row_valid
    )
    grad_cols = finish(
        1, lane_cols(gate_cols), lane_cols(close_cols), lane_cols(out_cols), col_valid
    )
    owned = jnp.sum(sums, axis=2).reshape(2, 2, 2, N)
    weights = lax.dynamic_slice_in_dim(mixed[:2], 2 * pair_at, 2, axis=3)
    grad_own = jnp.einsum("kefs,sken->fn", weights, owned, precision=HIGHEST)
    all_offsets = jnp.arange(N, dtype=jnp.int32)
    own_map = lax.dynamic_index_in_dim(block_map, own, axis=0, keepdims=False)
    own_count = lax.dynamic_index_in_dim(block_count, own, axis=0, keepdims=False)
    own_marks = lax.dynamic_index_in_dim(residue_mask, own, axis=0, keepdims=False)
    own_valid = (
        (all_offsets % W).reshape(8, W) < own_count[:, None]
    ) & (own_marks.reshape(8, W) == 1)
    grad_own = grad_own.reshape(C, 8, W).transpose(1, 0, 2) * own_valid.astype(F32)[:, None, :]
    blank = jnp.zeros_like(grad_rows)
    grad_rows = jnp.concatenate(
        [jnp.where(half == 0, grad_rows, blank), jnp.where(half == 0, blank, grad_rows)], axis=2
    )
    entries = jnp.concatenate([grad_own, grad_rows, grad_cols], axis=0).astype(BF)
    kept = jnp.where(core == 0, entries[:, :32], entries[:, 32:])
    given = jnp.where(core == 0, entries[:, 32:], entries[:, :32])
    entries = jnp.concatenate([kept, swap_cores(given)], axis=0)
    targets = jnp.concatenate([own_map, row_ids, col_ids, own_map, row_ids, other_ids])
    place = (targets[None, :] == blocks[:, None]).astype(BF)
    placed = jnp.einsum(
        "be,ex->bx", place, entries.reshape(32, 32 * W), preferred_element_type=F32
    ).astype(BF)
    back = exchange(placed.reshape(128, 32, W)).reshape(64, 2 * 32, W)
    feat_grad = jnp.sum(back.astype(F32), axis=0)[None]
    return (embedding, feat_grad)


def solution(mesh):
    return jax.shard_map(
        per_device,
        mesh=mesh,
        in_specs=(
            P(None, None, "row", "col"),
            P(("row", "col"), None, None),
            P(),
            P(),
            P(),
            P(),
            P(),
            P(),
            P(),
            P(),
            P(),
            P(),
            P(None, "row", "col"),
        ),
        out_specs=(P(None, "row", "col"), P(("row", "col"), None, None)),
        check_vma=False,
    )
```

time: 1300 us -> 424 us (0.33); the launches traced: 1280 us -> 423 us
  waiting for transfers between devices: 876 us -> 74.7 us
  blocking collectives: 57.3 us -> 195 us
  matrix products: 141 us -> 8.64 us
  Pallas kernels: 0 us -> 86.4 us
  local copies, waits for them, and re-layouts: 103 us -> 16.7 us
  other arithmetic: 49.2 us -> 14.2 us
  between operations: 15.1 us -> 1.24 us
    reduce_scatter x1 -> x0, waiting for transfers between devices: 630 us -> none  [per_device(): lax.psum_scatter(scatter_terms(block_total, row_blocks, row_offsets, grad...]
    all_to_all x1 -> x3, blocking collectives: 57.3 us -> 195 us  [exchange(): return lax.all_to_all(value, AXES, split_axis=0, concat_axis=0, tiled=True)]
    dot_general x21 -> x13, matrix products: 141 us -> 8.64 us  [the longest x1 2.55 us: expand(): wide = jnp.einsum('nad,bd->nab', tall, to, preferred_element_type=F32)]
    all_to_all x5 -> x3, waiting for transfers between devices: 181 us -> 72.4 us  [exchange(): return lax.all_to_all(value, AXES, split_axis=0, concat_axis=0, tiled=True)]
    pallas_call x0 -> x5, Pallas kernels: none -> 86.4 us  [the longest x1 27.6 us: run_gate(): pl.pallas_call(gate_kernel, grid=(T,), in_specs=[each(C, H, W), each(C, H...]
    all_gather x1 -> x0, waiting for transfers between devices: 64.5 us -> none  [per_device(): lax.all_gather(template_feat, ('row', 'col'), axis=0, tiled=True)]
    transpose x3 -> x0, local copies, waits for them, and re-layouts: 34.6 us -> none  [spread_pairs(): shaped.transpose(0, 1, 3, 2, 4)]
    reduce_sum x7 -> x6, other arithmetic: 32.8 us -> 3.77 us  [the longest x3 2.76 us: lane_cols(): return jnp.sum(sums.reshape(*lead, C, 8, W), axis=-2)]
  transfers between devices with their start and end apart: 7 -> 7, of which waited for: 7 -> 6; matrix products, arithmetic and copies ran while one was open for 7% -> 5% of each run, Pallas kernels for 0% -> 0%
where the time goes in v1:
time: 424 us; the launch traced here: 423 us
  blocking collectives  195 us (46%)
  Pallas kernels  86.4 us (20%)
  waiting for transfers between devices  74.7 us (18%)
  starting transfers between devices  25.9 us (6%)
  local copies, waits for them, and re-layouts  16.7 us (4%)
  other arithmetic  14.2 us (3%)
  matrix products  8.64 us (2%)
    all_to_all x3, blocking collectives, exchange(): return lax.all_to_all(value, AXES, split_axis=0, concat_axis=0, tiled=True)  195 us
    all_to_all x3, waiting for transfers between devices, exchange(): return lax.all_to_all(value, AXES, split_axis=0, concat_axis=0, tiled=True)  72.4 us
    pallas_call x1, Pallas kernels, run_gate(): pl.pallas_call(gate_kernel, grid=(T,), in_specs=[each(C, H, W), each(C, H...  27.6 us
    pallas_call x1, Pallas kernels, run_factor(): pl.pallas_call(factor_kernel, grid=(2,), in_specs=[spec(0), spec(2), spec...  23.4 us
    all_to_all x3, starting transfers between devices, exchange(): return lax.all_to_all(value, AXES, split_axis=0, concat_axis=0, tiled=True)  20.9 us
    pallas_call x1, Pallas kernels, run_norm(): pl.pallas_call(norm_kernel, grid=(T,), in_specs=[pl.BlockSpec((1, C, H, W...  18.7 us
    pallas_call x1, Pallas kernels, run_product(): pl.pallas_call(product_kernel, grid=(2,), in_specs=[spec(0), spec(2)], ou...  11.4 us
  transfers between devices with their start and end apart: 7, of which 6 were waited for; matrix products, arithmetic and copies ran while one was open for 5% of the time, Pallas kernels for 0%

profile of v1, /device:TPU:1, one launch (start us, length us, event | category | flops | bytes accessed | tf_op | source)
XLA Modules:
  0.0 423.0 jit_solution(5877474936842531369)
XLA Ops:
  1.5 1.2 broadcast_in_dim.16
  2.7 11.5 %all-to-all-start = ((bf16[128,32,128]{2,1,0:T(8,128)(2,1)}), bf16[128,32,128]{2,1,0:T(8,128)(2,1)S(1)}, u32[]{:S(2)}, u32[]{:S(2)}) async-start(bf16[128,32,128]{2,1,0:T(8,128)(2,1)} %bitcast), calls=%async_computation | async-start | bytes 2097152 | tf_op jit(solution)/shard_map/all_to_all | solution.py:381
  15.2 2.6 select_convert_fusion
  17.7 3.3 slice_bitcast_fusion.2
  21.0 12.1 %all-to-all-done = bf16[128,32,128]{2,1,0:T(8,128)(2,1)S(1)} async-done(((bf16[128,32,128]{2,1,0:T(8,128)(2,1)}), bf16[128,32,128]{2,1,0:T(8,128)(2,1)S(1)}, u32[]{:S(2)}, u32[]{:S(2)}) %all-to-all-start) | async-done | bytes 1048608 | tf_op jit(solution)/shard_map/all_to_all | solution.py:381
  33.6 1.3 collective-permute-start
  36.1 1.3 copy.80
  37.7 1.0 broadcast_in_dim.17.right_ref
  39.6 18.7 %pair_norm.1 = (bf16[4,32,288,128]{3,2,1,0:T(8,128)(2,1)}, bf16[4,64,64,128]{3,2,1,0:T(8,128)(2,1)}, f32[4,64,128]{2,1,0:T(8,128)}, f32[64,64,128]{2,1,0:T(8,128)}) custom-call(bf16[4,64,64,128]{3,2,1,0:T(8,128)(2,1)} %pair_ref.1, f32[4,512,8]{2,1,0:T(8,128)} %bitcast.203, f32[4,64,8,128]{3,2,1,0:T(8,128)} %broadcast_in_dim.17.right_ref, ...), custom_call_target="tpu_custom_call" | custom-call | tf_op jit(solution)/shard_map/pair_norm/pallas_call | solution.py:89
  58.3 113.9 %all_to_all.30.left_ref.right_ref = bf16[128,288,128]{2,1,0:T(8,128)(2,1)} all-to-all(bf16[128,288,128]{2,1,0:T(8,128)(2,1)} %bitcast.197), channel_id=1, replica_groups=mesh['row'=16,'col'=8] {'row','col'}, dimensions={0} | all-to-all | bytes 18874368 | tf_op jit(solution)/shard_map/all_to_all | solution.py:381
  172.2 11.4 %triangle_product.1 = bf16[128,128,128]{2,1,0:T(8,128)(2,1)} custom-call(bf16[128,288,128]{2,1,0:T(8,128)(2,1)} %all_to_all.30.left_ref.right_ref, bf16[128,288,128]{2,1,0:T(8,128)(2,1)} %all_to_all.30.left_ref.right_ref), custom_call_target="tpu_custom_call" | custom-call | tf_op jit(solution)/shard_map/triangle_product/pallas_call | solution.py:143
  183.5 59.0 %all_to_all.31 = bf16[128,128,128]{2,1,0:T(8,128)(2,1)} all-to-all(bf16[128,128,128]{2,1,0:T(8,128)(2,1)} %triangle_product.1), channel_id=1, replica_groups=mesh['row'=16,'col'=8] {'row','col'}, dimensions={0} | all-to-all | bytes 8388608 | tf_op jit(solution)/shard_map/all_to_all | solution.py:381
  242.5 27.6 %gate_and_grad.1 = (bf16[64,64,128]{2,1,0:T(8,128)(2,1)}, bf16[4,64,64,128]{3,2,1,0:T(8,128)(2,1)}, f32[4,64,128]{2,1,0:T(8,128)}, f32[4,512,128]{2,1,0:T(8,128)...) custom-call(bf16[4,64,64,128]{3,2,1,0:T(8,128)(2,1)} %bitcast.196, ...), custom_call_target="tpu_custom_call" | custom-call | tf_op jit(solution)/shard_map/gate_and_grad/pallas_call | solution.py:239
  270.1 5.4 %all-to-all-start.3 = ((bf16[128,128,128]{2,1,0:T(8,128)(2,1)}), bf16[128,128,128]{2,1,0:T(8,128)(2,1)}, u32[]{:S(2)}, u32[]{:S(2)}) async-start(bf16[128,128,128]{2,1,0:T(8,128)(2,1)} %bitcast.198), calls=%async_computation.3 | async-start | bytes 8388608 | tf_op jit(solution)/shard_map/all_to_all | solution.py:381
  276.0 1.3 slice.106
  277.3 1.6 collective-permute-start.1
  281.1 1.4 broadcast_select_fusion.2
  282.5 1.6 pad_maximum_fusion.inv_ref
  284.1 44.3 %all-to-all-done.3.grad_ref = bf16[128,128,128]{2,1,0:T(8,128)(2,1)} async-done(((bf16[128,128,128]{2,1,0:T(8,128)(2,1)}), bf16[128,128,128]{2,1,0:T(8,128)(2,1)}, u32[]{:S(2)}, u32[]{:S(2)}) %all-to-all-start.3) | async-done | bytes 4194336 | tf_op jit(solution)/shard_map/all_to_all | solution.py:381
  328.4 23.4 %factor_grads.1 = (bf16[128,64,128]{2,1,0:T(8,128)(2,1)}, f32[2,4,8,1024]{3,2,1,0:T(8,128)}) custom-call(bf16[128,288,128]{2,1,0:T(8,128)(2,1)} %all_to_all.30.left_ref.right_ref, bf16[128,288,128]{2,1,0:T(8,128)(2,1)} %all_to_all.30.left_ref.right_ref, bf16[128,128,128]{2,1,0:T(8,128)(2,1)} %all-to-all-done.3.grad_ref, ...), custom_call_target="tpu_custom_call" | custom-call | tf_op jit(solution)/shard_map/factor_grads/pallas_call | solution.py:313
  351.8 2.7 broadcast_select_fusion
  356.8 1.3 slice_bitcast_fusion.1
  359.5 1.5 fusion.34
  361.0 2.7 add_convert_fusion
  363.7 4.0 all-to-all-start.4
  369.1 1.2 fusion.4
  370.3 16.0 %all-to-all-done.4 = bf16[128,32,128]{2,1,0:T(8,128)(2,1)S(1)} async-done(((bf16[128,32,128]{2,1,0:T(8,128)(2,1)}), bf16[128,32,128]{2,1,0:T(8,128)(2,1)S(1)}, u32[]{:S(2)}, u32[]{:S(2)}) %all-to-all-start.4) | async-done | bytes 1048608 | tf_op jit(solution)/shard_map/all_to_all | solution.py:381
  387.3 5.4 %close_sums.1 = (f32[4,512,128]{2,1,0:T(8,128)}, f32[4,512,128]{2,1,0:T(8,128)}) custom-call(bf16[4,16,2,32,128]{4,3,2,1,0:T(8,128)(2,1)} %bitcast.202, f32[4,64,128]{2,1,0:T(8,128)} %get-tuple-element.26.mean_ref, f32[4,64,128]{2,1,0:T(8,128)} %get-tuple-element.20.inv_ref, bf16[4,64,64,128]{3,2,1,0:T(8,128)(2,1)} %get-tuple-element.18.scaled_ref, ...), custom_call_target="tpu_custom_call" | custom-call | tf_op jit(solution)/shard_map/close_sums/pallas_call | solution.py:362
  392.7 1.5 bitcast_reduce_fusion
  394.2 1.3 slice_bitcast_fusion
  396.8 1.3 collective-permute-start.3
  399.8 22.4 %all_to_all.32 = bf16[128,32,128]{2,1,0:T(8,128)(2,1)S(1)} all-to-all(bf16[128,32,128]{2,1,0:T(8,128)(2,1)S(1)} %bitcast.200), channel_id=1, replica_groups=mesh['row'=16,'col'=8] {'row','col'}, dimensions={0} | all-to-all | bytes 2097152 | tf_op jit(solution)/shard_map/all_to_all | solution.py:381
  (111 shorter events, 16.7 us)
Async XLA Ops:
  0.6 14.6 %copy-start.23 = (bf16[512,64,1]{0,1,2:T(8,128)(2,1)S(1)}, bf16[512,64,1]{0,1,2:T(8,128)(2,1)}, u32[]{:S(2)}) copy-start(bf16[512,64,1]{0,1,2:T(8,128)(2,1)} %constant.140) | copy-start | bytes 196612
  0.6 13.7 %copy-start.11 = (bf16[64,64]{1,0:T(8,128)(2,1)S(1)}, bf16[64,64]{1,0:T(8,128)(2,1)}, u32[]{:S(2)}) copy-start(bf16[64,64]{1,0:T(8,128)(2,1)} %param.23) | copy-start | bytes 24580
  0.7 13.7 %copy-start.10 = (bf16[64,64]{1,0:T(8,128)(2,1)S(1)}, bf16[64,64]{1,0:T(8,128)(2,1)}, u32[]{:S(2)}) copy-start(bf16[64,64]{1,0:T(8,128)(2,1)} %param.26) | copy-start | bytes 24580
  0.7 13.8 %copy-start.12 = (bf16[64,64]{1,0:T(8,128)(2,1)S(1)}, bf16[64,64]{1,0:T(8,128)(2,1)}, u32[]{:S(2)}) copy-start(bf16[64,64]{1,0:T(8,128)(2,1)} %param.24) | copy-start | bytes 24580
  0.7 13.8 %copy-start.13 = (bf16[64,64]{1,0:T(8,128)(2,1)S(1)}, bf16[64,64]{1,0:T(8,128)(2,1)}, u32[]{:S(2)}) copy-start(bf16[64,64]{1,0:T(8,128)(2,1)} %param.25) | copy-start | bytes 24580
  0.7 13.8 %copy-start.14 = (s32[4,8]{1,0:T(4,128)S(1)}, s32[4,8]{1,0:T(4,128)}, u32[]{:S(2)}) copy-start(s32[4,8]{1,0:T(4,128)} %param.17) | copy-start | bytes 388
  0.7 13.8 %copy-start.15 = (s32[4,8]{1,0:T(4,128)S(1)}, s32[4,8]{1,0:T(4,128)}, u32[]{:S(2)}) copy-start(s32[4,8]{1,0:T(4,128)} %param.18) | copy-start | bytes 388
  0.7 14.2 %copy-start.21 = (s32[4,1024]{1,0:T(4,128)S(1)}, s32[4,1024]{1,0:T(4,128)}, u32[]{:S(2)}) copy-start(s32[4,1024]{1,0:T(4,128)} %param.19) | copy-start | bytes 49156
  2.7 30.4 %all-to-all-start = ((bf16[128,32,128]{2,1,0:T(8,128)(2,1)}), bf16[128,32,128]{2,1,0:T(8,128)(2,1)S(1)}, u32[]{:S(2)}, u32[]{:S(2)}) async-start(bf16[128,32,128]{2,1,0:T(8,128)(2,1)} %bitcast), calls=%async_computation | async-start | bytes 2097152 | tf_op jit(solution)/shard_map/all_to_all | solution.py:381
  14.8 6.2 %copy-start.16 = (s32[4]{0:T(128)}, s32[4]{0:T(128)S(1)}, u32[]{:S(2)}) copy-start(s32[4]{0:T(128)S(1)} %get-tuple-element.34) | copy-start | bytes 52
  14.8 6.2 %copy-start.18 = (s32[4]{0:T(128)}, s32[4]{0:T(128)S(1)}, u32[]{:S(2)}) copy-start(s32[4]{0:T(128)S(1)} %get-tuple-element.36) | copy-start | bytes 52
  17.7 18.1 %copy-start.6 = (bf16[64,64]{1,0:T(8,128)(2,1)S(1)}, bf16[64,64]{1,0:T(8,128)(2,1)}, u32[]{:S(2)}) copy-start(bf16[64,64]{1,0:T(8,128)(2,1)} %param.20) | copy-start | bytes 24580
  21.0 16.5 %copy-start.7 = (bf16[64,64]{1,0:T(8,128)(2,1)S(1)}, bf16[64,64]{1,0:T(8,128)(2,1)}, u32[]{:S(2)}) copy-start(bf16[64,64]{1,0:T(8,128)(2,1)} %param.21) | copy-start | bytes 24580
  21.0 17.7 %copy-start.22 = (bf16[64]{0:T(256)(128)(2,1)S(1)}, bf16[64]{0:T(256)(128)(2,1)}, u32[]{:S(2)}) copy-start(bf16[64]{0:T(256)(128)(2,1)} %param.22) | copy-start | bytes 388
  33.6 2.2 collective-permute-start
  270.1 58.4 %all-to-all-start.3 = ((bf16[128,128,128]{2,1,0:T(8,128)(2,1)}), bf16[128,128,128]{2,1,0:T(8,128)(2,1)}, u32[]{:S(2)}, u32[]{:S(2)}) async-start(bf16[128,128,128]{2,1,0:T(8,128)(2,1)} %bitcast.198), calls=%async_computation.3 | async-start | bytes 8388608 | tf_op jit(solution)/shard_map/all_to_all | solution.py:381
  277.3 3.9 collective-permute-start.1
  351.8 4.2 %copy-start.5 = (f32[512,128]{1,0:T(8,128)S(1)}, f32[512,128]{1,0:T(8,128)}, u32[]{:S(2)}) copy-start(f32[512,128]{1,0:T(8,128)} %get-tuple-element.28) | copy-start | bytes 786436
  354.5 6.5 %copy-start = (bf16[128,64,128]{2,1,0:T(8,128)(2,1)S(1)}, bf16[128,64,128]{2,1,0:T(8,128)(2,1)}, u32[]{:S(2)}) copy-start(bf16[128,64,128]{2,1,0:T(8,128)(2,1)} %get-tuple-element.25) | copy-start | bytes 6291460
  354.5 6.5 %collective-permute-start.2 = (bf16[128,32,128]{2,1,0:T(8,128)(2,1)}, bf16[128,32,128]{2,1,0:T(8,128)(2,1)}, u32[]{:S(2)}, u32[]{:S(2)}) collective-permute-start(bf16[128,32,128]{2,1,0:T(8,128)(2,1)} %broadcast_select_fusion), channel_id=1, source_target_pairs={{0,1},{1,0},{2,3},{3,2},{4,5},{5,4},{6,7},{7,6},{8,9},{9,8},{10,11... | collective-permute-start | bytes 3145736 | tf_op jit(solution)/shard_map/ppermute | solution.py:377
  361.0 6.7 %copy-start.2 = (f32[4,512,128]{2,1,0:T(8,128)S(1)}, f32[4,512,128]{2,1,0:T(8,128)}, u32[]{:S(2)}) copy-start(f32[4,512,128]{2,1,0:T(8,128)} %get-tuple-element.29) | copy-start | bytes 3145732
  363.7 4.3 %copy-start.3 = (f32[2,64,64]{2,1,0:T(8,128)S(1)}, f32[2,64,64]{2,1,0:T(8,128)}, u32[]{:S(2)}) copy-start(f32[2,64,64]{2,1,0:T(8,128)} %get-tuple-element.56) | copy-start | bytes 98308
  363.7 4.3 %copy-start.9 = (f32[64,8,8]{0,1,2:T(8,128)S(1)}, f32[64,8,8]{0,1,2:T(8,128)}, u32[]{:S(2)}) copy-start(f32[64,8,8]{0,1,2:T(8,128)} %copy.94) | copy-start | bytes 49156
  363.7 5.3 %copy-start.4 = (f32[2,4,8,1024]{3,2,1,0:T(8,128)S(1)}, f32[2,4,8,1024]{3,2,1,0:T(8,128)}, u32[]{:S(2)}) copy-start(f32[2,4,8,1024]{3,2,1,0:T(8,128)} %get-tuple-element.23) | copy-start | bytes 786436
  363.7 5.4 %copy-start.20 = (f32[8,128]{1,0:T(8,128)S(1)}, f32[8,128]{1,0:T(8,128)}, u32[]{:S(2)}) copy-start(f32[8,128]{1,0:T(8,128)} %fusion.51) | copy-start | bytes 12292
  363.7 22.6 %all-to-all-start.4 = ((bf16[128,32,128]{2,1,0:T(8,128)(2,1)}), bf16[128,32,128]{2,1,0:T(8,128)(2,1)S(1)}, u32[]{:S(2)}, u32[]{:S(2)}) async-start(bf16[128,32,128]{2,1,0:T(8,128)(2,1)} %add_convert_fusion), calls=%async_computation.4 | async-start | bytes 2097152 | tf_op jit(solution)/shard_map/all_to_all | solution.py:381
  386.4 1.0 copy-start.1
  392.7 3.2 copy-start.8
  394.2 4.0 copy-start.17
  394.2 4.0 copy-start.19
  396.8 2.3 collective-permute-start.3

commit v2 on v1

--- a/solution.py
+++ b/solution.py
@@ -152,32 +152,98 @@
     )(factors, factors)
 
 
+def halves(value):
+    return value[:, :8, :], value[:, 8:, :]
+
+
+def mean_channels(value):
+    return jnp.sum(value, axis=0, keepdims=True) * (1.0 / C)
+
+
+def back_kernel(scaled_ref, grad_ref, kg_ref, kb_ref, out_ref):
+    for g in range(4):
+        rows = slice(g * 16, g * 16 + 16)
+        scaled = stack_rows(*halves(scaled_ref[0, :, rows, :].astype(F32))).astype(BF)
+        opened = unstack_rows(jnp.dot(kg_ref[...], scaled, preferred_element_type=F32))
+        grads = halves(grad_ref[:, rows, :].astype(F32))
+        grad_projs = [
+            grads[part] * (1.0 / T) * jax.nn.sigmoid(opened[part]) for part in range(2)
+        ]
+        grad_norms = unstack_rows(
+            jnp.dot(kb_ref[...], stack_rows(*grad_projs).astype(BF), preferred_element_type=F32)
+        )
+        outs = [grad_norm - mean_channels(grad_norm) for grad_norm in grad_norms]
+        out_ref[0, :, rows, :] = join_rows(*outs).astype(BF)
+
+
+def whole_spec(*shape):
+    return pl.BlockSpec(shape, lambda t: (0,) * len(shape))
+
+
+def each_spec(*shape):
+    return pl.BlockSpec((1, *shape), lambda t: (t,) + (0,) * len(shape))
+
+
+def run_back(scaled, grad, kg, kb):
+    return pl.pallas_call(
+        back_kernel,
+        grid=(T,),
+        in_specs=[each_spec(C, H, W), whole_spec(C, H, W), whole_spec(K8, K8), whole_spec(K8, K8)],
+        out_specs=each_spec(C, H, W),
+        out_shape=jax.ShapeDtypeStruct((T, C, H, W), BF),
+        compiler_params=params(),
+        cost_estimate=pl.CostEstimate(flops=4 * 2**31, bytes_accessed=9 * 2**20, transcendentals=2**21),
+        name="back_project",
+    )(scaled, grad, kg, kb)
+
+
+def product_norm(product):
+    shifted = product - mean_channels(product)
+    return shifted, lax.rsqrt(mean_channels(shifted * shifted) + EPS)
+
+
+def grad_kernel(prod_ref, back_ref, out_ref):
+    for g in range(8):
+        rows = slice(g * 8, g * 8 + 8)
+        shifted, inverse = product_norm(prod_ref[0, :, rows, :].astype(F32))
+        back = back_ref[0, :, rows, :].astype(F32)
+        slope = mean_channels(back * shifted) * inverse * inverse
+        out_ref[0, :, rows, :] = ((back - shifted * slope) * inverse).astype(BF)
+
+
+def run_grad(prod, back):
+    return pl.pallas_call(
+        grad_kernel,
+        grid=(T,),
+        in_specs=[each_spec(C, H, W), each_spec(C, H, W)],
+        out_specs=each_spec(C, H, W),
+        out_shape=jax.ShapeDtypeStruct((T, C, H, W), BF),
+        compiler_params=params(),
+        cost_estimate=pl.CostEstimate(flops=2**25, bytes_accessed=12 * 2**20, transcendentals=0),
+        name="product_grad",
+    )(prod, back)
+
+
 def gate_kernel(
-    prod_ref, scaled_ref, grad_ref, sum_ref, inv_ref, kg_ref, ko_ref, kb_ref, pick_ref,
-    emb_ref, out_ref, mean_ref, rows_ref, cols_ref, grows_ref, gcols_ref, total,
+    prod_ref, scaled_ref, grad_ref, sum_ref, inv_ref, kg_ref, ko_ref, pick_ref,
+    emb_ref, mean_ref, rows_ref, cols_ref, grows_ref, gcols_ref, total,
 ):
     step = pl.program_id(0)
-    halves = lambda v: (v[:, :8, :], v[:, 8:, :])
     row_sums = jnp.zeros((K8, W), F32)
     col_sums = jnp.zeros((C, 8, W), F32)
     for g in range(4):
         rows = slice(g * 16, g * 16 + 16)
         scaled = stack_rows(*halves(scaled_ref[0, :, rows, :].astype(F32))).astype(BF)
         opened = unstack_rows(jnp.dot(kg_ref[...], scaled, preferred_element_type=F32))
-        normed, prod_invs = [], []
+        normed = []
         for product in halves(prod_ref[0, :, rows, :].astype(F32)):
-            center = jnp.sum(product, axis=0, keepdims=True) * (1.0 / C)
-            shifted = product - center
-            inverse = lax.rsqrt(
-                jnp.sum(shifted * shifted, axis=0, keepdims=True) * (1.0 / C) + EPS
-            )
+            shifted, inverse = product_norm(product)
             normed.append(shifted * inverse)
-            prod_invs.append(inverse)
         projected = unstack_rows(
             jnp.dot(ko_ref[...], stack_rows(*normed).astype(BF), preferred_element_type=F32)
         )
         grads = halves(grad_ref[:, rows, :].astype(F32))
-        grad_projs, weighted = [], []
+        weighted = []
         for part in range(2):
             first = g * 16 + part * 8
             where = (slice(None), slice(first, first + 8), slice(None))
@@ -192,9 +258,7 @@
             def _():
                 total[where] += gated
 
-            grad_out = grads[part] * (1.0 / T)
-            grad_projs.append(grad_out * gate)
-            grad_gate = grad_out * gated * (1.0 - gate)
+            grad_gate = grads[part] * (1.0 / T) * gated * (1.0 - gate)
             mean_ref[0, first : first + 8, :] = jnp.sum(grad_gate * opened[part], axis=0)
             term = grad_gate * inv_ref[0, first : first + 8, :][None]
             col_sums = col_sums + term
@@ -202,16 +266,6 @@
         row_sums = row_sums + jnp.dot(
             stack_rows(*weighted).astype(BF), pick_ref[g], preferred_element_type=F32
         )
-        grad_norms = unstack_rows(
-            jnp.dot(kb_ref[...], stack_rows(*grad_projs).astype(BF), preferred_element_type=F32)
-        )
-        outs = []
-        for part in range(2):
-            grad_norm = grad_norms[part]
-            first_mean = jnp.sum(grad_norm, axis=0, keepdims=True) * (1.0 / C)
-            second_mean = jnp.sum(grad_norm * normed[part], axis=0, keepdims=True) * (1.0 / C)
-            outs.append((grad_norm - first_mean - normed[part] * second_mean) * prod_invs[part])
-        out_ref[0, :, rows, :] = join_rows(*outs).astype(BF)
     rows_ref[0] = row_sums
     cols_ref[0] = col_sums.reshape(K8, W)
 
@@ -233,23 +287,20 @@
         emb_ref[...] = (total[...] * (1.0 / T)).astype(BF)
 
 
-def run_gate(prod, scaled, grad, pair_sum, inv, kg, ko, kb, pick):
-    whole = lambda *shape: pl.BlockSpec(shape, lambda t: (0,) * len(shape))
-    each = lambda *shape: pl.BlockSpec((1, *shape), lambda t: (t,) + (0,) * len(shape))
+def run_gate(prod, scaled, grad, pair_sum, inv, kg, ko, pick):
     return pl.pallas_call(
         gate_kernel,
         grid=(T,),
         in_specs=[
-            each(C, H, W), each(C, H, W), whole(C, H, W), whole(C, H, W), each(H, W),
-            whole(K8, K8), whole(K8, K8), whole(K8, K8), whole(4, 2 * W, W),
+            each_spec(C, H, W), each_spec(C, H, W), whole_spec(C, H, W), whole_spec(C, H, W),
+            each_spec(H, W), whole_spec(K8, K8), whole_spec(K8, K8), whole_spec(4, 2 * W, W),
         ],
         out_specs=[
-            whole(C, H, W), each(C, H, W), each(H, W), each(K8, W), each(K8, W),
-            whole(K8, W), whole(K8, W),
+            whole_spec(C, H, W), each_spec(H, W), each_spec(K8, W), each_spec(K8, W),
+            whole_spec(K8, W), whole_spec(K8, W),
         ],
         out_shape=[
             jax.ShapeDtypeStruct((C, H, W), BF),
-            jax.ShapeDtypeStruct((T, C, H, W), BF),
             jax.ShapeDtypeStruct((T, H, W), F32),
             jax.ShapeDtypeStruct((T, K8, W), F32),
             jax.ShapeDtypeStruct((T, K8, W), F32),
@@ -258,21 +309,46 @@
         ],
         scratch_shapes=[pltpu.VMEM((C, H, W), F32)],
         compiler_params=params(),
-        name="gate_and_grad",
-    )(prod, scaled, grad, pair_sum, inv, kg, ko, kb, pick)
-
-
-def factor_kernel(
-    left_ref, right_ref, grad_ref, inv_ref, out_ref, sums_ref, left, right, grad, inv, mean
-):
+        cost_estimate=pl.CostEstimate(flops=4 * 2**31, bytes_accessed=12 * 2**20, transcendentals=2**21),
+        name="gate_and_embed",
+    )(prod, scaled, grad, pair_sum, inv, kg, ko, pick)
+
+
+def square_kernel(left_ref, right_ref, inv_ref, left, right, inv):
     step = pl.program_id(0)
-    spread(left_ref, left)
-    spread(right_ref, right)
-    spread(grad_ref, grad)
+    spread(left_ref, left.at[0])
+    spread(right_ref, right.at[0])
 
     @pl.when(step == 0)
     def _():
         spread(inv_ref, inv)
+
+
+def run_square(factors, inv):
+    spec = lambda first: pl.BlockSpec((128, H, W), lambda s: (0, first + s, 0))
+    out = pl.BlockSpec((1, N, N), lambda s: (s, 0, 0))
+    return pl.pallas_call(
+        square_kernel,
+        grid=(2,),
+        in_specs=[spec(0), spec(2), pl.BlockSpec((128, H, W), lambda s: (0, 0, 0))],
+        out_specs=[out, out, pl.BlockSpec((N, N), lambda s: (0, 0))],
+        out_shape=[jax.ShapeDtypeStruct((2, N, N), BF)] * 2 + [jax.ShapeDtypeStruct((N, N), BF)],
+        compiler_params=params(),
+        cost_estimate=pl.CostEstimate(flops=2**20, bytes_accessed=20 * 2**20, transcendentals=0),
+        name="to_matrices",
+    )(factors, factors, inv)
+
+
+def factor_kernel(
+    core_ref, left_ref, right_ref, grad_ref, inv_ref, kept_ref, given_ref, sums_ref, grad, mean
+):
+    step = pl.program_id(0)
+    core = core_ref[0]
+    left, right = left_ref.at[0], right_ref.at[0]
+    spread(grad_ref, grad)
+
+    @pl.when(step == 0)
+    def _():
         mean[...] = jnp.zeros_like(mean)
 
     sums_ref[...] = jnp.zeros_like(sums_ref)
@@ -280,7 +356,7 @@
 
     def finish(value, rows, factor, kind):
         mean[rows, :] += value * factor[rows, :].astype(F32)
-        term = value * inv[rows, :].astype(F32)
+        term = value * inv_ref[rows, :].astype(F32)
         sums_ref[0, 2 * kind + 1] += jnp.sum(term.reshape(32, 8, N), axis=0)
         lanes = term[:, :W]
         for c in range(1, 8):
@@ -304,34 +380,39 @@
     def _():
         @pl.loop(0, 16)
         def _(r):
+            mine = pl.ds(pl.multiple_of(r * H + core * 32, 32), 32)
+            other = pl.ds(pl.multiple_of(r * H + (1 - core) * 32, 32), 32)
             for c in range(8):
-                out_ref[r * 8 + c] = mean[pl.ds(r * H, H), c * W : (c + 1) * W].astype(BF)
-
-
-def run_factor(factors, grad, inv):
-    spec = lambda first: pl.BlockSpec((128, H, W), lambda s: (0, first + s, 0))
+                kept_ref[r * 8 + c] = mean[mine, c * W : (c + 1) * W].astype(BF)
+                given_ref[r * 8 + c] = mean[other, c * W : (c + 1) * W].astype(BF)
+
+
+def run_factor(core, left, right, grad, inv):
+    matrix = pl.BlockSpec((1, N, N), lambda s: (s, 0, 0))
     return pl.pallas_call(
         factor_kernel,
         grid=(2,),
-        in_specs=[spec(0), spec(2), spec(0), pl.BlockSpec((128, H, W), lambda s: (0, 0, 0))],
+        in_specs=[
+            pl.BlockSpec(memory_space=pltpu.SMEM),
+            matrix,
+            matrix,
+            pl.BlockSpec((128, H, W), lambda s: (0, s, 0)),
+            pl.BlockSpec((N, N), lambda s: (0, 0)),
+        ],
         out_specs=[
-            pl.BlockSpec((128, H, W), lambda s: (0, 0, 0)),
+            pl.BlockSpec((128, H // 2, W), lambda s: (0, 0, 0)),
+            pl.BlockSpec((128, H // 2, W), lambda s: (0, 0, 0)),
             pl.BlockSpec((1, 4, 8, N), lambda s: (s, 0, 0, 0)),
         ],
         out_shape=[
-            jax.ShapeDtypeStruct((128, H, W), BF),
+            jax.ShapeDtypeStruct((128, H // 2, W), BF),
+            jax.ShapeDtypeStruct((128, H // 2, W), BF),
             jax.ShapeDtypeStruct((2, 4, 8, N), F32),
         ],
-        scratch_shapes=[
-            pltpu.VMEM((N, N), BF),
-            pltpu.VMEM((N, N), BF),
-            pltpu.VMEM((N, N), BF),
-            pltpu.VMEM((N, N), BF),
-            pltpu.VMEM((N, N), F32),
-        ],
+        scratch_shapes=[pltpu.VMEM((N, N), BF), pltpu.VMEM((N, N), F32)],
         compiler_params=params(),
         name="factor_grads",
-    )(factors, factors, grad, inv)
+    )(core.reshape(1), left, right, grad, inv)
 
 
 def close_kernel(recv_ref, mean_ref, inv_ref, scaled_ref, pick_ref, rows_ref, cols_ref):
@@ -477,17 +558,25 @@
 
     sent, scaled, inv, pair_sum = run_norm(template_pair, left_cut, right_wide, gain_wide, kl, kr)
     factors = exchange(sent.reshape(128, ROWS, W))
+    back = run_back(scaled, embed_grad, kg, kb)
+    factors, back = lax.optimization_barrier((factors, back))
     my_inv = factors[:, 256:]
     inv_all = in_order(core, my_inv, swap_cores(my_inv), 1)
     prod = exchange(run_product(factors)).reshape(T, C, H, W)
-    embedding, grad_prod, gate_mean, gate_rows, gate_cols, out_rows, out_cols = run_gate(
-        prod, scaled, embed_grad, pair_sum, inv, kg, ko, kb, pick
-    )
-    grads = exchange(grad_prod.reshape(128, 2 * H, W))
-    part_mean, sums = run_factor(factors, grads, inv_all)
-    kept = jnp.where(core == 0, part_mean[:, :32], part_mean[:, 32:])
-    given = jnp.where(core == 0, part_mean[:, 32:], part_mean[:, :32])
+    left, right, inv_matrix = run_square(factors, inv_all)
+    prod, left, right, inv_matrix = lax.optimization_barrier((prod, left, right, inv_matrix))
+    grads = exchange(run_grad(prod, back).reshape(128, 2 * H, W))
+    embedding, gate_mean, gate_rows, gate_cols, out_rows, out_cols = run_gate(
+        prod, scaled, embed_grad, pair_sum, inv, kg, ko, pick
+    )
+    grads, embedding, gate_mean, gate_rows, gate_cols, out_rows, out_cols = (
+        lax.optimization_barrier(
+            (grads, embedding, gate_mean, gate_rows, gate_cols, out_rows, out_cols)
+        )
+    )
+    kept, given, sums = run_factor(core, left, right, grads, inv_matrix)
     mean_half = (kept.astype(F32) + swap_cores(given).astype(F32)).astype(BF)
+    sums, mean_half = lax.optimization_barrier((sums, mean_half))
     recv = exchange(mean_half).reshape(T, 16, 2, H // 2, W)
     close_rows, close_cols = run_close(recv, gate_mean, inv, scaled, pick)
 

time: 424 us -> 402 us (0.948)
  blocking collectives: 195 us -> 22.4 us
  waiting for transfers between devices: 74.7 us -> 190 us
  Pallas kernels: 86.4 us -> 106 us
  starting transfers between devices: 25.9 us -> 38.6 us
  local copies, waits for them, and re-layouts: 16.7 us -> 21.7 us
    all_to_all x3 -> x1, blocking collectives: 195 us -> 22.4 us  [exchange(): return lax.all_to_all(value, AXES, split_axis=0, concat_axis=0, tiled=True)]
    all_to_all x3 -> x5, waiting for transfers between devices: 72.4 us -> 187 us  [exchange(): return lax.all_to_all(value, AXES, split_axis=0, concat_axis=0, tiled=True)]
    pallas_call x2 -> x5, Pallas kernels: 51 us -> 70.4 us  [the longest x1 22.7 us: run_gate(): pl.pallas_call(gate_kernel, grid=(T,), in_specs=[each_spec(C, H, W), each...]
    all_to_all x3 -> x5, starting transfers between devices: 20.9 us -> 33.7 us  [exchange(): return lax.all_to_all(value, AXES, split_axis=0, concat_axis=0, tiled=True)]
  transfers between devices with their start and end apart: 7 -> 9, of which waited for: 6 -> 8; matrix products, arithmetic and copies ran while one was open for 5% -> 7% of each run, Pallas kernels for 0% -> 10%
where the time goes in v2:
time: 402 us; the launch traced here: 400 us
  waiting for transfers between devices  190 us (47%)
  Pallas kernels  106 us (26%)
  starting transfers between devices  38.6 us (10%)
  blocking collectives  22.4 us (6%)
  local copies, waits for them, and re-layouts  21.7 us (5%)
  other arithmetic  12.2 us (3%)
  matrix products  8.19 us (2%)
    all_to_all x5, waiting for transfers between devices, exchange(): return lax.all_to_all(value, AXES, split_axis=0, concat_axis=0, tiled=True)  187 us
    all_to_all x5, starting transfers between devices, exchange(): return lax.all_to_all(value, AXES, split_axis=0, concat_axis=0, tiled=True)  33.7 us
    pallas_call x1, Pallas kernels, run_gate(): pl.pallas_call(gate_kernel, grid=(T,), in_specs=[each_spec(C, H, W), each...  22.7 us
    all_to_all x1, blocking collectives, exchange(): return lax.all_to_all(value, AXES, split_axis=0, concat_axis=0, tiled=True)  22.4 us
    pallas_call x1, Pallas kernels, run_factor(): pl.pallas_call(factor_kernel, grid=(2,), in_specs=[pl.BlockSpec(memory_sp...  21.4 us
    pallas_call x1, Pallas kernels, run_norm(): pl.pallas_call(norm_kernel, grid=(T,), in_specs=[pl.BlockSpec((1, C, H, W...  18.8 us
    pallas_call x1, Pallas kernels, run_product(): pl.pallas_call(product_kernel, grid=(2,), in_specs=[spec(0), spec(2)], ou...  11.4 us
    pallas_call x1, Pallas kernels, run_back(): pl.pallas_call(back_kernel, grid=(T,), in_specs=[each_spec(C, H, W), whol...  10.1 us
  transfers between devices with their start and end apart: 9, of which 8 were waited for; matrix products, arithmetic and copies ran while one was open for 7% of the time, Pallas kernels for 10%

profile of v2, /device:TPU:1, one launch (start us, length us, event | category | flops | bytes accessed | tf_op | source)
XLA Modules:
  0.0 400.2 jit_solution(13325223533135207209)
XLA Ops:
  2.6 11.5 %all-to-all-start = ((bf16[128,32,128]{2,1,0:T(8,128)(2,1)}), bf16[128,32,128]{2,1,0:T(8,128)(2,1)S(1)}, u32[]{:S(2)}, u32[]{:S(2)}) async-start(bf16[128,32,128]{2,1,0:T(8,128)(2,1)} %bitcast), calls=%async_computation | async-start | bytes 2097152 | tf_op jit(solution)/shard_map/all_to_all | solution.py:462
  20.0 3.5 select_convert_fusion
  23.4 3.3 slice_bitcast_fusion.2
  26.8 6.2 %all-to-all-done = bf16[128,32,128]{2,1,0:T(8,128)(2,1)S(1)} async-done(((bf16[128,32,128]{2,1,0:T(8,128)(2,1)}), bf16[128,32,128]{2,1,0:T(8,128)(2,1)S(1)}, u32[]{:S(2)}, u32[]{:S(2)}) %all-to-all-start) | async-done | bytes 1048608 | tf_op jit(solution)/shard_map/all_to_all | solution.py:462
  33.4 1.3 collective-permute-start
  36.0 1.3 copy.80
  39.4 18.8 %pair_norm.1 = (bf16[4,32,288,128]{3,2,1,0:T(8,128)(2,1)}, bf16[4,64,64,128]{3,2,1,0:T(8,128)(2,1)}, f32[4,64,128]{2,1,0:T(8,128)}, f32[64,64,128]{2,1,0:T(8,128)}) custom-call(bf16[4,64,64,128]{3,2,1,0:T(8,128)(2,1)} %pair_ref.1, f32[4,512,8]{2,1,0:T(8,128)} %bitcast.203, f32[4,64,8,128]{3,2,1,0:T(8,128)} %broadcast_in_dim.17.right_ref, ...), custom_call_target="tpu_custom_call" | custom-call | tf_op jit(solution)/shard_map/pair_norm/pallas_call | solution.py:89
  58.2 5.0 %all-to-all-start.1 = ((bf16[128,288,128]{2,1,0:T(8,128)(2,1)}), bf16[128,288,128]{2,1,0:T(8,128)(2,1)}, u32[]{:S(2)}, u32[]{:S(2)}) async-start(bf16[128,288,128]{2,1,0:T(8,128)(2,1)} %bitcast.198), calls=%async_computation.1 | async-start | bytes 18874368 | tf_op jit(solution)/shard_map/all_to_all | solution.py:462
  63.2 10.1 %back_project.1.back_ref = bf16[4,64,64,128]{3,2,1,0:T(8,128)(2,1)} custom-call(bf16[4,64,64,128]{3,2,1,0:T(8,128)(2,1)} %get-tuple-element.36.scaled_ref, bf16[64,64,128]{2,1,0:T(8,128)(2,1)} %grad_ref.3, bf16[512,512]{1,0:T(8,128)(2,1)} %get-tuple-element.80.kg_ref, bf16[512,512]{1,0:T(8,128)(2,1)} %get-tuple-element.79.kb_ref), custom_call_target="tpu_custom_call" | custom-call | flops 8589934592 | bytes 9437184 | tf_op jit(solution)/shard_map/back_project/pallas_call | solution.py:188
  73.3 102.3 %all-to-all-done.1.left_ref.right_ref = bf16[128,288,128]{2,1,0:T(8,128)(2,1)} async-done(((bf16[128,288,128]{2,1,0:T(8,128)(2,1)}), bf16[128,288,128]{2,1,0:T(8,128)(2,1)}, u32[]{:S(2)}, u32[]{:S(2)}) %all-to-all-start.1) | async-done | bytes 9437216 | tf_op jit(solution)/shard_map/all_to_all | solution.py:462
  175.5 11.4 %triangle_product.1 = bf16[128,128,128]{2,1,0:T(8,128)(2,1)} custom-call(bf16[128,288,128]{2,1,0:T(8,128)(2,1)} %all-to-all-done.1.left_ref.right_ref, bf16[128,288,128]{2,1,0:T(8,128)(2,1)} %all-to-all-done.1.left_ref.right_ref), custom_call_target="tpu_custom_call" | custom-call | tf_op jit(solution)/shard_map/triangle_product/pallas_call | solution.py:143
  186.9 7.9 %all-to-all-start.2 = ((bf16[128,128,128]{2,1,0:T(8,128)(2,1)}), bf16[128,128,128]{2,1,0:T(8,128)(2,1)}, u32[]{:S(2)}, u32[]{:S(2)}) async-start(bf16[128,128,128]{2,1,0:T(8,128)(2,1)} %triangle_product.1), calls=%async_computation.2 | async-start | bytes 8388608 | tf_op jit(solution)/shard_map/all_to_all | solution.py:462
  194.8 1.3 slice.77
  197.3 2.3 collective-permute-done.1
  199.6 1.4 broadcast_select_fusion.1
  201.0 1.6 pad_maximum_fusion.inv_ref
  202.6 8.1 %to_matrices.1 = (bf16[2,1024,1024]{2,1,0:T(8,128)(2,1)}, bf16[2,1024,1024]{2,1,0:T(8,128)(2,1)}, bf16[1024,1024]{1,0:T(8,128)(2,1)}) custom-call(bf16[128,288,128]{2,1,0:T(8,128)(2,1)} %all-to-all-done.1.left_ref.right_ref, bf16[128,288,128]{2,1,0:T(8,128)(2,1)} %all-to-all-done.1.left_ref.right_ref, bf16[128,64,128]{2,1,0:T(8,128)(2,1)} %pad_maximum_fusion.inv_ref), custom_call_target="tpu_custom_call" | custom-call | flops 1048576 | bytes 20971520 | tf_op jit(solution)/shard_map/to_matrices/pallas_call | solution.py:330
  210.7 36.9 %all-to-all-done.2 = bf16[128,128,128]{2,1,0:T(8,128)(2,1)} async-done(((bf16[128,128,128]{2,1,0:T(8,128)(2,1)}), bf16[128,128,128]{2,1,0:T(8,128)(2,1)}, u32[]{:S(2)}, u32[]{:S(2)}) %all-to-all-start.2) | async-done | bytes 4194336 | tf_op jit(solution)/shard_map/all_to_all | solution.py:462
  247.6 8.1 %product_grad.1 = bf16[4,64,64,128]{3,2,1,0:T(8,128)(2,1)} custom-call(bf16[4,64,64,128]{3,2,1,0:T(8,128)(2,1)} %bitcast.26.prod_ref, bf16[4,64,64,128]{3,2,1,0:T(8,128)(2,1)} %back_project.1.back_ref), custom_call_target="tpu_custom_call" | custom-call | flops 33554432 | bytes 12582912 | tf_op jit(solution)/shard_map/product_grad/pallas_call | solution.py:215
  255.7 5.5 %all-to-all-start.3 = ((bf16[128,128,128]{2,1,0:T(8,128)(2,1)}), bf16[128,128,128]{2,1,0:T(8,128)(2,1)}, u32[]{:S(2)}, u32[]{:S(2)}) async-start(bf16[128,128,128]{2,1,0:T(8,128)(2,1)} %bitcast.197), calls=%async_computation.3 | async-start | bytes 8388608 | tf_op jit(solution)/shard_map/all_to_all | solution.py:462
  263.4 22.7 %gate_and_embed.1 = (bf16[64,64,128]{2,1,0:T(8,128)(2,1)}, f32[4,64,128]{2,1,0:T(8,128)}, f32[4,512,128]{2,1,0:T(8,128)}, f32[4,512,128]{2,1,0:T(8,128)}, f32[512,128]{1,0:T(8,128)}, /*index=5*/f32[512,128]{1,0:T(8,128)}) custom-call(bf16[4,64,64,128]{3,2,1,0:T(8,128)(2,1)} %bitcast.26.prod_ref, bf16[4,64,64,128]{3,2,1,0:T(8,128)(2,1)} %get-tuple-element.36.scaled_ref, ...), custom_call_target="tpu_custom_call" | custom-call | flops 8589934592 | bytes 12582912 | tf_op jit(solution)/shard_map/gate_and_embed/pallas_call | solution.py:291
  286.1 28.1 %all-to-all-done.3.grad_ref = bf16[128,128,128]{2,1,0:T(8,128)(2,1)} async-done(((bf16[128,128,128]{2,1,0:T(8,128)(2,1)}), bf16[128,128,128]{2,1,0:T(8,128)(2,1)}, u32[]{:S(2)}, u32[]{:S(2)}) %all-to-all-start.3) | async-done | bytes 4194336 | tf_op jit(solution)/shard_map/all_to_all | solution.py:462
  314.2 21.4 %factor_grads.1 = (bf16[128,32,128]{2,1,0:T(8,128)(2,1)}, bf16[128,32,128]{2,1,0:T(8,128)(2,1)}, f32[2,4,8,1024]{3,2,1,0:T(8,128)}) custom-call(s32[1]{0:T(128)} %bitcast.41.core_ref, bf16[2,1024,1024]{2,1,0:T(8,128)(2,1)} %get-tuple-element.52.left_ref, bf16[2,1024,1024]{2,1,0:T(8,128)(2,1)} %get-tuple-element.53.right_ref, ...), custom_call_target="tpu_custom_call" | custom-call | tf_op jit(solution)/shard_map/factor_grads/pallas_call | solution.py:392
  338.1 1.3 slice_bitcast_fusion.1
  339.4 1.3 add_convert_fusion
  340.7 3.8 all-to-all-start.4
  344.5 1.5 bitcast_reduce_fusion.1
  349.6 13.9 %all-to-all-done.4 = bf16[128,32,128]{2,1,0:T(8,128)(2,1)S(1)} async-done(((bf16[128,32,128]{2,1,0:T(8,128)(2,1)}), bf16[128,32,128]{2,1,0:T(8,128)(2,1)S(1)}, u32[]{:S(2)}, u32[]{:S(2)}) %all-to-all-start.4) | async-done | bytes 1048608 | tf_op jit(solution)/shard_map/all_to_all | solution.py:462
  364.5 5.4 %close_sums.1 = (f32[4,512,128]{2,1,0:T(8,128)}, f32[4,512,128]{2,1,0:T(8,128)}) custom-call(bf16[4,16,2,32,128]{4,3,2,1,0:T(8,128)(2,1)} %bitcast.202, f32[4,64,128]{2,1,0:T(8,128)} %get-tuple-element.62.mean_ref, f32[4,64,128]{2,1,0:T(8,128)} %get-tuple-element.44.inv_ref, bf16[4,64,64,128]{3,2,1,0:T(8,128)(2,1)} %get-tuple-element.36.scaled_ref, ...), custom_call_target="tpu_custom_call" | custom-call | tf_op jit(solution)/shard_map/close_sums/pallas_call | solution.py:443
  371.5 1.5 bitcast_reduce_fusion
  373.9 1.3 collective-permute-start.3
  377.0 22.4 %all_to_all.30 = bf16[128,32,128]{2,1,0:T(8,128)(2,1)S(1)} all-to-all(bf16[128,32,128]{2,1,0:T(8,128)(2,1)S(1)} %bitcast.200), channel_id=1, replica_groups=mesh['row'=16,'col'=8] {'row','col'}, dimensions={0} | all-to-all | bytes 2097152 | tf_op jit(solution)/shard_map/all_to_all | solution.py:462
  (87 shorter events, 26.8 us)
Async XLA Ops:
  2.6 30.4 %all-to-all-start = ((bf16[128,32,128]{2,1,0:T(8,128)(2,1)}), bf16[128,32,128]{2,1,0:T(8,128)(2,1)S(1)}, u32[]{:S(2)}, u32[]{:S(2)}) async-start(bf16[128,32,128]{2,1,0:T(8,128)(2,1)} %bitcast), calls=%async_computation | async-start | bytes 2097152 | tf_op jit(solution)/shard_map/all_to_all | solution.py:462
  23.4 12.3 %copy-start.4 = (bf16[64,64]{1,0:T(8,128)(2,1)S(1)}, bf16[64,64]{1,0:T(8,128)(2,1)}, u32[]{:S(2)}) copy-start(bf16[64,64]{1,0:T(8,128)(2,1)} %param.20) | copy-start | bytes 24580
  23.4 13.9 %copy-start.5 = (bf16[64,64]{1,0:T(8,128)(2,1)S(1)}, bf16[64,64]{1,0:T(8,128)(2,1)}, u32[]{:S(2)}) copy-start(bf16[64,64]{1,0:T(8,128)(2,1)} %param.21) | copy-start | bytes 24580
  23.4 15.2 %copy-start.9 = (bf16[64]{0:T(256)(128)(2,1)S(1)}, bf16[64]{0:T(256)(128)(2,1)}, u32[]{:S(2)}) copy-start(bf16[64]{0:T(256)(128)(2,1)} %param.22) | copy-start | bytes 388
  33.4 2.2 collective-permute-start
  58.2 117.3 %all-to-all-start.1 = ((bf16[128,288,128]{2,1,0:T(8,128)(2,1)}), bf16[128,288,128]{2,1,0:T(8,128)(2,1)}, u32[]{:S(2)}, u32[]{:S(2)}) async-start(bf16[128,288,128]{2,1,0:T(8,128)(2,1)} %bitcast.198), calls=%async_computation.1 | async-start | bytes 18874368 | tf_op jit(solution)/shard_map/all_to_all | solution.py:462
  186.9 60.7 %all-to-all-start.2 = ((bf16[128,128,128]{2,1,0:T(8,128)(2,1)}), bf16[128,128,128]{2,1,0:T(8,128)(2,1)}, u32[]{:S(2)}, u32[]{:S(2)}) async-start(bf16[128,128,128]{2,1,0:T(8,128)(2,1)} %triangle_product.1), calls=%async_computation.2 | async-start | bytes 8388608 | tf_op jit(solution)/shard_map/all_to_all | solution.py:462
  196.1 3.5 collective-permute-start.1
  255.7 5.6 %copy-start.6 = (bf16[64,64]{1,0:T(8,128)(2,1)S(1)}, bf16[64,64]{1,0:T(8,128)(2,1)}, u32[]{:S(2)}) copy-start(bf16[64,64]{1,0:T(8,128)(2,1)} %param.23) | copy-start | bytes 24580
  255.7 5.7 %copy-start.7 = (bf16[64,64]{1,0:T(8,128)(2,1)S(1)}, bf16[64,64]{1,0:T(8,128)(2,1)}, u32[]{:S(2)}) copy-start(bf16[64,64]{1,0:T(8,128)(2,1)} %param.24) | copy-start | bytes 24580
  255.7 5.8 %copy-start.8 = (bf16[64,64]{1,0:T(8,128)(2,1)S(1)}, bf16[64,64]{1,0:T(8,128)(2,1)}, u32[]{:S(2)}) copy-start(bf16[64,64]{1,0:T(8,128)(2,1)} %param.25) | copy-start | bytes 24580
  255.7 58.5 %all-to-all-start.3 = ((bf16[128,128,128]{2,1,0:T(8,128)(2,1)}), bf16[128,128,128]{2,1,0:T(8,128)(2,1)}, u32[]{:S(2)}, u32[]{:S(2)}) async-start(bf16[128,128,128]{2,1,0:T(8,128)(2,1)} %bitcast.197), calls=%async_computation.3 | async-start | bytes 8388608 | tf_op jit(solution)/shard_map/all_to_all | solution.py:462
  314.2 23.5 %copy-start.3 = (f32[512,128]{1,0:T(8,128)S(1)}, f32[512,128]{1,0:T(8,128)}, u32[]{:S(2)}) copy-start(f32[512,128]{1,0:T(8,128)} %get-tuple-element.64) | copy-start | bytes 786436
  335.6 3.8 copy-start.1
  335.6 3.7 collective-permute-start.2
  340.7 7.6 %copy-start.2 = (f32[2,4,8,1024]{3,2,1,0:T(8,128)S(1)}, f32[2,4,8,1024]{3,2,1,0:T(8,128)}, u32[]{:S(2)}) copy-start(f32[2,4,8,1024]{3,2,1,0:T(8,128)} %get-tuple-element.59) | copy-start | bytes 786436
  340.7 22.8 %all-to-all-start.4 = ((bf16[128,32,128]{2,1,0:T(8,128)(2,1)}), bf16[128,32,128]{2,1,0:T(8,128)(2,1)S(1)}, u32[]{:S(2)}, u32[]{:S(2)}) async-start(bf16[128,32,128]{2,1,0:T(8,128)(2,1)} %add_convert_fusion), calls=%async_computation.4 | async-start | bytes 2097152 | tf_op jit(solution)/shard_map/all_to_all | solution.py:462
  363.5 1.0 copy-start
  373.9 2.3 collective-permute-start.3

commit v3 on v2

v3 whole, which is shorter than its diff:
```python
import jax
import jax.numpy as jnp
import numpy as np
from jax import lax
from jax.experimental import pallas as pl
from jax.experimental.pallas import tpu as pltpu
from jax.sharding import PartitionSpec as P

EPS = 1e-05
HIGHEST = lax.Precision.HIGHEST
F32 = jnp.float32
BF = jnp.bfloat16
AXES = ("row", "col")
VMEM = 60 * 2**20

C = 64
T = 4
H = 64
W = 128
N = 1024
K8 = C * 8
ROWS = 288


def params():
    return pltpu.CompilerParams(vmem_limit_bytes=VMEM)


def stack_rows(top, bottom):
    return jnp.concatenate([top.reshape(K8, W), bottom.reshape(K8, W)], axis=1)


def unstack_rows(wide):
    return wide[:, :W].reshape(C, 8, W), wide[:, W:].reshape(C, 8, W)


def join_rows(top, bottom):
    return jnp.concatenate([top, bottom], axis=1)


def halves(value):
    return value[:, :8, :], value[:, 8:, :]


def mean_channels(value):
    return jnp.sum(value, axis=0, keepdims=True) * (1.0 / C)


def whole_spec(*shape):
    return pl.BlockSpec(shape, lambda t: (0,) * len(shape))


def each_spec(*shape):
    return pl.BlockSpec((1, *shape), lambda t: (t,) + (0,) * len(shape))


def row_mask(width):
    lane = lax.broadcasted_iota(jnp.int32, (8, width), 1)
    return (lane % 8 == lax.broadcasted_iota(jnp.int32, (8, width), 0)).astype(F32)


def spread_terms(left_ref, right_ref, right):
    mask = row_mask(W)
    rows = []
    for c in range(C):
        right[c] = jnp.broadcast_to(right_ref[0, c : c + 1, :], (8, W))
        rows.append(jnp.broadcast_to(left_ref[0, c : c + 1, :], (8, W)) * mask)
    value = jnp.concatenate(rows, axis=0)
    rest = value - value.astype(BF).astype(F32)
    lane = lax.broadcasted_iota(jnp.int32, (K8, W), 1)
    return jnp.where(lane < H, value, rest).astype(BF)


def make_pairs(pair_ref, left, lanes_ref, right, g):
    terms = unstack_rows(jnp.dot(left, lanes_ref[g], preferred_element_type=F32))
    raw = halves(pair_ref[0, :, g * 16 : g * 16 + 16, :].astype(F32))
    return [raw[part] + terms[part] + right[...] for part in range(2)]


def norm_kernel(
    pair_ref, left_ref, right_ref, lanes_ref, gain_ref, kl_ref, kr_ref, pay_ref, inv_ref, right
):
    left = spread_terms(left_ref, right_ref, right)
    for g in range(4):
        scaleds, invs = [], []
        for pair in make_pairs(pair_ref, left, lanes_ref, right, g):
            shifted = pair - mean_channels(pair)
            inverse = lax.rsqrt(mean_channels(shifted * shifted) + EPS)
            scaleds.append(shifted * inverse * gain_ref[...])
            invs.append(inverse[0])
        both = jnp.concatenate(invs, axis=0)
        inv_ref[0, g * 16 : g * 16 + 16, :] = both
        wide = stack_rows(*scaleds).astype(BF)
        for k, weight in enumerate((kl_ref, kr_ref)):
            out = jnp.dot(weight[...], wide, preferred_element_type=F32)
            out = join_rows(*unstack_rows(out)).astype(BF).reshape(C // 2, 2, 16, W)
            for s in range(2):
                first = k * 128 + s * 64 + g * 16
                pay_ref[0, :, first : first + 16, :] = out[:, s]
        first = 256 + (g % 2) * 16
        for q in range(g // 2, C // 2, 2):
            pay_ref[0, q, first : first + 16, :] = both.astype(BF)


TERM_SPECS = [each_spec(C, H, W), each_spec(C, W), each_spec(C, W), whole_spec(4, W, 2 * W), whole_spec(C, 8, W)]


def run_norm(pair, left, right, lanes, gain, kl, kr):
    return pl.pallas_call(
        norm_kernel,
        grid=(T,),
        in_specs=[*TERM_SPECS, whole_spec(K8, K8), whole_spec(K8, K8)],
        out_specs=[each_spec(C // 2, ROWS, W), each_spec(H, W)],
        out_shape=[
            jax.ShapeDtypeStruct((T, C // 2, ROWS, W), BF),
            jax.ShapeDtypeStruct((T, H, W), F32),
        ],
        scratch_shapes=[pltpu.VMEM((C, 8, W), F32)],
        compiler_params=params(),
        name="pair_norm",
    )(pair, left, right, lanes, gain, kl, kr)


def spread(blocks_ref, full_ref):
    @pl.loop(0, 16)
    def _(r):
        for c in range(8):
            full_ref[pl.ds(r * H, H), c * W : (c + 1) * W] = blocks_ref[r * 8 + c]


def product_kernel(left_ref, right_ref, out_ref, left, right):
    spread(left_ref, left)
    spread(right_ref, right)

    out = lax.dot_general(
        left[...], right[...], (((1,), (1,)), ((), ())), preferred_element_type=F32
    ).astype(BF)
    for r in range(16):
        for c in range(8):
            out_ref[r * 8 + c] = out[r * H : (r + 1) * H, c * W : (c + 1) * W]


def run_product(factors):
    spec = lambda first: pl.BlockSpec((128, H, W), lambda s: (0, first + s, 0))
    return pl.pallas_call(
        product_kernel,
        grid=(2,),
        in_specs=[spec(0), spec(2)],
        out_specs=pl.BlockSpec((128, H, W), lambda s: (0, s, 0)),
        out_shape=jax.ShapeDtypeStruct((128, 2 * H, W), BF),
        scratch_shapes=[pltpu.VMEM((N, N), BF), pltpu.VMEM((N, N), BF)],
        compiler_params=params(),
        name="triangle_product",
    )(factors, factors)


def back_kernel(
    pair_ref, left_ref, right_ref, lanes_ref, gain_ref, inv_ref, grad_ref, kg_ref, kb_ref,
    scaled_ref, out_ref, sum_ref, right,
):
    step = pl.program_id(0)
    left = spread_terms(left_ref, right_ref, right)

    @pl.when(step == 0)
    def _():
        sum_ref[...] = jnp.zeros_like(sum_ref)

    for g in range(4):
        rows = slice(g * 16, g * 16 + 16)
        pairs = make_pairs(pair_ref, left, lanes_ref, right, g)
        sum_ref[:, rows, :] += join_rows(*pairs)
        scaleds = []
        for part in range(2):
            first = g * 16 + part * 8
            inverse = inv_ref[0, first : first + 8, :][None]
            scaleds.append((pairs[part] - mean_channels(pairs[part])) * inverse * gain_ref[...])
        scaled_ref[0, :, rows, :] = join_rows(*scaleds).astype(BF)
        opened = unstack_rows(
            jnp.dot(kg_ref[...], stack_rows(*scaleds).astype(BF), preferred_element_type=F32)
        )
        grads = halves(grad_ref[:, rows, :].astype(F32))
        grad_projs = [
            grads[part] * (1.0 / T) * jax.nn.sigmoid(opened[part]) for part in range(2)
        ]
        grad_norms = unstack_rows(
            jnp.dot(kb_ref[...], stack_rows(*grad_projs).astype(BF), preferred_element_type=F32)
        )
        outs = [grad_norm - mean_channels(grad_norm) for grad_norm in grad_norms]
        out_ref[0, :, rows, :] = join_rows(*outs).astype(BF)


def run_back(pair, left, right, lanes, gain, inv, grad, kg, kb):
    return pl.pallas_call(
        back_kernel,
        grid=(T,),
        in_specs=[
            *TERM_SPECS, each_spec(H, W), whole_spec(C, H, W), whole_spec(K8, K8), whole_spec(K8, K8)
        ],
        out_specs=[each_spec(C, H, W), each_spec(C, H, W), whole_spec(C, H, W)],
        out_shape=[
            jax.ShapeDtypeStruct((T, C, H, W), BF),
            jax.ShapeDtypeStruct((T, C, H, W), BF),
            jax.ShapeDtypeStruct((C, H, W), F32),
        ],
        scratch_shapes=[pltpu.VMEM((C, 8, W), F32)],
        compiler_params=params(),
        cost_estimate=pl.CostEstimate(flops=4 * 2**31, bytes_accessed=16 * 2**20, transcendentals=2**21),
        name="back_project",
    )(pair, left, right, lanes, gain, inv, grad, kg, kb)


def product_norm(product):
    shifted = product - mean_channels(product)
    return shifted, lax.rsqrt(mean_channels(shifted * shifted) + EPS)


def grad_kernel(prod_ref, back_ref, out_ref):
    for g in range(4):
        rows = slice(g * 16, g * 16 + 16)
        shifted, inverse = product_norm(prod_ref[0, :, rows, :].astype(F32))
        back = back_ref[0, :, rows, :].astype(F32)
        slope = mean_channels(back * shifted) * inverse * inverse
        out_ref[0, :, rows, :] = ((back - shifted * slope) * inverse).astype(BF)


def run_grad(prod, back):
    return pl.pallas_call(
        grad_kernel,
        grid=(T,),
        in_specs=[each_spec(C, H, W), each_spec(C, H, W)],
        out_specs=each_spec(C, H, W),
        out_shape=jax.ShapeDtypeStruct((T, C, H, W), BF),
        compiler_params=params(),
        cost_estimate=pl.CostEstimate(flops=2**25, bytes_accessed=12 * 2**20, transcendentals=0),
        name="product_grad",
    )(prod, back)


def fold_rows(sums):
    return jnp.sum(sums.reshape(C, 8, W) * row_mask(W)[None], axis=1)


def gate_kernel(
    prod_ref, scaled_ref, grad_ref, sum_ref, inv_ref, kg_ref, ko_ref, pick_ref,
    emb_ref, mean_ref, rows_ref, cols_ref, grows_ref, gcols_ref, total,
):
    step = pl.program_id(0)
    row_sums = jnp.zeros((K8, W), F32)
    col_sums = jnp.zeros((C, 8, W), F32)
    for g in range(4):
        rows = slice(g * 16, g * 16 + 16)
        scaled = stack_rows(*halves(scaled_ref[0, :, rows, :].astype(F32))).astype(BF)
        opened = unstack_rows(jnp.dot(kg_ref[...], scaled, preferred_element_type=F32))
        normed = []
        for product in halves(prod_ref[0, :, rows, :].astype(F32)):
            shifted, inverse = product_norm(product)
            normed.append(shifted * inverse)
        projected = unstack_rows(
            jnp.dot(ko_ref[...], stack_rows(*normed).astype(BF), preferred_element_type=F32)
        )
        grads = halves(grad_ref[:, rows, :].astype(F32))
        weighted = []
        for part in range(2):
            first = g * 16 + part * 8
            where = (slice(None), slice(first, first + 8), slice(None))
            gate = jax.nn.sigmoid(opened[part])
            gated = gate * projected[part]

            @pl.when(step == 0)
            def _():
                total[where] = sum_ref[where] + gated

            @pl.when(step > 0)
            def _():
                total[where] += gated

            grad_gate = grads[part] * (1.0 / T) * gated * (1.0 - gate)
            mean_ref[0, first : first + 8, :] = jnp.sum(grad_gate * opened[part], axis=0)
            term = grad_gate * inv_ref[0, first : first + 8, :][None]
            col_sums = col_sums + term
            weighted.append(term)
        row_sums = row_sums + jnp.dot(
            stack_rows(*weighted).astype(BF), pick_ref[g], preferred_element_type=F32
        )
    rows_ref[0] = fold_rows(row_sums)
    cols_ref[0] = jnp.sum(col_sums, axis=1)

    @pl.when(step == 0)
    def _():
        grad_rows = jnp.zeros((K8, W), F32)
        grad_cols = jnp.zeros((C, 8, W), F32)
        for g in range(4):
            top, bottom = halves(grad_ref[:, g * 16 : g * 16 + 16, :].astype(F32))
            grad_cols = grad_cols + top + bottom
            grad_rows = grad_rows + jnp.dot(
                stack_rows(top, bottom).astype(BF), pick_ref[g], preferred_element_type=F32
            )
        grows_ref[...] = fold_rows(grad_rows)
        gcols_ref[...] = jnp.sum(grad_cols, axis=1)

    @pl.when(step == T - 1)
    def _():
        emb_ref[...] = (total[...] * (1.0 / T)).astype(BF)


def run_gate(prod, scaled, grad, pair_sum, inv, kg, ko, pick):
    return pl.pallas_call(
        gate_kernel,
        grid=(T,),
        in_specs=[
            each_spec(C, H, W), each_spec(C, H, W), whole_spec(C, H, W), whole_spec(C, H, W),
            each_spec(H, W), whole_spec(K8, K8), whole_spec(K8, K8), whole_spec(4, 2 * W, W),
        ],
        out_specs=[
            whole_spec(C, H, W), each_spec(H, W), each_spec(C, W), each_spec(C, W),
            whole_spec(C, W), whole_spec(C, W),
        ],
        out_shape=[
            jax.ShapeDtypeStruct((C, H, W), BF),
            jax.ShapeDtypeStruct((T, H, W), F32),
            jax.ShapeDtypeStruct((T, C, W), F32),
            jax.ShapeDtypeStruct((T, C, W), F32),
            jax.ShapeDtypeStruct((C, W), F32),
            jax.ShapeDtypeStruct((C, W), F32),
        ],
        scratch_shapes=[pltpu.VMEM((C, H, W), F32)],
        compiler_params=params(),
        cost_estimate=pl.CostEstimate(flops=4 * 2**31, bytes_accessed=12 * 2**20, transcendentals=2**21),
        name="gate_and_embed",
    )(prod, scaled, grad, pair_sum, inv, kg, ko, pick)


def square_kernel(left_ref, right_ref, inv_ref, left, right, inv):
    step = pl.program_id(0)
    spread(left_ref, left.at[0])
    spread(right_ref, right.at[0])

    @pl.when(step == 0)
    def _():
        spread(inv_ref, inv)


def run_square(factors, inv):
    spec = lambda first: pl.BlockSpec((128, H, W), lambda s: (0, first + s, 0))
    out = pl.BlockSpec((1, N, N), lambda s: (s, 0, 0))
    return pl.pallas_call(
        square_kernel,
        grid=(2,),
        in_specs=[spec(0), spec(2), pl.BlockSpec((128, H, W), lambda s: (0, 0, 0))],
        out_specs=[out, out, pl.BlockSpec((N, N), lambda s: (0, 0))],
        out_shape=[jax.ShapeDtypeStruct((2, N, N), BF)] * 2 + [jax.ShapeDtypeStruct((N, N), BF)],
        compiler_params=params(),
        cost_estimate=pl.CostEstimate(flops=2**20, bytes_accessed=20 * 2**20, transcendentals=0),
        name="to_matrices",
    )(factors, factors, inv)


def factor_kernel(
    core_ref, left_ref, right_ref, grad_ref, inv_ref,
    kept_ref, given_ref, cols_ref, rows_ref, grad, mean,
):
    step = pl.program_id(0)
    core = core_ref[0]
    left, right = left_ref.at[0], right_ref.at[0]
    spread(grad_ref, grad)

    @pl.when(step == 0)
    def _():
        mean[...] = jnp.zeros_like(mean)

    def finish(value, rows, factor, kind):
        mean[rows, :] += value * factor[rows, :].astype(F32)
        term = value * inv_ref[rows, :].astype(F32)
        part = jnp.sum(term.reshape(64, 8, N), axis=0)
        lanes = term[:, :W]
        for c in range(1, 8):
            lanes = lanes + term[:, c * W : (c + 1) * W]
        rows_ref[0, kind, rows, :] = lanes
        return part

    blocks = [slice(b * 512, b * 512 + 512) for b in range(2)]
    total = None
    for rows in blocks:
        value = jnp.dot(grad[rows, :], right[...], preferred_element_type=F32)
        part = finish(value, rows, left, 0)
        total = part if total is None else total + part
    cols_ref[0, 0] = total
    total = None
    for rows in blocks:
        value = lax.dot_general(
            grad[:, rows], left[...], (((0,), (0,)), ((), ())), preferred_element_type=F32
        )
        part = finish(value, rows, right, 1)
        total = part if total is None else total + part
    cols_ref[0, 1] = total

    @pl.when(step == 1)
    def _():
        @pl.loop(0, 16)
        def _(r):
            mine = pl.ds(pl.multiple_of(r * H + core * 32, 32), 32)
            other = pl.ds(pl.multiple_of(r * H + (1 - core) * 32, 32), 32)
            for c in range(8):
                kept_ref[r * 8 + c] = mean[mine, c * W : (c + 1) * W].astype(BF)
                given_ref[r * 8 + c] = mean[other, c * W : (c + 1) * W].astype(BF)


def run_factor(core, left, right, grad, inv):
    matrix = pl.BlockSpec((1, N, N), lambda s: (s, 0, 0))
    return pl.pallas_call(
        factor_kernel,
        grid=(2,),
        in_specs=[
            pl.BlockSpec(memory_space=pltpu.SMEM),
            matrix,
            matrix,
            pl.BlockSpec((128, H, W), lambda s: (0, s, 0)),
            pl.BlockSpec((N, N), lambda s: (0, 0)),
        ],
        out_specs=[
            pl.BlockSpec((128, H // 2, W), lambda s: (0, 0, 0)),
            pl.BlockSpec((128, H // 2, W), lambda s: (0, 0, 0)),
            pl.BlockSpec((1, 2, 8, N), lambda s: (s, 0, 0, 0)),
            pl.BlockSpec((1, 2, N, W), lambda s: (s, 0, 0, 0)),
        ],
        out_shape=[
            jax.ShapeDtypeStruct((128, H // 2, W), BF),
            jax.ShapeDtypeStruct((128, H // 2, W), BF),
            jax.ShapeDtypeStruct((2, 2, 8, N), F32),
            jax.ShapeDtypeStruct((2, 2, N, W), F32),
        ],
        scratch_shapes=[pltpu.VMEM((N, N), BF), pltpu.VMEM((N, N), F32)],
        compiler_params=params(),
        name="factor_grads",
    )(core.reshape(1), left, right, grad, inv)


def close_kernel(
    recv_ref, mean_ref, inv_ref, scaled_ref, pick_ref, weight_ref, valid_ref, base_ref, out_ref
):
    got = recv_ref[0].astype(F32)
    total = got[0]
    for k in range(1, 16):
        total = total + got[k]
    weight = (total.reshape(H, W) + mean_ref[0]) * inv_ref[0] * (1.0 / C)
    row_sums = jnp.zeros((K8, W), F32)
    col_sums = jnp.zeros((C, 8, W), F32)
    for g in range(4):
        scaled = scaled_ref[0, :, g * 16 : g * 16 + 16, :].astype(F32)
        terms = []
        for part in range(2):
            first = g * 16 + part * 8
            term = scaled[:, part * 8 : part * 8 + 8, :] * weight[first : first + 8, :][None]
            col_sums = col_sums + term
            terms.append(term)
        row_sums = row_sums + jnp.dot(
            stack_rows(*terms).astype(BF), pick_ref[g], preferred_element_type=F32
        )
    for side, sums in enumerate((fold_rows(row_sums), jnp.sum(col_sums, axis=1))):
        value = jnp.dot(weight_ref[side], sums, precision=HIGHEST, preferred_element_type=F32)
        out_ref[side, 0] = (base_ref[side, 0] + value * valid_ref[side, 0]).astype(BF)


def run_close(recv, mean, inv, scaled, pick, weights, valid, base):
    both = lambda *shape: pl.BlockSpec((2, 1, *shape), lambda t: (0, t) + (0,) * len(shape))
    return pl.pallas_call(
        close_kernel,
        grid=(T,),
        in_specs=[
            each_spec(16, 2, H // 2, W), each_spec(H, W), each_spec(H, W), each_spec(C, H, W),
            whole_spec(4, 2 * W, W), whole_spec(2, C, C), both(1, W), both(C, W),
        ],
        out_specs=both(C, W),
        out_shape=jax.ShapeDtypeStruct((2, T, C, W), BF),
        compiler_params=params(),
        name="close_sums",
    )(recv, mean, inv, scaled, pick, weights, valid, base)


def from_member(value, k):
    return lax.ppermute(value, "col", [(i, i ^ k) for i in range(8)])


def swap_cores(value):
    return from_member(value, 1)


def exchange(value):
    return lax.all_to_all(value, AXES, split_axis=0, concat_axis=0, tiled=True)


def in_order(core, mine, other, axis):
    first = jnp.where(core == 0, mine, other)
    second = jnp.where(core == 0, other, mine)
    return jnp.concatenate([first, second], axis=axis)


def by_member(value, member):
    lead, last = value.shape[:-2], value.shape[-1]
    cut = value.reshape(*lead, 2, 2, 16, last)
    cut = jnp.where(member % 2 == 1, cut[..., ::-1, :, :], cut)
    cut = jnp.where(member // 2 == 1, cut[..., ::-1, :, :, :], cut)
    return cut.reshape(*lead, 64, last)


def expand(weights):
    to = jnp.asarray(np.kron(np.eye(C), np.ones((8, 1))), BF)
    tall = jnp.einsum("ac,ncd->nad", to, weights, preferred_element_type=F32).astype(BF)
    wide = jnp.einsum("nad,bd->nab", tall, to, preferred_element_type=F32)
    index = jnp.arange(K8, dtype=jnp.int32) % 8
    return jnp.where(index[:, None] == index[None, :], wide, 0.0).astype(BF)


def per_device(
    template_pair,
    template_feat,
    block_map,
    block_count,
    residue_mask,
    row_embed,
    col_embed,
    norm_gain,
    left_proj,
    right_proj,
    gate_proj,
    out_proj,
    embed_grad,
):
    row = lax.axis_index("row")
    col = lax.axis_index("col")
    core = col % 2
    me = row * 8 + col
    own = me // 32
    pair_at = me % 32
    blocks = jnp.arange(128, dtype=jnp.int32)
    half = row % 2
    row_block = row // 2

    member = col % 4
    sent_feat = jnp.broadcast_to(template_feat.reshape(1, 4, 16, W), (32, 4, 16, W))
    pool = exchange(sent_feat.reshape(128, 16, W))
    column_ids = lambda m, at: lax.dynamic_index_in_dim(m, at, axis=1, keepdims=False)
    row_ids = column_ids(block_map, row_block)
    member_ids = [column_ids(block_map, col ^ k) for k in range(4)]
    wanted = jnp.concatenate([jnp.concatenate([ids, row_ids]) for ids in member_ids])
    choose = (wanted[:, None] == blocks[None, :]).astype(BF)
    picked = jnp.einsum(
        "eb,bx->ex", choose, pool.reshape(128, 16 * W), preferred_element_type=F32
    ).astype(BF)
    picked = picked.reshape(4, 8, 16, W)
    feats = jnp.concatenate(
        [picked[0]] + [from_member(picked[k], k) for k in range(1, 4)], axis=1
    )
    embeds = by_member(jnp.stack([row_embed, col_embed]), member)

    offsets = jnp.arange(W, dtype=jnp.int32)

    def marks(at):
        kept = lax.dynamic_slice_in_dim(residue_mask, at * W, W, axis=1) == 1
        return kept & (offsets[None, :] < column_ids(block_count, at)[:, None])

    col_valid = marks(col).astype(F32)
    row_valid = (marks(row_block) & (offsets // H == half)[None, :]).astype(F32)
    left_terms = jnp.einsum("fc,tfi->tci", embeds[0], feats[4:], preferred_element_type=F32)
    left_terms = left_terms * row_valid[:, None, :]
    near, far = left_terms[:, :, :H], left_terms[:, :, H:]
    left_twice = near + far
    left_twice = jnp.concatenate([left_twice, left_twice], axis=2)
    right_terms = jnp.einsum("fc,tfj->tcj", embeds[1], feats[:4], preferred_element_type=F32)
    right_terms = right_terms * col_valid[:, None, :]
    gain = norm_gain.astype(F32)
    gain_wide = jnp.broadcast_to(gain[:, None, None], (C, 8, W))
    kl, kr, kg, ko, kb = expand(
        jnp.stack([left_proj.T, right_proj.T, gate_proj.T, out_proj.T, out_proj])
    )
    group = 2 * np.arange(4)[:, None, None] + (np.arange(2 * W) // W)[None, :, None]
    lanes = np.arange(W)[None, None, :] % H // 8 == group
    terms_pick = jnp.asarray(lanes.transpose(0, 2, 1), BF)
    sums_pick = jnp.where((offsets // H == half)[None, None, :], jnp.asarray(lanes, BF), 0)

    terms = (template_pair, left_twice, right_terms, terms_pick, gain_wide)
    sent, inv = run_norm(*terms, kl, kr)
    factors = exchange(sent.reshape(128, ROWS, W))
    scaled, back, pair_sum = run_back(*terms, inv, embed_grad, kg, kb)
    factors, scaled, back, pair_sum = lax.optimization_barrier((factors, scaled, back, pair_sum))
    my_inv = factors[:, 256:]
    inv_all = in_order(core, my_inv, swap_cores(my_inv), 1)
    prod = exchange(run_product(factors)).reshape(T, C, H, W)
    left, right, inv_matrix = run_square(factors, inv_all)
    prod, left, right, inv_matrix = lax.optimization_barrier((prod, left, right, inv_matrix))
    grads = exchange(run_grad(prod, back).reshape(128, 2 * H, W))
    embedding, gate_mean, gate_rows, gate_cols, out_rows, out_cols = run_gate(
        prod, scaled, embed_grad, pair_sum, inv, kg, ko, sums_pick
    )
    grads, embedding, gate_mean, gate_rows, gate_cols, out_rows, out_cols = (
        lax.optimization_barrier(
            (grads, embedding, gate_mean, gate_rows, gate_cols, out_rows, out_cols)
        )
    )
    kept, given, col_sums, row_sums = run_factor(core, left, right, grads, inv_matrix)
    mean_half = (kept.astype(F32) + swap_cores(given).astype(F32)).astype(BF)
    col_sums, row_sums, mean_half = lax.optimization_barrier((col_sums, row_sums, mean_half))
    recv = exchange(mean_half).reshape(T, 16, 2, H // 2, W)

    def center(weights):
        scaled_weights = gain[:, None] * weights.astype(F32)
        return scaled_weights - jnp.mean(scaled_weights, axis=0, keepdims=True)

    embeds = embeds.astype(F32)
    mixed = jnp.einsum(
        "efd,kdc->kefc",
        embeds,
        jnp.stack([center(left_proj), center(right_proj), center(gate_proj)]),
        precision=HIGHEST,
    )
    closing = -embeds / gain[None, None, :]
    opening = embeds * (1.0 / T)
    valid = jnp.stack([row_valid, col_valid])[:, :, None, :]
    base = jnp.einsum(
        "efc,etcp->etfp", mixed[2], jnp.stack([gate_rows, gate_cols]), precision=HIGHEST
    )
    opened = jnp.einsum(
        "efc,ecp->efp", opening, jnp.stack([out_rows, out_cols]), precision=HIGHEST
    )
    base = (base + opened[:, None]) * valid
    owned = jnp.stack([jnp.sum(row_sums, axis=3), jnp.sum(col_sums, axis=2)], axis=2)
    weights = lax.dynamic_slice_in_dim(mixed[:2], 2 * pair_at, 2, axis=3)
    grad_own = jnp.einsum("kefs,sken->fn", weights, owned, precision=HIGHEST)
    own_map = lax.dynamic_index_in_dim(block_map, own, axis=0, keepdims=False)
    own_count = lax.dynamic_index_in_dim(block_count, own, axis=0, keepdims=False)
    own_marks = lax.dynamic_index_in_dim(residue_mask, own, axis=0, keepdims=False)
    own_valid = (offsets[None, :] < own_count[:, None]) & (own_marks.reshape(8, W) == 1)
    grad_own = grad_own.reshape(C, 8, W).transpose(1, 0, 2) * own_valid.astype(F32)[:, None, :]
    grad_own = grad_own.astype(BF)
    targets = jnp.concatenate([jnp.concatenate([own_map, row_ids, ids]) for ids in member_ids])
    place = (targets[None, :] == blocks[:, None]).astype(BF)
    recv, base, grad_own, place = lax.optimization_barrier((recv, base, grad_own, place))

    closed = run_close(recv, gate_mean, inv, scaled, sums_pick, closing, valid, base)
    entries = jnp.concatenate([grad_own, closed.reshape(2 * T, C, W)], axis=0)
    quarters = [entries[:, k * 16 : k * 16 + 16] for k in range(4)]
    entries = jnp.concatenate(
        [quarters[0]] + [from_member(quarters[k], k) for k in range(1, 4)], axis=0
    )
    placed = jnp.einsum(
        "be,ex->bx", place, entries.reshape(64, 16 * W), preferred_element_type=F32
    ).astype(BF)
    result = exchange(placed.reshape(128, 16, W)).reshape(32, 4 * 16, W)
    feat_grad = jnp.sum(result.astype(F32), axis=0)[None]
    return (embedding, feat_grad)


def solution(mesh):
    return jax.shard_map(
        per_device,
        mesh=mesh,
        in_specs=(
            P(None, None, "row", "col"),
            P(("row", "col"), None, None),
            P(),
            P(),
            P(),
            P(),
            P(),
            P(),
            P(),
            P(),
            P(),
            P(),
            P(None, "row", "col"),
        ),
        out_specs=(P(None, "row", "col"), P(("row", "col"), None, None)),
        check_vma=False,
    )
```

time: 402 us -> 391 us (0.973)
  starting transfers between devices: 38.6 us -> 46.3 us
  waiting for transfers between devices: 190 us -> 183 us
  blocking collectives: 22.4 us -> 17 us
  local copies, waits for them, and re-layouts: 21.7 us -> 16.7 us
    all_to_all x5, waiting for transfers between devices: 187 us -> 175 us  [exchange(): return lax.all_to_all(value, AXES, split_axis=0, concat_axis=0, tiled=True)]
    ppermute x4 -> x8, waiting for transfers between devices: 2.66 us -> 8.05 us  [from_member(): return lax.ppermute(value, 'col', [(i, i ^ k) for i in range(8)])]
    all_to_all x1, blocking collectives: 22.4 us -> 17 us  [exchange(): return lax.all_to_all(value, AXES, split_axis=0, concat_axis=0, tiled=True)]
    reshape x7 -> x0, local copies, waits for them, and re-layouts: 4.77 us -> none  [the longest x6 3.43 us: lane_rows(): cut = sums[..., :8].reshape(*lead, C, 8, 8)]
    all_to_all x5, starting transfers between devices: 33.7 us -> 38.2 us  [exchange(): return lax.all_to_all(value, AXES, split_axis=0, concat_axis=0, tiled=True)]
    pallas_call x1, Pallas kernels: 21.4 us -> 17.3 us  [run_factor(): pl.pallas_call(factor_kernel, grid=(2,), in_specs=[pl.BlockSpec(memory_sp...]
    ppermute x4 -> x8, starting transfers between devices: 4.97 us -> 8.08 us  [from_member(): return lax.ppermute(value, 'col', [(i, i ^ k) for i in range(8)])]
  transfers between devices with their start and end apart: 9 -> 13, of which waited for: 8 -> 10; matrix products, arithmetic and copies ran while one was open for 7% -> 7% of each run, Pallas kernels for 10% -> 12%
where the time goes in v3:
time: 391 us; the launch traced here: 390 us
  waiting for transfers between devices  183 us (47%)
  Pallas kernels  102 us (26%)
  starting transfers between devices  46.3 us (12%)
  blocking collectives  17 us (4%)
  local copies, waits for them, and re-layouts  16.7 us (4%)
  other arithmetic  15.1 us (4%)
  matrix products  7.99 us (2%)
    all_to_all x5, waiting for transfers between devices, exchange(): return lax.all_to_all(value, AXES, split_axis=0, concat_axis=0, tiled=True)  175 us
    all_to_all x5, starting transfers between devices, exchange(): return lax.all_to_all(value, AXES, split_axis=0, concat_axis=0, tiled=True)  38.2 us
    pallas_call x1, Pallas kernels, run_gate(): pl.pallas_call(gate_kernel, grid=(T,), in_specs=[each_spec(C, H, W), each...  22.5 us
    pallas_call x1, Pallas kernels, run_factor(): pl.pallas_call(factor_kernel, grid=(2,), in_specs=[pl.BlockSpec(memory_sp...  17.3 us
    all_to_all x1, blocking collectives, exchange(): return lax.all_to_all(value, AXES, split_axis=0, concat_axis=0, tiled=True)  17 us
    pallas_call x1, Pallas kernels, run_back(): pl.pallas_call(back_kernel, grid=(T,), in_specs=[*TERM_SPECS, each_spec(H...  16 us
    pallas_call x1, Pallas kernels, run_norm(): pl.pallas_call(norm_kernel, grid=(T,), in_specs=[*TERM_SPECS, whole_spec(...  14.5 us
    pallas_call x1, Pallas kernels, run_product(): pl.pallas_call(product_kernel, grid=(2,), in_specs=[spec(0), spec(2)], ou...  10.2 us
  transfers between devices with their start and end apart: 13, of which 10 were waited for; matrix products, arithmetic and copies ran while one was open for 7% of the time, Pallas kernels for 12%

profile of v3, /device:TPU:1, one launch (start us, length us, event | category | flops | bytes accessed | tf_op | source)
XLA Modules:
  0.0 389.7 jit_solution(12134243152296575074)
XLA Ops:
  0.7 1.6 broadcast_in_dim.31
  2.3 11.5 %all-to-all-start = ((bf16[128,16,128]{2,1,0:T(8,128)(2,1)}), bf16[128,16,128]{2,1,0:T(8,128)(2,1)S(1)}, u32[]{:S(2)}, u32[]{:S(2)}) async-start(bf16[128,16,128]{2,1,0:T(8,128)(2,1)} %bitcast.1), calls=%async_computation | async-start | bytes 1048576 | tf_op jit(solution)/shard_map/all_to_all | solution.py:489
  16.9 1.3 constant_dynamic-update-slice_fusion.6
  21.7 2.0 select_convert_fusion
  25.2 1.5 slice_bitcast_fusion
  29.0 1.5 collective-permute-start.2
  35.6 14.5 %pair_norm.1 = (bf16[4,32,288,128]{3,2,1,0:T(8,128)(2,1)}, f32[4,64,128]{2,1,0:T(8,128)}) custom-call(bf16[4,64,64,128]{3,2,1,0:T(8,128)(2,1)} %pair_ref.3, f32[4,64,128]{2,1,0:T(8,128)} %pad_maximum_fusion.2.left_ref, f32[4,64,128]{2,1,0:T(8,128)} %fusion.4.right_ref, bf16[4,128,256]{2,1,0:T(8,128)(2,1)} %constant.168.clone.lanes_ref, ...), custom_call_target="tpu_custom_call" | custom-call | tf_op jit(solution)/shard_map/pair_norm/pallas_call | solution.py:109
  50.1 9.5 %all-to-all-start.1 = ((bf16[128,288,128]{2,1,0:T(8,128)(2,1)}), bf16[128,288,128]{2,1,0:T(8,128)(2,1)}, u32[]{:S(2)}, u32[]{:S(2)}) async-start(bf16[128,288,128]{2,1,0:T(8,128)(2,1)} %bitcast.149), calls=%async_computation.1 | async-start | bytes 18874368 | tf_op jit(solution)/shard_map/all_to_all | solution.py:489
  59.6 16.0 %back_project.1 = (bf16[4,64,64,128]{3,2,1,0:T(8,128)(2,1)}, bf16[4,64,64,128]{3,2,1,0:T(8,128)(2,1)}, f32[64,64,128]{2,1,0:T(8,128)}) custom-call(bf16[4,64,64,128]{3,2,1,0:T(8,128)(2,1)} %pair_ref.3, f32[4,64,128]{2,1,0:T(8,128)} %pad_maximum_fusion.2.left_ref, f32[4,64,128]{2,1,0:T(8,128)} %fusion.4.right_ref, ...), custom_call_target="tpu_custom_call" | custom-call | flops 8589934592 | bytes 16777216 | tf_op jit(solution)/shard_map/back_project/pallas_call | solution.py:193
  75.6 96.2 %all-to-all-done.1.left_ref.right_ref = bf16[128,288,128]{2,1,0:T(8,128)(2,1)} async-done(((bf16[128,288,128]{2,1,0:T(8,128)(2,1)}), bf16[128,288,128]{2,1,0:T(8,128)(2,1)}, u32[]{:S(2)}, u32[]{:S(2)}) %all-to-all-start.1) | async-done | bytes 9437216 | tf_op jit(solution)/shard_map/all_to_all | solution.py:489
  171.8 10.2 %triangle_product.1 = bf16[128,128,128]{2,1,0:T(8,128)(2,1)} custom-call(bf16[128,288,128]{2,1,0:T(8,128)(2,1)} %all-to-all-done.1.left_ref.right_ref, bf16[128,288,128]{2,1,0:T(8,128)(2,1)} %all-to-all-done.1.left_ref.right_ref), custom_call_target="tpu_custom_call" | custom-call | tf_op jit(solution)/shard_map/triangle_product/pallas_call | solution.py:145
  182.0 7.9 %all-to-all-start.2 = ((bf16[128,128,128]{2,1,0:T(8,128)(2,1)}), bf16[128,128,128]{2,1,0:T(8,128)(2,1)}, u32[]{:S(2)}, u32[]{:S(2)}) async-start(bf16[128,128,128]{2,1,0:T(8,128)(2,1)} %triangle_product.1), calls=%async_computation.2 | async-start | bytes 8388608 | tf_op jit(solution)/shard_map/all_to_all | solution.py:489
  192.4 2.3 collective-permute-done.3
  194.7 1.4 broadcast_select_fusion.1
  196.1 1.6 pad_maximum_fusion.inv_ref
  197.7 8.1 %to_matrices.1 = (bf16[2,1024,1024]{2,1,0:T(8,128)(2,1)}, bf16[2,1024,1024]{2,1,0:T(8,128)(2,1)}, bf16[1024,1024]{1,0:T(8,128)(2,1)}) custom-call(bf16[128,288,128]{2,1,0:T(8,128)(2,1)} %all-to-all-done.1.left_ref.right_ref, bf16[128,288,128]{2,1,0:T(8,128)(2,1)} %all-to-all-done.1.left_ref.right_ref, bf16[128,64,128]{2,1,0:T(8,128)(2,1)} %pad_maximum_fusion.inv_ref), custom_call_target="tpu_custom_call" | custom-call | flops 1048576 | bytes 20971520 | tf_op jit(solution)/shard_map/to_matrices/pallas_call | solution.py:346
  205.8 36.9 %all-to-all-done.2 = bf16[128,128,128]{2,1,0:T(8,128)(2,1)} async-done(((bf16[128,128,128]{2,1,0:T(8,128)(2,1)}), bf16[128,128,128]{2,1,0:T(8,128)(2,1)}, u32[]{:S(2)}, u32[]{:S(2)}) %all-to-all-start.2) | async-done | bytes 4194336 | tf_op jit(solution)/shard_map/all_to_all | solution.py:489
  242.7 7.9 %product_grad.1 = bf16[4,64,64,128]{3,2,1,0:T(8,128)(2,1)} custom-call(bf16[4,64,64,128]{3,2,1,0:T(8,128)(2,1)} %bitcast.30.prod_ref, bf16[4,64,64,128]{3,2,1,0:T(8,128)(2,1)} %get-tuple-element.52.back_ref), custom_call_target="tpu_custom_call" | custom-call | flops 33554432 | bytes 12582912 | tf_op jit(solution)/shard_map/product_grad/pallas_call | solution.py:227
  250.6 5.5 %all-to-all-start.3 = ((bf16[128,128,128]{2,1,0:T(8,128)(2,1)}), bf16[128,128,128]{2,1,0:T(8,128)(2,1)}, u32[]{:S(2)}, u32[]{:S(2)}) async-start(bf16[128,128,128]{2,1,0:T(8,128)(2,1)} %bitcast.148), calls=%async_computation.3 | async-start | bytes 8388608 | tf_op jit(solution)/shard_map/all_to_all | solution.py:489
  257.4 22.5 %gate_and_embed.1 = (bf16[64,64,128]{2,1,0:T(8,128)(2,1)}, f32[4,64,128]{2,1,0:T(8,128)}, f32[4,64,128]{2,1,0:T(8,128)}, f32[4,64,128]{2,1,0:T(8,128)}, f32[64,128]{1,0:T(8,128)}, /*index=5*/f32[64,128]{1,0:T(8,128)}) custom-call(bf16[4,64,64,128]{3,2,1,0:T(8,128)(2,1)} %bitcast.30.prod_ref, bf16[4,64,64,128]{3,2,1,0:T(8,128)(2,1)} %get-tuple-element.53.scaled_ref, ...), custom_call_target="tpu_custom_call" | custom-call | flops 8589934592 | bytes 12582912 | tf_op jit(solution)/shard_map/gate_and_embed/pallas_call | solution.py:307
  279.9 29.2 %all-to-all-done.3.grad_ref = bf16[128,128,128]{2,1,0:T(8,128)(2,1)} async-done(((bf16[128,128,128]{2,1,0:T(8,128)(2,1)}), bf16[128,128,128]{2,1,0:T(8,128)(2,1)}, u32[]{:S(2)}, u32[]{:S(2)}) %all-to-all-start.3) | async-done | bytes 4194336 | tf_op jit(solution)/shard_map/all_to_all | solution.py:489
  309.1 17.3 %factor_grads.1 = (bf16[128,32,128]{2,1,0:T(8,128)(2,1)}, bf16[128,32,128]{2,1,0:T(8,128)(2,1)}, f32[2,2,8,1024]{3,2,1,0:T(8,128)}, f32[2,2,1024,128]{3,2,1,0:T(8,128)}) custom-call(s32[1]{0:T(128)} %bitcast.33.core_ref, bf16[2,1024,1024]{2,1,0:T(8,128)(2,1)} %get-tuple-element.62.left_ref, bf16[2,1024,1024]{2,1,0:T(8,128)(2,1)} %get-tuple-element.63.right_ref, ...), custom_call_target="tpu_custom_call" | custom-call | tf_op jit(solution)/shard_map/factor_grads/pallas_call | solution.py:410
  332.3 2.5 add_convert_fusion
  334.8 3.8 all-to-all-start.4
  340.2 2.0 fusion.3.base_ref
  345.1 12.2 %all-to-all-done.4 = bf16[128,32,128]{2,1,0:T(8,128)(2,1)S(1)} async-done(((bf16[128,32,128]{2,1,0:T(8,128)(2,1)}), bf16[128,32,128]{2,1,0:T(8,128)(2,1)S(1)}, u32[]{:S(2)}, u32[]{:S(2)}) %all-to-all-start.4) | async-done | bytes 1048608 | tf_op jit(solution)/shard_map/all_to_all | solution.py:489
  358.3 5.8 %close_sums.1 = bf16[2,4,64,128]{3,2,1,0:T(8,128)(2,1)} custom-call(bf16[4,16,2,32,128]{4,3,2,1,0:T(8,128)(2,1)} %bitcast.150, f32[4,64,128]{2,1,0:T(8,128)} %get-tuple-element.80.mean_ref, f32[4,64,128]{2,1,0:T(8,128)} %get-tuple-element.43.inv_ref, bf16[4,64,64,128]{3,2,1,0:T(8,128)(2,1)} %get-tuple-element.53.scaled_ref, ...), custom_call_target="tpu_custom_call" | custom-call | tf_op jit(solution)/shard_map/close_sums/pallas_call | solution.py:466
  365.0 1.3 collective-permute-start.5
  366.4 1.6 collective-permute-start.7
  368.0 1.9 collective-permute-done.6
  369.9 1.6 collective-permute-done.7
  372.0 17.0 %all_to_all.30 = bf16[128,16,128]{2,1,0:T(8,128)(2,1)S(1)} all-to-all(bf16[128,16,128]{2,1,0:T(8,128)(2,1)S(1)} %bitcast.152), channel_id=1, replica_groups=mesh['row'=16,'col'=8] {'row','col'}, dimensions={0} | all-to-all | bytes 1048576 | tf_op jit(solution)/shard_map/all_to_all | solution.py:489
  (99 shorter events, 32.2 us)
Async XLA Ops:
  0.6 23.0 %copy-start.7 = (s32[4,8]{1,0:T(4,128)S(1)}, s32[4,8]{1,0:T(4,128)}, u32[]{:S(2)}) copy-start(s32[4,8]{1,0:T(4,128)} %param.18) | copy-start | bytes 388
  0.6 23.0 %copy-start.9 = (s32[4,8]{1,0:T(4,128)S(1)}, s32[4,8]{1,0:T(4,128)}, u32[]{:S(2)}) copy-start(s32[4,8]{1,0:T(4,128)} %param.19) | copy-start | bytes 388
  2.3 25.0 %all-to-all-start = ((bf16[128,16,128]{2,1,0:T(8,128)(2,1)}), bf16[128,16,128]{2,1,0:T(8,128)(2,1)S(1)}, u32[]{:S(2)}, u32[]{:S(2)}) async-start(bf16[128,16,128]{2,1,0:T(8,128)(2,1)} %bitcast.1), calls=%async_computation | async-start | bytes 1048576 | tf_op jit(solution)/shard_map/all_to_all | solution.py:489
  23.7 11.1 %copy-start.13 = (bf16[64]{0:T(256)(128)(2,1)S(1)}, bf16[64]{0:T(256)(128)(2,1)}, u32[]{:S(2)}) copy-start(bf16[64]{0:T(256)(128)(2,1)} %param.23) | copy-start | bytes 388
  24.0 0.5 copy-start.12
  27.6 2.9 collective-permute-start
  28.8 2.8 collective-permute-start.1
  29.0 3.8 collective-permute-start.2
  50.1 121.7 %all-to-all-start.1 = ((bf16[128,288,128]{2,1,0:T(8,128)(2,1)}), bf16[128,288,128]{2,1,0:T(8,128)(2,1)}, u32[]{:S(2)}, u32[]{:S(2)}) async-start(bf16[128,288,128]{2,1,0:T(8,128)(2,1)} %bitcast.149), calls=%async_computation.1 | async-start | bytes 18874368 | tf_op jit(solution)/shard_map/all_to_all | solution.py:489
  182.0 60.7 %all-to-all-start.2 = ((bf16[128,128,128]{2,1,0:T(8,128)(2,1)}), bf16[128,128,128]{2,1,0:T(8,128)(2,1)}, u32[]{:S(2)}, u32[]{:S(2)}) async-start(bf16[128,128,128]{2,1,0:T(8,128)(2,1)} %triangle_product.1), calls=%async_computation.2 | async-start | bytes 8388608 | tf_op jit(solution)/shard_map/all_to_all | solution.py:489
  191.2 3.5 collective-permute-start.3
  250.6 5.6 %copy-start.4 = (bf16[64,64]{1,0:T(8,128)(2,1)S(1)}, bf16[64,64]{1,0:T(8,128)(2,1)}, u32[]{:S(2)}) copy-start(bf16[64,64]{1,0:T(8,128)(2,1)} %param.24) | copy-start | bytes 24580
  250.6 5.7 %copy-start.5 = (bf16[64,64]{1,0:T(8,128)(2,1)S(1)}, bf16[64,64]{1,0:T(8,128)(2,1)}, u32[]{:S(2)}) copy-start(bf16[64,64]{1,0:T(8,128)(2,1)} %param.25) | copy-start | bytes 24580
  250.6 5.8 %copy-start.6 = (bf16[64,64]{1,0:T(8,128)(2,1)S(1)}, bf16[64,64]{1,0:T(8,128)(2,1)}, u32[]{:S(2)}) copy-start(bf16[64,64]{1,0:T(8,128)(2,1)} %param.26) | copy-start | bytes 24580
  250.6 6.1 %copy-start.2 = (bf16[4,256,128]{2,1,0:T(8,128)(2,1)S(1)}, bf16[4,256,128]{2,1,0:T(8,128)(2,1)}, u32[]{:S(2)}) copy-start(bf16[4,256,128]{2,1,0:T(8,128)(2,1)} %constant.169.clone) | copy-start | bytes 786436
  250.6 58.5 %all-to-all-start.3 = ((bf16[128,128,128]{2,1,0:T(8,128)(2,1)}), bf16[128,128,128]{2,1,0:T(8,128)(2,1)}, u32[]{:S(2)}, u32[]{:S(2)}) async-start(bf16[128,128,128]{2,1,0:T(8,128)(2,1)} %bitcast.148), calls=%async_computation.3 | async-start | bytes 8388608 | tf_op jit(solution)/shard_map/all_to_all | solution.py:489
  256.2 71.1 %copy-start.10 = (f32[64]{0:T(128)}, f32[64]{0:T(128)S(1)}, u32[]{:S(2)}) copy-start(f32[64]{0:T(128)S(1)} %convert_element_type.73) | copy-start | bytes 772
  326.3 13.9 %copy-start.3 = (f32[4,64,128]{2,1,0:T(8,128)S(1)}, f32[4,64,128]{2,1,0:T(8,128)}, u32[]{:S(2)}) copy-start(f32[4,64,128]{2,1,0:T(8,128)} %get-tuple-element.71) | copy-start | bytes 393220
  326.3 16.9 %copy-start.1 = (f32[2,2,1024,128]{3,2,1,0:T(8,128)S(1)}, f32[2,2,1024,128]{3,2,1,0:T(8,128)}, u32[]{:S(2)}) copy-start(f32[2,2,1024,128]{3,2,1,0:T(8,128)} %get-tuple-element.75) | copy-start | bytes 6291460
  326.4 5.9 %collective-permute-start.4 = (bf16[128,32,128]{2,1,0:T(8,128)(2,1)}, bf16[128,32,128]{2,1,0:T(8,128)(2,1)S(1)}, u32[]{:S(2)}, u32[]{:S(2)}) collective-permute-start(bf16[128,32,128]{2,1,0:T(8,128)(2,1)} %get-tuple-element.69), channel_id=1, source_target_pairs={{0,1},{1,0},{2,3},{3,2},{4,5},{5,4},{6,7},{7,6},{8,9},{9,8},{10,11... | collective-permute-start | bytes 3145736 | tf_op jit(solution)/shard_map/ppermute | solution.py:481
  327.4 11.2 %copy-start.11 = (f32[64]{0:T(128)S(1)}, f32[64]{0:T(128)}, u32[]{:S(2)}) copy-start(f32[64]{0:T(128)} %copy-done.10) | copy-start | bytes 772
  330.9 13.0 %copy-start.8 = (f32[2,4,128]{2,1,0:T(4,128)}, f32[2,4,128]{2,1,0:T(4,128)S(1)}, u32[]{:S(2)}) copy-start(f32[2,4,128]{2,1,0:T(4,128)S(1)} %pad_maximum_fusion.5) | copy-start | bytes 12292
  334.8 22.5 %all-to-all-start.4 = ((bf16[128,32,128]{2,1,0:T(8,128)(2,1)}), bf16[128,32,128]{2,1,0:T(8,128)(2,1)S(1)}, u32[]{:S(2)}, u32[]{:S(2)}) async-start(bf16[128,32,128]{2,1,0:T(8,128)(2,1)} %add_convert_fusion), calls=%async_computation.4 | async-start | bytes 2097152 | tf_op jit(solution)/shard_map/all_to_all | solution.py:489
  357.3 1.0 copy-start
  365.0 3.1 collective-permute-start.5
  366.3 3.6 collective-permute-start.6
  366.4 5.1 %collective-permute-start.7 = (bf16[16,16,128]{2,1,0:T(8,128)(2,1)S(1)}, bf16[16,16,128]{2,1,0:T(8,128)(2,1)S(1)}, u32[]{:S(2)}, u32[]{:S(2)}) collective-permute-start(bf16[16,16,128]{2,1,0:T(8,128)(2,1)S(1)} %get-tuple-element.101), channel_id=1, source_target_pairs={{0,3},{1,2},{2,1},{3,0},{4,7},{5,6},{6,5},{7,4},{8,11},{9,10},{10,... | collective-permute-start | bytes 196616 | tf_op jit(solution)/shard_map/ppermute | solution.py:481

commit v4 on v3

--- a/solution.py
+++ b/solution.py
@@ -11,7 +11,6 @@
 F32 = jnp.float32
 BF = jnp.bfloat16
 AXES = ("row", "col")
-VMEM = 60 * 2**20
 
 C = 64
 T = 4
@@ -22,8 +21,8 @@
 ROWS = 288
 
 
-def params():
-    return pltpu.CompilerParams(vmem_limit_bytes=VMEM)
+def params(mib):
+    return pltpu.CompilerParams(vmem_limit_bytes=mib * 2**20)
 
 
 def stack_rows(top, bottom):
@@ -78,28 +77,35 @@
 
 
 def norm_kernel(
-    pair_ref, left_ref, right_ref, lanes_ref, gain_ref, kl_ref, kr_ref, pay_ref, inv_ref, right
+    pair_ref, left_ref, right_ref, lanes_ref, gain_ref, kl_ref, kr_ref, pay_ref, inv_ref,
+    right, terms, wide,
 ):
     left = spread_terms(left_ref, right_ref, right)
     for g in range(4):
+        terms[g] = jnp.dot(left, lanes_ref[g], preferred_element_type=F32)
+    for g in range(4):
         scaleds, invs = [], []
-        for pair in make_pairs(pair_ref, left, lanes_ref, right, g):
+        left_terms = unstack_rows(terms[g])
+        raw = halves(pair_ref[0, :, g * 16 : g * 16 + 16, :].astype(F32))
+        for part in range(2):
+            pair = raw[part] + left_terms[part] + right[...]
             shifted = pair - mean_channels(pair)
             inverse = lax.rsqrt(mean_channels(shifted * shifted) + EPS)
             scaleds.append(shifted * inverse * gain_ref[...])
             invs.append(inverse[0])
         both = jnp.concatenate(invs, axis=0)
         inv_ref[0, g * 16 : g * 16 + 16, :] = both
-        wide = stack_rows(*scaleds).astype(BF)
-        for k, weight in enumerate((kl_ref, kr_ref)):
-            out = jnp.dot(weight[...], wide, preferred_element_type=F32)
-            out = join_rows(*unstack_rows(out)).astype(BF).reshape(C // 2, 2, 16, W)
+        wide[:, g * 256 : g * 256 + 256] = stack_rows(*scaleds).astype(BF)
+        first = 256 + (g % 2) * 16
+        for q in range(g // 2, C // 2, 2):
+            pay_ref[0, q, first : first + 16, :] = both.astype(BF)
+    for k, weight in enumerate((kl_ref, kr_ref)):
+        outs = jnp.dot(weight[...], wide[...], preferred_element_type=F32)
+        for g in range(4):
+            out = join_rows(*unstack_rows(outs[:, g * 256 : g * 256 + 256])).astype(BF).reshape(C // 2, 2, 16, W)
             for s in range(2):
                 first = k * 128 + s * 64 + g * 16
                 pay_ref[0, :, first : first + 16, :] = out[:, s]
-        first = 256 + (g % 2) * 16
-        for q in range(g // 2, C // 2, 2):
-            pay_ref[0, q, first : first + 16, :] = both.astype(BF)
 
 
 TERM_SPECS = [each_spec(C, H, W), each_spec(C, W), each_spec(C, W), whole_spec(4, W, 2 * W), whole_spec(C, 8, W)]
@@ -112,11 +118,15 @@
         in_specs=[*TERM_SPECS, whole_spec(K8, K8), whole_spec(K8, K8)],
         out_specs=[each_spec(C // 2, ROWS, W), each_spec(H, W)],
         out_shape=[
-            jax.ShapeDtypeStruct((T, C // 2, ROWS, W), BF),
+            pltpu.HBM((T, C // 2, ROWS, W), BF),
             jax.ShapeDtypeStruct((T, H, W), F32),
         ],
-        scratch_shapes=[pltpu.VMEM((C, 8, W), F32)],
-        compiler_params=params(),
+        scratch_shapes=[
+            pltpu.VMEM((C, 8, W), F32),
+            pltpu.VMEM((4, K8, 2 * W), F32),
+            pltpu.VMEM((K8, N), BF),
+        ],
+        compiler_params=params(24),
         name="pair_norm",
     )(pair, left, right, lanes, gain, kl, kr)
 
@@ -147,9 +157,9 @@
         grid=(2,),
         in_specs=[spec(0), spec(2)],
         out_specs=pl.BlockSpec((128, H, W), lambda s: (0, s, 0)),
-        out_shape=jax.ShapeDtypeStruct((128, 2 * H, W), BF),
+        out_shape=pltpu.HBM((128, 2 * H, W), BF),
         scratch_shapes=[pltpu.VMEM((N, N), BF), pltpu.VMEM((N, N), BF)],
-        compiler_params=params(),
+        compiler_params=params(28),
         name="triangle_product",
     )(factors, factors)
 
@@ -203,7 +213,7 @@
             jax.ShapeDtypeStruct((C, H, W), F32),
         ],
         scratch_shapes=[pltpu.VMEM((C, 8, W), F32)],
-        compiler_params=params(),
+        compiler_params=params(24),
         cost_estimate=pl.CostEstimate(flops=4 * 2**31, bytes_accessed=16 * 2**20, transcendentals=2**21),
         name="back_project",
     )(pair, left, right, lanes, gain, inv, grad, kg, kb)
@@ -229,8 +239,8 @@
         grid=(T,),
         in_specs=[each_spec(C, H, W), each_spec(C, H, W)],
         out_specs=each_spec(C, H, W),
-        out_shape=jax.ShapeDtypeStruct((T, C, H, W), BF),
-        compiler_params=params(),
+        out_shape=pltpu.HBM((T, C, H, W), BF),
+        compiler_params=params(16),
         cost_estimate=pl.CostEstimate(flops=2**25, bytes_accessed=12 * 2**20, transcendentals=0),
         name="product_grad",
     )(prod, back)
@@ -324,7 +334,7 @@
             jax.ShapeDtypeStruct((C, W), F32),
         ],
         scratch_shapes=[pltpu.VMEM((C, H, W), F32)],
-        compiler_params=params(),
+        compiler_params=params(24),
         cost_estimate=pl.CostEstimate(flops=4 * 2**31, bytes_accessed=12 * 2**20, transcendentals=2**21),
         name="gate_and_embed",
     )(prod, scaled, grad, pair_sum, inv, kg, ko, pick)
@@ -349,7 +359,7 @@
         in_specs=[spec(0), spec(2), pl.BlockSpec((128, H, W), lambda s: (0, 0, 0))],
         out_specs=[out, out, pl.BlockSpec((N, N), lambda s: (0, 0))],
         out_shape=[jax.ShapeDtypeStruct((2, N, N), BF)] * 2 + [jax.ShapeDtypeStruct((N, N), BF)],
-        compiler_params=params(),
+        compiler_params=params(28),
         cost_estimate=pl.CostEstimate(flops=2**20, bytes_accessed=20 * 2**20, transcendentals=0),
         name="to_matrices",
     )(factors, factors, inv)
@@ -371,14 +381,14 @@
     def finish(value, rows, factor, kind):
         mean[rows, :] += value * factor[rows, :].astype(F32)
         term = value * inv_ref[rows, :].astype(F32)
-        part = jnp.sum(term.reshape(64, 8, N), axis=0)
+        part = jnp.sum(term.reshape(128, 8, N), axis=0)
         lanes = term[:, :W]
         for c in range(1, 8):
             lanes = lanes + term[:, c * W : (c + 1) * W]
         rows_ref[0, kind, rows, :] = lanes
         return part
 
-    blocks = [slice(b * 512, b * 512 + 512) for b in range(2)]
+    blocks = [slice(0, N)]
     total = None
     for rows in blocks:
         value = jnp.dot(grad[rows, :], right[...], preferred_element_type=F32)
@@ -430,7 +440,7 @@
             jax.ShapeDtypeStruct((2, 2, N, W), F32),
         ],
         scratch_shapes=[pltpu.VMEM((N, N), BF), pltpu.VMEM((N, N), F32)],
-        compiler_params=params(),
+        compiler_params=params(44),
         name="factor_grads",
     )(core.reshape(1), left, right, grad, inv)
 
@@ -472,7 +482,7 @@
         ],
         out_specs=both(C, W),
         out_shape=jax.ShapeDtypeStruct((2, T, C, W), BF),
-        compiler_params=params(),
+        compiler_params=params(16),
         name="close_sums",
     )(recv, mean, inv, scaled, pick, weights, valid, base)
 

time: 391 us -> 393 us (level)
  local copies, waits for them, and re-layouts: 16.7 us -> 46.7 us
  Pallas kernels: 102 us -> 83 us
  waiting for transfers between devices: 183 us -> 172 us
    unnamed x40 -> x116, local copies, waits for them, and re-layouts: 7.93 us -> 36.3 us
    all_to_all x5, waiting for transfers between devices: 175 us -> 163 us  [exchange(): return lax.all_to_all(value, AXES, split_axis=0, concat_axis=0, tiled=True)]
    pallas_call x1, Pallas kernels: 14.5 us -> 9.53 us  [run_norm(): pl.pallas_call(norm_kernel, grid=(T,), in_specs=[*TERM_SPECS, whole_spec(...]
  transfers between devices with their start and end apart: 13 -> 13, of which waited for: 10 -> 9; matrix products, arithmetic and copies ran while one was open for 7% -> 8% of each run, Pallas kernels for 12% -> 10%
where the time goes in v4:
time: 393 us; the launch traced here: 391 us
  waiting for transfers between devices  172 us (44%)
  Pallas kernels  83 us (21%)
  local copies, waits for them, and re-layouts  46.7 us (12%)
  starting transfers between devices  46.3 us (12%)
  blocking collectives  17 us (4%)
  other arithmetic  13.7 us (3%)
  matrix products  10.9 us (3%)
    all_to_all x5, waiting for transfers between devices, exchange(): return lax.all_to_all(value, AXES, split_axis=0, concat_axis=0, tiled=True)  163 us
    all_to_all x5, starting transfers between devices, exchange(): return lax.all_to_all(value, AXES, split_axis=0, concat_axis=0, tiled=True)  38.3 us
    unnamed x116, local copies, waits for them, and re-layouts  36.3 us
    pallas_call x1, Pallas kernels, run_gate(): pl.pallas_call(gate_kernel, grid=(T,), in_specs=[each_spec(C, H, W), each...  20.4 us
    all_to_all x1, blocking collectives, exchange(): return lax.all_to_all(value, AXES, split_axis=0, concat_axis=0, tiled=True)  17 us
    pallas_call x1, Pallas kernels, run_factor(): pl.pallas_call(factor_kernel, grid=(2,), in_specs=[pl.BlockSpec(memory_sp...  15.4 us
    pallas_call x1, Pallas kernels, run_back(): pl.pallas_call(back_kernel, grid=(T,), in_specs=[*TERM_SPECS, each_spec(H...  12.6 us
    pallas_call x1, Pallas kernels, run_product(): pl.pallas_call(product_kernel, grid=(2,), in_specs=[spec(0), spec(2)], ou...  10.2 us
  transfers between devices with their start and end apart: 13, of which 9 were waited for; matrix products, arithmetic and copies ran while one was open for 8% of the time, Pallas kernels for 10%

profile of v4, /device:TPU:1, one launch (start us, length us, event | category | flops | bytes accessed | tf_op | source)
XLA Modules:
  0.0 390.6 jit_solution(13202767219185184790)
XLA Ops:
  2.3 11.5 %all-to-all-start = ((bf16[128,16,128]{2,1,0:T(8,128)(2,1)}), bf16[128,16,128]{2,1,0:T(8,128)(2,1)S(1)}, u32[]{:S(2)}, u32[]{:S(2)}) async-start(bf16[128,16,128]{2,1,0:T(8,128)(2,1)} %bitcast.1), calls=%async_computation | async-start | bytes 1048576 | tf_op jit(solution)/shard_map/all_to_all | solution.py:499
  19.9 3.4 select_convert_fusion
  36.7 2.2 copy-done.4
  38.9 9.5 %pair_norm.1 = (bf16[4,32,288,128]{3,2,1,0:T(8,128)(2,1)}, f32[4,64,128]{2,1,0:T(8,128)S(1)}) custom-call(bf16[4,64,64,128]{3,2,1,0:T(8,128)(2,1)S(1)} %copy-done.4, f32[4,64,128]{2,1,0:T(8,128)S(1)} %pad_maximum_fusion.2.left_ref, f32[4,64,128]{2,1,0:T(8,128)S(1)} %fusion.4.right_ref, bf16[4,128,256]{2,1,0:T(8,128)(2,1)S(1)} %copy-done.12, ...), custom_call_target="tpu_custom_call" | custom-call | tf_op jit(solution)/shard_map/pair_norm/pallas_call | solution.py:115
  48.4 9.8 %all-to-all-start.1 = ((bf16[128,288,128]{2,1,0:T(8,128)(2,1)}), bf16[128,288,128]{2,1,0:T(8,128)(2,1)}, u32[]{:S(2)}, u32[]{:S(2)}) async-start(bf16[128,288,128]{2,1,0:T(8,128)(2,1)} %bitcast.156), calls=%async_computation.1 | async-start | bytes 18874368 | tf_op jit(solution)/shard_map/all_to_all | solution.py:499
  58.3 2.2 copy-done.5
  60.5 12.6 %back_project.1 = (bf16[4,64,64,128]{3,2,1,0:T(8,128)(2,1)S(1)}, bf16[4,64,64,128]{3,2,1,0:T(8,128)(2,1)S(1)}, f32[64,64,128]{2,1,0:T(8,128)S(1)}) custom-call(bf16[4,64,64,128]{3,2,1,0:T(8,128)(2,1)S(1)} %copy-done.5, f32[4,64,128]{2,1,0:T(8,128)S(1)} %pad_maximum_fusion.2.left_ref, f32[4,64,128]{2,1,0:T(8,128)S(1)} %fusion.4.right_ref, ...), custom_call_target="tpu_custom_call" | custom-call | flops 8589934592 | bytes 16777216 | tf_op jit(solution)/shard_map/back_project/pallas_call | solution.py:203
  73.1 2.1 copy-done.2
  75.2 2.0 copy-done.6
  78.5 91.9 %all-to-all-done.1.left_ref.right_ref = bf16[128,288,128]{2,1,0:T(8,128)(2,1)} async-done(((bf16[128,288,128]{2,1,0:T(8,128)(2,1)}), bf16[128,288,128]{2,1,0:T(8,128)(2,1)}, u32[]{:S(2)}, u32[]{:S(2)}) %all-to-all-start.1) | async-done | bytes 9437216 | tf_op jit(solution)/shard_map/all_to_all | solution.py:499
  170.5 10.2 %triangle_product.1 = bf16[128,128,128]{2,1,0:T(8,128)(2,1)} custom-call(bf16[128,288,128]{2,1,0:T(8,128)(2,1)} %all-to-all-done.1.left_ref.right_ref, bf16[128,288,128]{2,1,0:T(8,128)(2,1)} %all-to-all-done.1.left_ref.right_ref), custom_call_target="tpu_custom_call" | custom-call | tf_op jit(solution)/shard_map/triangle_product/pallas_call | solution.py:155
  180.6 7.9 %all-to-all-start.2 = ((bf16[128,128,128]{2,1,0:T(8,128)(2,1)}), bf16[128,128,128]{2,1,0:T(8,128)(2,1)}, u32[]{:S(2)}, u32[]{:S(2)}) async-start(bf16[128,128,128]{2,1,0:T(8,128)(2,1)} %triangle_product.1), calls=%async_computation.2 | async-start | bytes 8388608 | tf_op jit(solution)/shard_map/all_to_all | solution.py:499
  188.5 2.3 slice.67
  192.0 2.6 collective-permute-done.3
  196.6 4.5 %to_matrices.1 = (bf16[2,1024,1024]{2,1,0:T(8,128)(2,1)S(1)}, bf16[2,1024,1024]{2,1,0:T(8,128)(2,1)S(1)}, bf16[1024,1024]{1,0:T(8,128)(2,1)S(1)}) custom-call(bf16[128,288,128]{2,1,0:T(8,128)(2,1)} %all-to-all-done.1.left_ref.right_ref, bf16[128,288,128]{2,1,0:T(8,128)(2,1)} %all-to-all-done.1.left_ref.right_ref, ...), custom_call_target="tpu_custom_call" | custom-call | flops 1048576 | bytes 20971520 | tf_op jit(solution)/shard_map/to_matrices/pallas_call | solution.py:356
  201.0 2.0 copy-done
  203.0 2.0 copy-done.1
  206.4 35.0 %all-to-all-done.2 = bf16[128,128,128]{2,1,0:T(8,128)(2,1)} async-done(((bf16[128,128,128]{2,1,0:T(8,128)(2,1)}), bf16[128,128,128]{2,1,0:T(8,128)(2,1)}, u32[]{:S(2)}, u32[]{:S(2)}) %all-to-all-start.2) | async-done | bytes 4194336 | tf_op jit(solution)/shard_map/all_to_all | solution.py:499
  241.3 2.2 copy-done.3
  243.5 7.2 %product_grad.1 = bf16[4,64,64,128]{3,2,1,0:T(8,128)(2,1)} custom-call(bf16[4,64,64,128]{3,2,1,0:T(8,128)(2,1)} %bitcast.30.prod_ref, bf16[4,64,64,128]{3,2,1,0:T(8,128)(2,1)S(1)} %copy-done.3), custom_call_target="tpu_custom_call" | custom-call | flops 33554432 | bytes 12582912 | tf_op jit(solution)/shard_map/product_grad/pallas_call | solution.py:237
  250.7 5.5 %all-to-all-start.3 = ((bf16[128,128,128]{2,1,0:T(8,128)(2,1)}), bf16[128,128,128]{2,1,0:T(8,128)(2,1)}, u32[]{:S(2)}, u32[]{:S(2)}) async-start(bf16[128,128,128]{2,1,0:T(8,128)(2,1)} %bitcast.155), calls=%async_computation.3 | async-start | bytes 8388608 | tf_op jit(solution)/shard_map/all_to_all | solution.py:499
  258.0 2.2 copy-done.7
  261.8 20.4 %gate_and_embed.1 = (bf16[64,64,128]{2,1,0:T(8,128)(2,1)}, f32[4,64,128]{2,1,0:T(8,128)S(1)}, f32[4,64,128]{2,1,0:T(8,128)S(1)}, f32[4,64,128]{2,1,0:T(8,128)S(1...) custom-call(bf16[4,64,64,128]{3,2,1,0:T(8,128)(2,1)} %bitcast.30.prod_ref, bf16[4,64,64,128]{3,2,1,0:T(8,128)(2,1)S(1)} %copy-done.7, ...), custom_call_target="tpu_custom_call" | custom-call | flops 8589934592 | bytes 12582912 | tf_op jit(solution)/shard_map/gate_and_embed/pallas_call | solution.py:317
  285.4 23.8 %all-to-all-done.3.grad_ref = bf16[128,128,128]{2,1,0:T(8,128)(2,1)} async-done(((bf16[128,128,128]{2,1,0:T(8,128)(2,1)}), bf16[128,128,128]{2,1,0:T(8,128)(2,1)}, u32[]{:S(2)}, u32[]{:S(2)}) %all-to-all-start.3) | async-done | bytes 4194336 | tf_op jit(solution)/shard_map/all_to_all | solution.py:499
  310.9 15.4 %factor_grads.1 = (bf16[128,32,128]{2,1,0:T(8,128)(2,1)S(1)}, bf16[128,32,128]{2,1,0:T(8,128)(2,1)}, f32[2,2,8,1024]{3,2,1,0:T(8,128)S(1)}, f32[2,2,1024,128]{3,2,1,0:T(8,128)S(1)}) custom-call(s32[1]{0:T(128)} %bitcast.33.core_ref, bf16[2,1024,1024]{2,1,0:T(8,128)(2,1)} %copy-done, bf16[2,1024,1024]{2,1,0:T(8,128)(2,1)} %copy-done.1, ...), custom_call_target="tpu_custom_call" | custom-call | tf_op jit(solution)/shard_map/factor_grads/pallas_call | solution.py:420
  332.6 2.5 add_convert_fusion
  335.1 3.6 all-to-all-start.4
  340.5 2.1 fusion.3.base_ref
  345.4 12.2 %all-to-all-done.4 = bf16[128,32,128]{2,1,0:T(8,128)(2,1)S(1)} async-done(((bf16[128,32,128]{2,1,0:T(8,128)(2,1)}), bf16[128,32,128]{2,1,0:T(8,128)(2,1)S(1)}, u32[]{:S(2)}, u32[]{:S(2)}) %all-to-all-start.4) | async-done | bytes 1048608 | tf_op jit(solution)/shard_map/all_to_all | solution.py:499
  357.6 2.2 copy-done.8
  362.6 3.2 close_sums.1
  372.8 17.0 %all_to_all.30 = bf16[128,16,128]{2,1,0:T(8,128)(2,1)S(1)} all-to-all(bf16[128,16,128]{2,1,0:T(8,128)(2,1)S(1)} %bitcast.158), channel_id=1, replica_groups=mesh['row'=16,'col'=8] {'row','col'}, dimensions={0} | all-to-all | bytes 1048576 | tf_op jit(solution)/shard_map/all_to_all | solution.py:499
  (175 shorter events, 55.9 us)
Async XLA Ops:
  0.6 22.7 %copy-start.37 = (s32[4,8]{1,0:T(4,128)S(1)}, s32[4,8]{1,0:T(4,128)}, u32[]{:S(2)}) copy-start(s32[4,8]{1,0:T(4,128)} %param.18) | copy-start | bytes 388
  0.6 22.7 %copy-start.39 = (s32[4,8]{1,0:T(4,128)S(1)}, s32[4,8]{1,0:T(4,128)}, u32[]{:S(2)}) copy-start(s32[4,8]{1,0:T(4,128)} %param.19) | copy-start | bytes 388
  2.3 25.3 %all-to-all-start = ((bf16[128,16,128]{2,1,0:T(8,128)(2,1)}), bf16[128,16,128]{2,1,0:T(8,128)(2,1)S(1)}, u32[]{:S(2)}, u32[]{:S(2)}) async-start(bf16[128,16,128]{2,1,0:T(8,128)(2,1)} %bitcast.1), calls=%async_computation | async-start | bytes 1048576 | tf_op jit(solution)/shard_map/all_to_all | solution.py:499
  15.9 8.4 %copy-start.48 = (pred[128]{0:T(512)(128)(4,1)}, pred[128]{0:T(512)(128)(4,1)S(1)}, u32[]{:S(2)}) copy-start(pred[128]{0:T(512)(128)(4,1)S(1)} %fusion.56) | copy-start | bytes 388
  23.3 13.4 %copy-start.12 = (bf16[4,128,256]{2,1,0:T(8,128)(2,1)S(1)}, bf16[4,128,256]{2,1,0:T(8,128)(2,1)}, u32[]{:S(2)}) copy-start(bf16[4,128,256]{2,1,0:T(8,128)(2,1)} %constant.168.clone.lanes_ref) | copy-start | bytes 786436
  28.5 3.0 collective-permute-start
  29.7 2.8 collective-permute-start.1
  30.4 3.5 collective-permute-start.2
  48.4 209.6 %copy-start.13 = (f32[4,64,128]{2,1,0:T(8,128)}, f32[4,64,128]{2,1,0:T(8,128)S(1)}, u32[]{:S(2)}) copy-start(f32[4,64,128]{2,1,0:T(8,128)S(1)} %get-tuple-element.43.inv_ref) | copy-start | bytes 393220
  48.4 9.9 %copy-start.22 = (bf16[64,64,128]{2,1,0:T(8,128)(2,1)S(1)}, bf16[64,64,128]{2,1,0:T(8,128)(2,1)}, u32[]{:S(2)}) copy-start(bf16[64,64,128]{2,1,0:T(8,128)(2,1)} %grad_ref.3) | copy-start | bytes 3145732
  48.4 122.0 %all-to-all-start.1 = ((bf16[128,288,128]{2,1,0:T(8,128)(2,1)}), bf16[128,288,128]{2,1,0:T(8,128)(2,1)}, u32[]{:S(2)}, u32[]{:S(2)}) async-start(bf16[128,288,128]{2,1,0:T(8,128)(2,1)} %bitcast.156), calls=%async_computation.1 | async-start | bytes 18874368 | tf_op jit(solution)/shard_map/all_to_all | solution.py:499
  180.6 60.7 %all-to-all-start.2 = ((bf16[128,128,128]{2,1,0:T(8,128)(2,1)}), bf16[128,128,128]{2,1,0:T(8,128)(2,1)}, u32[]{:S(2)}, u32[]{:S(2)}) async-start(bf16[128,128,128]{2,1,0:T(8,128)(2,1)} %triangle_product.1), calls=%async_computation.2 | async-start | bytes 8388608 | tf_op jit(solution)/shard_map/all_to_all | solution.py:499
  190.8 3.8 collective-permute-start.3
  250.7 5.7 %copy-start.35 = (bf16[64,64]{1,0:T(8,128)(2,1)S(1)}, bf16[64,64]{1,0:T(8,128)(2,1)}, u32[]{:S(2)}) copy-start(bf16[64,64]{1,0:T(8,128)(2,1)} %param.25) | copy-start | bytes 24580
  250.7 5.8 %copy-start.36 = (bf16[64,64]{1,0:T(8,128)(2,1)S(1)}, bf16[64,64]{1,0:T(8,128)(2,1)}, u32[]{:S(2)}) copy-start(bf16[64,64]{1,0:T(8,128)(2,1)} %param.26) | copy-start | bytes 24580
  250.7 7.2 %copy-start.28 = (bf16[4,256,128]{2,1,0:T(8,128)(2,1)S(1)}, bf16[4,256,128]{2,1,0:T(8,128)(2,1)}, u32[]{:S(2)}) copy-start(bf16[4,256,128]{2,1,0:T(8,128)(2,1)} %constant.169.clone) | copy-start | bytes 786436
  250.7 7.2 %copy-start.49 = (pred[128]{0:T(512)(128)(4,1)S(1)}, pred[128]{0:T(512)(128)(4,1)}, u32[]{:S(2)}) copy-start(pred[128]{0:T(512)(128)(4,1)} %copy-done.48) | copy-start | bytes 388
  250.7 58.5 %all-to-all-start.3 = ((bf16[128,128,128]{2,1,0:T(8,128)(2,1)}), bf16[128,128,128]{2,1,0:T(8,128)(2,1)}, u32[]{:S(2)}, u32[]{:S(2)}) async-start(bf16[128,128,128]{2,1,0:T(8,128)(2,1)} %bitcast.155), calls=%async_computation.3 | async-start | bytes 8388608 | tf_op jit(solution)/shard_map/all_to_all | solution.py:499
  310.8 16.3 %copy-start.30 = (bf16[64,64]{0,1:T(8,128)(2,1)S(1)}, bf16[64,64]{0,1:T(8,128)(2,1)}, u32[]{:S(2)}) copy-start(bf16[64,64]{0,1:T(8,128)(2,1)} %copy-done.29) | copy-start | bytes 24580
  310.8 16.3 %copy-start.32 = (bf16[64,64]{0,1:T(8,128)(2,1)S(1)}, bf16[64,64]{0,1:T(8,128)(2,1)}, u32[]{:S(2)}) copy-start(bf16[64,64]{0,1:T(8,128)(2,1)} %copy-done.31) | copy-start | bytes 24580
  310.8 16.3 %copy-start.41 = (f32[64]{0:T(128)S(1)}, f32[64]{0:T(128)}, u32[]{:S(2)}) copy-start(f32[64]{0:T(128)} %copy-done.40) | copy-start | bytes 772
  310.8 16.3 %copy-start.46 = (f32[64]{0:T(128)S(1)}, f32[64]{0:T(128)}, u32[]{:S(2)}) copy-start(f32[64]{0:T(128)} %get-tuple-element.116) | copy-start | bytes 772
  310.8 16.3 %copy-start.47 = (f32[64]{0:T(128)S(1)}, f32[64]{0:T(128)}, u32[]{:S(2)}) copy-start(f32[64]{0:T(128)} %get-tuple-element.117) | copy-start | bytes 772
  310.8 16.3 %copy-start.51 = (f32[64]{0:T(128)S(1)}, f32[64]{0:T(128)}, u32[]{:S(2)}) copy-start(f32[64]{0:T(128)} %broadcast_multiply_fusion.2) | copy-start | bytes 772
  310.9 16.4 %copy-start.26 = (bf16[2,2,2,16,64]{4,3,2,1,0:T(8,128)(2,1)S(1)}, bf16[2,2,2,16,64]{4,3,2,1,0:T(8,128)(2,1)}, u32[]{:S(2)}) copy-start(bf16[2,2,2,16,64]{4,3,2,1,0:T(8,128)(2,1)} %copy-done.25) | copy-start | bytes 49156
  326.2 8.9 %copy-start.19 = (f32[2,2,8,1024]{3,2,1,0:T(8,128)}, f32[2,2,8,1024]{3,2,1,0:T(8,128)S(1)}, u32[]{:S(2)}) copy-start(f32[2,2,8,1024]{3,2,1,0:T(8,128)S(1)} %get-tuple-element.76) | copy-start | bytes 393220
  326.3 6.4 %collective-permute-start.4 = (bf16[128,32,128]{2,1,0:T(8,128)(2,1)}, bf16[128,32,128]{2,1,0:T(8,128)(2,1)}, u32[]{:S(2)}, u32[]{:S(2)}) collective-permute-start(bf16[128,32,128]{2,1,0:T(8,128)(2,1)} %get-tuple-element.69), channel_id=1, source_target_pairs={{0,1},{1,0},{2,3},{3,2},{4,5},{5,4},{6,7},{7,6},{8,9},{9,8},{10,11... | collective-permute-start | bytes 3145736 | tf_op jit(solution)/shard_map/ppermute | solution.py:491
  335.1 22.5 %all-to-all-start.4 = ((bf16[128,32,128]{2,1,0:T(8,128)(2,1)}), bf16[128,32,128]{2,1,0:T(8,128)(2,1)S(1)}, u32[]{:S(2)}, u32[]{:S(2)}) async-start(bf16[128,32,128]{2,1,0:T(8,128)(2,1)} %add_convert_fusion), calls=%async_computation.4 | async-start | bytes 2097152 | tf_op jit(solution)/shard_map/all_to_all | solution.py:499
  344.2 28.2 %copy-start.33 = (bf16[128,64]{1,0:T(8,128)(2,1)S(1)}, bf16[128,64]{1,0:T(8,128)(2,1)}, u32[]{:S(2)}) copy-start(bf16[128,64]{1,0:T(8,128)(2,1)} %fusion.27) | copy-start | bytes 49156
  365.8 3.1 collective-permute-start.5
  367.1 3.6 collective-permute-start.6
  367.3 5.1 %collective-permute-start.7 = (bf16[16,16,128]{2,1,0:T(8,128)(2,1)S(1)}, bf16[16,16,128]{2,1,0:T(8,128)(2,1)S(1)}, u32[]{:S(2)}, u32[]{:S(2)}) collective-permute-start(bf16[16,16,128]{2,1,0:T(8,128)(2,1)S(1)} %get-tuple-element.101), channel_id=1, source_target_pairs={{0,3},{1,2},{2,1},{3,0},{4,7},{5,6},{6,5},{7,4},{8,11},{9,10},{10,... | collective-permute-start | bytes 196616 | tf_op jit(solution)/shard_map/ppermute | solution.py:491
  (33 other events, 49.3 us)

commit v5 on v4

--- a/solution.py
+++ b/solution.py
@@ -21,8 +21,8 @@
 ROWS = 288
 
 
-def params(mib):
-    return pltpu.CompilerParams(vmem_limit_bytes=mib * 2**20)
+def params():
+    return pltpu.CompilerParams(vmem_limit_bytes=60 * 2**20)
 
 
 def stack_rows(top, bottom):
@@ -65,9 +65,8 @@
         right[c] = jnp.broadcast_to(right_ref[0, c : c + 1, :], (8, W))
         rows.append(jnp.broadcast_to(left_ref[0, c : c + 1, :], (8, W)) * mask)
     value = jnp.concatenate(rows, axis=0)
-    rest = value - value.astype(BF).astype(F32)
-    lane = lax.broadcasted_iota(jnp.int32, (K8, W), 1)
-    return jnp.where(lane < H, value, rest).astype(BF)
+    high = value.astype(BF)
+    return jnp.concatenate([high, (value - high.astype(F32)).astype(BF)], axis=1)
 
 
 def make_pairs(pair_ref, left, lanes_ref, right, g):
@@ -108,7 +107,13 @@
                 pay_ref[0, :, first : first + 16, :] = out[:, s]
 
 
-TERM_SPECS = [each_spec(C, H, W), each_spec(C, W), each_spec(C, W), whole_spec(4, W, 2 * W), whole_spec(C, 8, W)]
+TERM_SPECS = [
+    each_spec(C, H, W),
+    each_spec(C, W),
+    each_spec(C, W),
+    whole_spec(4, 2 * W, 2 * W),
+    whole_spec(C, 8, W),
+]
 
 
 def run_norm(pair, left, right, lanes, gain, kl, kr):
@@ -126,7 +131,7 @@
             pltpu.VMEM((4, K8, 2 * W), F32),
             pltpu.VMEM((K8, N), BF),
         ],
-        compiler_params=params(24),
+        compiler_params=params(),
         name="pair_norm",
     )(pair, left, right, lanes, gain, kl, kr)
 
@@ -138,12 +143,16 @@
             full_ref[pl.ds(r * H, H), c * W : (c + 1) * W] = blocks_ref[r * 8 + c]
 
 
-def product_kernel(left_ref, right_ref, out_ref, left, right):
-    spread(left_ref, left)
-    spread(right_ref, right)
-
+def matrix(blocks_ref):
+    rows = [
+        jnp.concatenate([blocks_ref[r * 8 + c] for c in range(8)], axis=1) for r in range(16)
+    ]
+    return jnp.concatenate(rows, axis=0)
+
+
+def product_kernel(left_ref, right_ref, out_ref):
     out = lax.dot_general(
-        left[...], right[...], (((1,), (1,)), ((), ())), preferred_element_type=F32
+        matrix(left_ref), matrix(right_ref), (((1,), (1,)), ((), ())), preferred_element_type=F32
     ).astype(BF)
     for r in range(16):
         for c in range(8):
@@ -158,8 +167,7 @@
         in_specs=[spec(0), spec(2)],
         out_specs=pl.BlockSpec((128, H, W), lambda s: (0, s, 0)),
         out_shape=pltpu.HBM((128, 2 * H, W), BF),
-        scratch_shapes=[pltpu.VMEM((N, N), BF), pltpu.VMEM((N, N), BF)],
-        compiler_params=params(28),
+        compiler_params=params(),
         name="triangle_product",
     )(factors, factors)
 
@@ -208,12 +216,12 @@
         ],
         out_specs=[each_spec(C, H, W), each_spec(C, H, W), whole_spec(C, H, W)],
         out_shape=[
-            jax.ShapeDtypeStruct((T, C, H, W), BF),
-            jax.ShapeDtypeStruct((T, C, H, W), BF),
+            pltpu.HBM((T, C, H, W), BF),
+            pltpu.HBM((T, C, H, W), BF),
             jax.ShapeDtypeStruct((C, H, W), F32),
         ],
         scratch_shapes=[pltpu.VMEM((C, 8, W), F32)],
-        compiler_params=params(24),
+        compiler_params=params(),
         cost_estimate=pl.CostEstimate(flops=4 * 2**31, bytes_accessed=16 * 2**20, transcendentals=2**21),
         name="back_project",
     )(pair, left, right, lanes, gain, inv, grad, kg, kb)
@@ -240,7 +248,7 @@
         in_specs=[each_spec(C, H, W), each_spec(C, H, W)],
         out_specs=each_spec(C, H, W),
         out_shape=pltpu.HBM((T, C, H, W), BF),
-        compiler_params=params(16),
+        compiler_params=params(),
         cost_estimate=pl.CostEstimate(flops=2**25, bytes_accessed=12 * 2**20, transcendentals=0),
         name="product_grad",
     )(prod, back)
@@ -334,7 +342,7 @@
             jax.ShapeDtypeStruct((C, W), F32),
         ],
         scratch_shapes=[pltpu.VMEM((C, H, W), F32)],
-        compiler_params=params(24),
+        compiler_params=params(),
         cost_estimate=pl.CostEstimate(flops=4 * 2**31, bytes_accessed=12 * 2**20, transcendentals=2**21),
         name="gate_and_embed",
     )(prod, scaled, grad, pair_sum, inv, kg, ko, pick)
@@ -358,8 +366,8 @@
         grid=(2,),
         in_specs=[spec(0), spec(2), pl.BlockSpec((128, H, W), lambda s: (0, 0, 0))],
         out_specs=[out, out, pl.BlockSpec((N, N), lambda s: (0, 0))],
-        out_shape=[jax.ShapeDtypeStruct((2, N, N), BF)] * 2 + [jax.ShapeDtypeStruct((N, N), BF)],
-        compiler_params=params(28),
+        out_shape=[pltpu.HBM((2, N, N), BF), pltpu.HBM((2, N, N), BF), pltpu.HBM((N, N), BF)],
+        compiler_params=params(),
         cost_estimate=pl.CostEstimate(flops=2**20, bytes_accessed=20 * 2**20, transcendentals=0),
         name="to_matrices",
     )(factors, factors, inv)
@@ -372,7 +380,7 @@
     step = pl.program_id(0)
     core = core_ref[0]
     left, right = left_ref.at[0], right_ref.at[0]
-    spread(grad_ref, grad)
+    grad[...] = matrix(grad_ref)
 
     @pl.when(step == 0)
     def _():
@@ -440,7 +448,7 @@
             jax.ShapeDtypeStruct((2, 2, N, W), F32),
         ],
         scratch_shapes=[pltpu.VMEM((N, N), BF), pltpu.VMEM((N, N), F32)],
-        compiler_params=params(44),
+        compiler_params=params(),
         name="factor_grads",
     )(core.reshape(1), left, right, grad, inv)
 
@@ -482,7 +490,7 @@
         ],
         out_specs=both(C, W),
         out_shape=jax.ShapeDtypeStruct((2, T, C, W), BF),
-        compiler_params=params(16),
+        compiler_params=params(),
         name="close_sums",
     )(recv, mean, inv, scaled, pick, weights, valid, base)
 
@@ -549,6 +557,9 @@
     member = col % 4
     sent_feat = jnp.broadcast_to(template_feat.reshape(1, 4, 16, W), (32, 4, 16, W))
     pool = exchange(sent_feat.reshape(128, 16, W))
+    gain = norm_gain.astype(F32)
+    gain_wide = jnp.broadcast_to(gain[:, None, None], (C, 8, W))
+    pool, gain_wide = lax.optimization_barrier((pool, gain_wide))
     column_ids = lambda m, at: lax.dynamic_index_in_dim(m, at, axis=1, keepdims=False)
     row_ids = column_ids(block_map, row_block)
     member_ids = [column_ids(block_map, col ^ k) for k in range(4)]
@@ -573,26 +584,48 @@
     row_valid = (marks(row_block) & (offsets // H == half)[None, :]).astype(F32)
     left_terms = jnp.einsum("fc,tfi->tci", embeds[0], feats[4:], preferred_element_type=F32)
     left_terms = left_terms * row_valid[:, None, :]
-    near, far = left_terms[:, :, :H], left_terms[:, :, H:]
-    left_twice = near + far
-    left_twice = jnp.concatenate([left_twice, left_twice], axis=2)
     right_terms = jnp.einsum("fc,tfj->tcj", embeds[1], feats[:4], preferred_element_type=F32)
     right_terms = right_terms * col_valid[:, None, :]
-    gain = norm_gain.astype(F32)
-    gain_wide = jnp.broadcast_to(gain[:, None, None], (C, 8, W))
     kl, kr, kg, ko, kb = expand(
         jnp.stack([left_proj.T, right_proj.T, gate_proj.T, out_proj.T, out_proj])
     )
     group = 2 * np.arange(4)[:, None, None] + (np.arange(2 * W) // W)[None, :, None]
     lanes = np.arange(W)[None, None, :] % H // 8 == group
-    terms_pick = jnp.asarray(lanes.transpose(0, 2, 1), BF)
+    terms_pick = jnp.asarray(np.tile(lanes.transpose(0, 2, 1), (1, 2, 1)), BF)
     sums_pick = jnp.where((offsets // H == half)[None, None, :], jnp.asarray(lanes, BF), 0)
 
-    terms = (template_pair, left_twice, right_terms, terms_pick, gain_wide)
+    terms = (template_pair, left_terms, right_terms, terms_pick, gain_wide)
     sent, inv = run_norm(*terms, kl, kr)
+    def center(weights):
+        scaled_weights = gain[:, None] * weights.astype(F32)
+        return scaled_weights - jnp.mean(scaled_weights, axis=0, keepdims=True)
+
+    embeds = embeds.astype(F32)
+    mixed = jnp.einsum(
+        "efd,kdc->kefc",
+        embeds,
+        jnp.stack([center(left_proj), center(right_proj), center(gate_proj)]),
+        precision=HIGHEST,
+    )
+    closing = -embeds / gain[None, None, :]
+    opening = embeds * (1.0 / T)
+    weights = lax.dynamic_slice_in_dim(mixed[:2], 2 * pair_at, 2, axis=3)
+    own_map = lax.dynamic_index_in_dim(block_map, own, axis=0, keepdims=False)
+    own_count = lax.dynamic_index_in_dim(block_count, own, axis=0, keepdims=False)
+    own_marks = lax.dynamic_index_in_dim(residue_mask, own, axis=0, keepdims=False)
+    own_valid = (offsets[None, :] < own_count[:, None]) & (own_marks.reshape(8, W) == 1)
+    own_valid = own_valid.astype(F32)
+    targets = jnp.concatenate(
+        [own_map] * 4 + [jnp.concatenate([row_ids, ids]) for ids in member_ids]
+    )
+    place = (targets[None, :] == blocks[:, None]).astype(BF)
     factors = exchange(sent.reshape(128, ROWS, W))
     scaled, back, pair_sum = run_back(*terms, inv, embed_grad, kg, kb)
-    factors, scaled, back, pair_sum = lax.optimization_barrier((factors, scaled, back, pair_sum))
+    factors, scaled, back, pair_sum, mixed, closing, opening, weights, own_valid, place = (
+        lax.optimization_barrier(
+            (factors, scaled, back, pair_sum, mixed, closing, opening, weights, own_valid, place)
+        )
+    )
     my_inv = factors[:, 256:]
     inv_all = in_order(core, my_inv, swap_cores(my_inv), 1)
     prod = exchange(run_product(factors)).reshape(T, C, H, W)
@@ -612,19 +645,6 @@
     col_sums, row_sums, mean_half = lax.optimization_barrier((col_sums, row_sums, mean_half))
     recv = exchange(mean_half).reshape(T, 16, 2, H // 2, W)
 
-    def center(weights):
-        scaled_weights = gain[:, None] * weights.astype(F32)
-        return scaled_weights - jnp.mean(scaled_weights, axis=0, keepdims=True)
-
-    embeds = embeds.astype(F32)
-    mixed = jnp.einsum(
-        "efd,kdc->kefc",
-        embeds,
-        jnp.stack([center(left_proj), center(right_proj), center(gate_proj)]),
-        precision=HIGHEST,
-    )
-    closing = -embeds / gain[None, None, :]
-    opening = embeds * (1.0 / T)
     valid = jnp.stack([row_valid, col_valid])[:, :, None, :]
     base = jnp.einsum(
         "efc,etcp->etfp", mixed[2], jnp.stack([gate_rows, gate_cols]), precision=HIGHEST
@@ -634,24 +654,18 @@
     )
     base = (base + opened[:, None]) * valid
     owned = jnp.stack([jnp.sum(row_sums, axis=3), jnp.sum(col_sums, axis=2)], axis=2)
-    weights = lax.dynamic_slice_in_dim(mixed[:2], 2 * pair_at, 2, axis=3)
     grad_own = jnp.einsum("kefs,sken->fn", weights, owned, precision=HIGHEST)
-    own_map = lax.dynamic_index_in_dim(block_map, own, axis=0, keepdims=False)
-    own_count = lax.dynamic_index_in_dim(block_count, own, axis=0, keepdims=False)
-    own_marks = lax.dynamic_index_in_dim(residue_mask, own, axis=0, keepdims=False)
-    own_valid = (offsets[None, :] < own_count[:, None]) & (own_marks.reshape(8, W) == 1)
-    grad_own = grad_own.reshape(C, 8, W).transpose(1, 0, 2) * own_valid.astype(F32)[:, None, :]
+    grad_own = grad_own.reshape(C, 8, W).transpose(1, 0, 2) * own_valid[:, None, :]
     grad_own = grad_own.astype(BF)
-    targets = jnp.concatenate([jnp.concatenate([own_map, row_ids, ids]) for ids in member_ids])
-    place = (targets[None, :] == blocks[:, None]).astype(BF)
-    recv, base, grad_own, place = lax.optimization_barrier((recv, base, grad_own, place))
-
+    def quarters(value):
+        cut = [value[:, k * 16 : k * 16 + 16] for k in range(4)]
+        return [cut[0]] + [from_member(cut[k], k) for k in range(1, 4)]
+
+    own_parts = quarters(grad_own)
+    recv, base, *own_parts = lax.optimization_barrier((recv, base, *own_parts))
     closed = run_close(recv, gate_mean, inv, scaled, sums_pick, closing, valid, base)
-    entries = jnp.concatenate([grad_own, closed.reshape(2 * T, C, W)], axis=0)
-    quarters = [entries[:, k * 16 : k * 16 + 16] for k in range(4)]
-    entries = jnp.concatenate(
-        [quarters[0]] + [from_member(quarters[k], k) for k in range(1, 4)], axis=0
-    )
+    parts = quarters(closed.reshape(2 * T, C, W))
+    entries = jnp.concatenate([*own_parts, *parts], axis=0)
     placed = jnp.einsum(
         "be,ex->bx", place, entries.reshape(64, 16 * W), preferred_element_type=F32
     ).astype(BF)

time: 393 us -> 381 us (0.969)
  local copies, waits for them, and re-layouts: 46.7 us -> 14.9 us
  Pallas kernels: 83 us -> 96.5 us
  waiting for transfers between devices: 172 us -> 182 us
    unnamed x116 -> x42, local copies, waits for them, and re-layouts: 36.3 us -> 7.54 us
    all_to_all x5, waiting for transfers between devices: 163 us -> 169 us  [exchange(): return lax.all_to_all(value, AXES, split_axis=0, concat_axis=0, tiled=True)]
    ppermute x8 -> x11, waiting for transfers between devices: 8.58 us -> 13.3 us  [from_member(): return lax.ppermute(value, 'col', [(i, i ^ k) for i in range(8)])]
    ppermute x8 -> x11, starting transfers between devices: 7.98 us -> 11.5 us  [from_member(): return lax.ppermute(value, 'col', [(i, i ^ k) for i in range(8)])]
  transfers between devices with their start and end apart: 13 -> 16, of which waited for: 9 -> 13; matrix products, arithmetic and copies ran while one was open for 8% -> 6% of each run, Pallas kernels for 10% -> 12%
where the time goes in v5:
time: 381 us; the launch traced here: 380 us
  waiting for transfers between devices  182 us (48%)
  Pallas kernels  96.5 us (25%)
  starting transfers between devices  48.6 us (13%)
  blocking collectives  17.7 us (5%)
  local copies, waits for them, and re-layouts  14.9 us (4%)
  other arithmetic  10.7 us (3%)
  matrix products  7.99 us (2%)
    all_to_all x5, waiting for transfers between devices, exchange(): return lax.all_to_all(value, AXES, split_axis=0, concat_axis=0, tiled=True)  169 us
    all_to_all x5, starting transfers between devices, exchange(): return lax.all_to_all(value, AXES, split_axis=0, concat_axis=0, tiled=True)  37.1 us
    pallas_call x1, Pallas kernels, run_gate(): pl.pallas_call(gate_kernel, grid=(T,), in_specs=[each_spec(C, H, W), each...  22.5 us
    all_to_all x1, blocking collectives, exchange(): return lax.all_to_all(value, AXES, split_axis=0, concat_axis=0, tiled=True)  17.7 us
    pallas_call x1, Pallas kernels, run_factor(): pl.pallas_call(factor_kernel, grid=(2,), in_specs=[pl.BlockSpec(memory_sp...  16.3 us
    pallas_call x1, Pallas kernels, run_back(): pl.pallas_call(back_kernel, grid=(T,), in_specs=[*TERM_SPECS, each_spec(H...  16 us
    ppermute x11, waiting for transfers between devices, from_member(): return lax.ppermute(value, 'col', [(i, i ^ k) for i in range(8)])  13.3 us
    ppermute x11, starting transfers between devices, from_member(): return lax.ppermute(value, 'col', [(i, i ^ k) for i in range(8)])  11.5 us
  transfers between devices with their start and end apart: 16, of which 13 were waited for; matrix products, arithmetic and copies ran while one was open for 6% of the time, Pallas kernels for 12%

profile of v5, /device:TPU:1, one launch (start us, length us, event | category | flops | bytes accessed | tf_op | source)
XLA Modules:
  0.0 379.9 jit_solution(9022928806426468185)
XLA Ops:
  0.7 1.6 broadcast_in_dim.31
  2.3 11.5 %all-to-all-start = ((bf16[128,16,128]{2,1,0:T(8,128)(2,1)}), bf16[128,16,128]{2,1,0:T(8,128)(2,1)S(1)}, u32[]{:S(2)}, u32[]{:S(2)}) async-start(bf16[128,16,128]{2,1,0:T(8,128)(2,1)} %bitcast.1), calls=%async_computation | async-start | bytes 1048576 | tf_op jit(solution)/shard_map/all_to_all | solution.py:507
  21.7 2.0 select_convert_fusion
  24.1 1.5 slice_bitcast_fusion
  25.7 1.7 all-to-all-done
  29.8 1.5 collective-permute-start.2
  35.3 11.5 %pair_norm.1 = (bf16[4,32,288,128]{3,2,1,0:T(8,128)(2,1)}, f32[4,64,128]{2,1,0:T(8,128)}) custom-call(bf16[4,64,64,128]{3,2,1,0:T(8,128)(2,1)} %pair_ref.3, f32[4,64,128]{2,1,0:T(8,128)} %fusion.5.left_ref, f32[4,64,128]{2,1,0:T(8,128)} %fusion.4.right_ref, bf16[4,256,256]{2,1,0:T(8,128)(2,1)} %constant.168.clone.lanes_ref, ...), custom_call_target="tpu_custom_call" | custom-call | tf_op jit(solution)/shard_map/pair_norm/pallas_call | solution.py:120
  46.7 8.5 %all-to-all-start.1 = ((bf16[128,288,128]{2,1,0:T(8,128)(2,1)}), bf16[128,288,128]{2,1,0:T(8,128)(2,1)}, u32[]{:S(2)}, u32[]{:S(2)}) async-start(bf16[128,288,128]{2,1,0:T(8,128)(2,1)} %bitcast.151), calls=%async_computation.1 | async-start | bytes 18874368 | tf_op jit(solution)/shard_map/all_to_all | solution.py:507
  57.1 16.0 %back_project.1 = (bf16[4,64,64,128]{3,2,1,0:T(8,128)(2,1)}, bf16[4,64,64,128]{3,2,1,0:T(8,128)(2,1)}, f32[64,64,128]{2,1,0:T(8,128)}) custom-call(bf16[4,64,64,128]{3,2,1,0:T(8,128)(2,1)} %pair_ref.3, f32[4,64,128]{2,1,0:T(8,128)} %fusion.5.left_ref, f32[4,64,128]{2,1,0:T(8,128)} %fusion.4.right_ref, bf16[4,256,256]{2,1,0:T(8,128)(2,1)} %constant.168.clone.lanes_ref, ...), custom_call_target="tpu_custom_call" | custom-call | flops 8589934592 | bytes 16777216 | tf_op jit(solution)/shard_map/back_project/pallas_call | solution.py:211
  73.1 94.3 %all-to-all-done.1.left_ref.right_ref = bf16[128,288,128]{2,1,0:T(8,128)(2,1)} async-done(((bf16[128,288,128]{2,1,0:T(8,128)(2,1)}), bf16[128,288,128]{2,1,0:T(8,128)(2,1)}, u32[]{:S(2)}, u32[]{:S(2)}) %all-to-all-start.1) | async-done | bytes 9437216 | tf_op jit(solution)/shard_map/all_to_all | solution.py:507
  167.4 8.4 %triangle_product.1 = bf16[128,128,128]{2,1,0:T(8,128)(2,1)} custom-call(bf16[128,288,128]{2,1,0:T(8,128)(2,1)} %all-to-all-done.1.left_ref.right_ref, bf16[128,288,128]{2,1,0:T(8,128)(2,1)} %all-to-all-done.1.left_ref.right_ref), custom_call_target="tpu_custom_call" | custom-call | tf_op jit(solution)/shard_map/triangle_product/pallas_call | solution.py:164
  175.8 7.9 %all-to-all-start.2 = ((bf16[128,128,128]{2,1,0:T(8,128)(2,1)}), bf16[128,128,128]{2,1,0:T(8,128)(2,1)}, u32[]{:S(2)}, u32[]{:S(2)}) async-start(bf16[128,128,128]{2,1,0:T(8,128)(2,1)} %triangle_product.1), calls=%async_computation.2 | async-start | bytes 8388608 | tf_op jit(solution)/shard_map/all_to_all | solution.py:507
  185.0 1.4 collective-permute-start.3
  186.4 2.3 collective-permute-done.3
  190.1 1.6 pad_maximum_fusion.inv_ref
  191.7 8.1 %to_matrices.1 = (bf16[2,1024,1024]{2,1,0:T(8,128)(2,1)}, bf16[2,1024,1024]{2,1,0:T(8,128)(2,1)}, bf16[1024,1024]{1,0:T(8,128)(2,1)}) custom-call(bf16[128,288,128]{2,1,0:T(8,128)(2,1)} %all-to-all-done.1.left_ref.right_ref, bf16[128,288,128]{2,1,0:T(8,128)(2,1)} %all-to-all-done.1.left_ref.right_ref, bf16[128,64,128]{2,1,0:T(8,128)(2,1)} %pad_maximum_fusion.inv_ref), custom_call_target="tpu_custom_call" | custom-call | flops 1048576 | bytes 20971520 | tf_op jit(solution)/shard_map/to_matrices/pallas_call | solution.py:364
  199.8 36.7 %all-to-all-done.2 = bf16[128,128,128]{2,1,0:T(8,128)(2,1)} async-done(((bf16[128,128,128]{2,1,0:T(8,128)(2,1)}), bf16[128,128,128]{2,1,0:T(8,128)(2,1)}, u32[]{:S(2)}, u32[]{:S(2)}) %all-to-all-start.2) | async-done | bytes 4194336 | tf_op jit(solution)/shard_map/all_to_all | solution.py:507
  236.5 7.9 %product_grad.1 = bf16[4,64,64,128]{3,2,1,0:T(8,128)(2,1)} custom-call(bf16[4,64,64,128]{3,2,1,0:T(8,128)(2,1)} %bitcast.40.prod_ref, bf16[4,64,64,128]{3,2,1,0:T(8,128)(2,1)} %get-tuple-element.64.back_ref), custom_call_target="tpu_custom_call" | custom-call | flops 33554432 | bytes 12582912 | tf_op jit(solution)/shard_map/product_grad/pallas_call | solution.py:245
  244.4 5.5 %all-to-all-start.3 = ((bf16[128,128,128]{2,1,0:T(8,128)(2,1)}), bf16[128,128,128]{2,1,0:T(8,128)(2,1)}, u32[]{:S(2)}, u32[]{:S(2)}) async-start(bf16[128,128,128]{2,1,0:T(8,128)(2,1)} %bitcast.150), calls=%async_computation.3 | async-start | bytes 8388608 | tf_op jit(solution)/shard_map/all_to_all | solution.py:507
  250.7 22.5 %gate_and_embed.1 = (bf16[64,64,128]{2,1,0:T(8,128)(2,1)}, f32[4,64,128]{2,1,0:T(8,128)}, f32[4,64,128]{2,1,0:T(8,128)}, f32[4,64,128]{2,1,0:T(8,128)}, f32[64,128]{1,0:T(8,128)}, /*index=5*/f32[64,128]{1,0:T(8,128)}) custom-call(bf16[4,64,64,128]{3,2,1,0:T(8,128)(2,1)} %bitcast.40.prod_ref, bf16[4,64,64,128]{3,2,1,0:T(8,128)(2,1)} %get-tuple-element.65.scaled_ref, ...), custom_call_target="tpu_custom_call" | custom-call | flops 8589934592 | bytes 12582912 | tf_op jit(solution)/shard_map/gate_and_embed/pallas_call | solution.py:325
  273.2 29.7 %all-to-all-done.3.grad_ref = bf16[128,128,128]{2,1,0:T(8,128)(2,1)} async-done(((bf16[128,128,128]{2,1,0:T(8,128)(2,1)}), bf16[128,128,128]{2,1,0:T(8,128)(2,1)}, u32[]{:S(2)}, u32[]{:S(2)}) %all-to-all-start.3) | async-done | bytes 4194336 | tf_op jit(solution)/shard_map/all_to_all | solution.py:507
  302.9 16.3 %factor_grads.1 = (bf16[128,32,128]{2,1,0:T(8,128)(2,1)}, bf16[128,32,128]{2,1,0:T(8,128)(2,1)}, f32[2,2,8,1024]{3,2,1,0:T(8,128)}, f32[2,2,1024,128]{3,2,1,0:T(8,128)}) custom-call(s32[1]{0:T(128)} %bitcast.43.core_ref, bf16[2,1024,1024]{2,1,0:T(8,128)(2,1)} %get-tuple-element.75.left_ref, bf16[2,1024,1024]{2,1,0:T(8,128)(2,1)} %get-tuple-element.76.right_ref, ...), custom_call_target="tpu_custom_call" | custom-call | tf_op jit(solution)/shard_map/factor_grads/pallas_call | solution.py:428
  320.3 2.5 collective-permute-done.4
  322.8 2.5 add_convert_fusion
  325.3 3.8 all-to-all-start.4
  335.2 2.1 fusion.3.base_ref
  337.3 2.1 collective-permute-done.6
  339.4 2.2 collective-permute-done.7
  341.6 6.6 %all-to-all-done.4 = bf16[128,32,128]{2,1,0:T(8,128)(2,1)S(1)} async-done(((bf16[128,32,128]{2,1,0:T(8,128)(2,1)}), bf16[128,32,128]{2,1,0:T(8,128)(2,1)S(1)}, u32[]{:S(2)}, u32[]{:S(2)}) %all-to-all-start.4) | async-done | bytes 1048608 | tf_op jit(solution)/shard_map/all_to_all | solution.py:507
  349.2 5.8 %close_sums.1 = bf16[2,4,64,128]{3,2,1,0:T(8,128)(2,1)} custom-call(bf16[4,16,2,32,128]{4,3,2,1,0:T(8,128)(2,1)} %bitcast.152, f32[4,64,128]{2,1,0:T(8,128)} %get-tuple-element.99.mean_ref, f32[4,64,128]{2,1,0:T(8,128)} %get-tuple-element.55.inv_ref, bf16[4,64,64,128]{3,2,1,0:T(8,128)(2,1)} %get-tuple-element.65.scaled_ref, ...), custom_call_target="tpu_custom_call" | custom-call | tf_op jit(solution)/shard_map/close_sums/pallas_call | solution.py:484
  357.3 1.6 collective-permute-start.10
  361.4 17.7 %all_to_all.30 = bf16[128,16,128]{2,1,0:T(8,128)(2,1)S(1)} all-to-all(bf16[128,16,128]{2,1,0:T(8,128)(2,1)S(1)} %bitcast.154), channel_id=1, replica_groups=mesh['row'=16,'col'=8] {'row','col'}, dimensions={0} | all-to-all | bytes 1048576 | tf_op jit(solution)/shard_map/all_to_all | solution.py:507
  (108 shorter events, 33.4 us)
Async XLA Ops:
  0.6 23.0 %copy-start.6 = (s32[4,8]{1,0:T(4,128)S(1)}, s32[4,8]{1,0:T(4,128)}, u32[]{:S(2)}) copy-start(s32[4,8]{1,0:T(4,128)} %param.18) | copy-start | bytes 388
  0.6 23.0 %copy-start.9 = (s32[4,8]{1,0:T(4,128)S(1)}, s32[4,8]{1,0:T(4,128)}, u32[]{:S(2)}) copy-start(s32[4,8]{1,0:T(4,128)} %param.19) | copy-start | bytes 388
  0.7 23.4 %copy-start.10 = (s32[4,1024]{1,0:T(4,128)S(1)}, s32[4,1024]{1,0:T(4,128)}, u32[]{:S(2)}) copy-start(s32[4,1024]{1,0:T(4,128)} %param.20) | copy-start | bytes 49156
  2.3 25.0 %all-to-all-start = ((bf16[128,16,128]{2,1,0:T(8,128)(2,1)}), bf16[128,16,128]{2,1,0:T(8,128)(2,1)S(1)}, u32[]{:S(2)}, u32[]{:S(2)}) async-start(bf16[128,16,128]{2,1,0:T(8,128)(2,1)} %bitcast.1), calls=%async_computation | async-start | bytes 1048576 | tf_op jit(solution)/shard_map/all_to_all | solution.py:507
  21.7 5.6 %copy-start.11 = (bf16[64]{0:T(256)(128)(2,1)S(1)}, bf16[64]{0:T(256)(128)(2,1)}, u32[]{:S(2)}) copy-start(bf16[64]{0:T(256)(128)(2,1)} %param.23) | copy-start | bytes 388
  28.4 2.9 collective-permute-start
  29.6 2.8 collective-permute-start.1
  29.8 3.7 collective-permute-start.2
  46.7 8.5 %copy-start.3 = (bf16[64,64]{1,0:T(8,128)(2,1)S(1)}, bf16[64,64]{1,0:T(8,128)(2,1)}, u32[]{:S(2)}) copy-start(bf16[64,64]{1,0:T(8,128)(2,1)} %param.24) | copy-start | bytes 24580
  46.7 8.6 %copy-start.4 = (bf16[64,64]{1,0:T(8,128)(2,1)S(1)}, bf16[64,64]{1,0:T(8,128)(2,1)}, u32[]{:S(2)}) copy-start(bf16[64,64]{1,0:T(8,128)(2,1)} %param.25) | copy-start | bytes 24580
  46.7 8.7 %copy-start.5 = (bf16[64,64]{1,0:T(8,128)(2,1)S(1)}, bf16[64,64]{1,0:T(8,128)(2,1)}, u32[]{:S(2)}) copy-start(bf16[64,64]{1,0:T(8,128)(2,1)} %param.26) | copy-start | bytes 24580
  46.7 120.6 %all-to-all-start.1 = ((bf16[128,288,128]{2,1,0:T(8,128)(2,1)}), bf16[128,288,128]{2,1,0:T(8,128)(2,1)}, u32[]{:S(2)}, u32[]{:S(2)}) async-start(bf16[128,288,128]{2,1,0:T(8,128)(2,1)} %bitcast.151), calls=%async_computation.1 | async-start | bytes 18874368 | tf_op jit(solution)/shard_map/all_to_all | solution.py:507
  175.8 60.7 %all-to-all-start.2 = ((bf16[128,128,128]{2,1,0:T(8,128)(2,1)}), bf16[128,128,128]{2,1,0:T(8,128)(2,1)}, u32[]{:S(2)}, u32[]{:S(2)}) async-start(bf16[128,128,128]{2,1,0:T(8,128)(2,1)} %triangle_product.1), calls=%async_computation.2 | async-start | bytes 8388608 | tf_op jit(solution)/shard_map/all_to_all | solution.py:507
  185.0 3.7 collective-permute-start.3
  244.4 5.5 %copy-start.2 = (bf16[4,256,128]{2,1,0:T(8,128)(2,1)S(1)}, bf16[4,256,128]{2,1,0:T(8,128)(2,1)}, u32[]{:S(2)}) copy-start(bf16[4,256,128]{2,1,0:T(8,128)(2,1)} %constant.169.clone) | copy-start | bytes 786436
  244.4 58.5 %all-to-all-start.3 = ((bf16[128,128,128]{2,1,0:T(8,128)(2,1)}), bf16[128,128,128]{2,1,0:T(8,128)(2,1)}, u32[]{:S(2)}, u32[]{:S(2)}) async-start(bf16[128,128,128]{2,1,0:T(8,128)(2,1)} %bitcast.150), calls=%async_computation.3 | async-start | bytes 8388608 | tf_op jit(solution)/shard_map/all_to_all | solution.py:507
  319.1 10.0 %copy-start.8 = (f32[64,128]{1,0:T(8,128)S(1)}, f32[64,128]{1,0:T(8,128)}, u32[]{:S(2)}) copy-start(f32[64,128]{1,0:T(8,128)} %get-tuple-element.88) | copy-start | bytes 98308
  319.1 11.9 %copy-start.1 = (f32[2,2,1024,128]{3,2,1,0:T(8,128)S(1)}, f32[2,2,1024,128]{3,2,1,0:T(8,128)}, u32[]{:S(2)}) copy-start(f32[2,2,1024,128]{3,2,1,0:T(8,128)} %get-tuple-element.91) | copy-start | bytes 6291460
  319.1 3.6 collective-permute-start.4
  320.3 15.0 %copy-start.7 = (f32[2,4,128]{2,1,0:T(4,128)}, f32[2,4,128]{2,1,0:T(4,128)S(1)}, u32[]{:S(2)}) copy-start(f32[2,4,128]{2,1,0:T(4,128)S(1)} %pad_maximum_fusion.2) | copy-start | bytes 12292
  325.3 22.8 %all-to-all-start.4 = ((bf16[128,32,128]{2,1,0:T(8,128)(2,1)}), bf16[128,32,128]{2,1,0:T(8,128)(2,1)S(1)}, u32[]{:S(2)}, u32[]{:S(2)}) async-start(bf16[128,32,128]{2,1,0:T(8,128)(2,1)} %add_convert_fusion), calls=%async_computation.4 | async-start | bytes 2097152 | tf_op jit(solution)/shard_map/all_to_all | solution.py:507
  332.2 5.1 %collective-permute-start.5 = (bf16[8,16,128]{2,1,0:T(8,128)(2,1)S(1)}, bf16[8,16,128]{2,1,0:T(8,128)(2,1)S(1)}, u32[]{:S(2)}, u32[]{:S(2)}) collective-permute-start(bf16[8,16,128]{2,1,0:T(8,128)(2,1)S(1)} %get-tuple-element.125), channel_id=1, source_target_pairs={{0,1},{1,0},{2,3},{3,2},{4,5},{5,4},{6,7},{7,6},{8,9},{9,8},{10,11... | collective-permute-start | bytes 98312 | tf_op jit(solution)/shard_map/ppermute | solution.py:499
  333.5 5.9 %collective-permute-start.6 = (bf16[8,16,128]{2,1,0:T(8,128)(2,1)S(1)}, bf16[8,16,128]{2,1,0:T(8,128)(2,1)S(1)}, u32[]{:S(2)}, u32[]{:S(2)}) collective-permute-start(bf16[8,16,128]{2,1,0:T(8,128)(2,1)S(1)} %get-tuple-element.124), channel_id=1, source_target_pairs={{0,2},{1,3},{2,0},{3,1},{4,6},{5,7},{6,4},{7,5},{8,10},{9,11},{10,... | collective-permute-start | bytes 98312 | tf_op jit(solution)/shard_map/ppermute | solution.py:499
  334.1 7.5 %collective-permute-start.7 = (bf16[8,16,128]{2,1,0:T(8,128)(2,1)S(1)}, bf16[8,16,128]{2,1,0:T(8,128)(2,1)S(1)}, u32[]{:S(2)}, u32[]{:S(2)}) collective-permute-start(bf16[8,16,128]{2,1,0:T(8,128)(2,1)S(1)} %get-tuple-element.123), channel_id=1, source_target_pairs={{0,3},{1,2},{2,1},{3,0},{4,7},{5,6},{6,5},{7,4},{8,11},{9,10},{10,... | collective-permute-start | bytes 98312 | tf_op jit(solution)/shard_map/ppermute | solution.py:499
  348.2 1.0 copy-start
  355.8 3.1 collective-permute-start.8
  357.2 2.8 collective-permute-start.9
  357.3 3.7 collective-permute-start.10

commit v6 on v5

--- a/solution.py
+++ b/solution.py
@@ -18,11 +18,11 @@
 W = 128
 N = 1024
 K8 = C * 8
-ROWS = 288
-
-
-def params():
-    return pltpu.CompilerParams(vmem_limit_bytes=60 * 2**20)
+ROWS = 272
+
+
+def params(mib=60):
+    return pltpu.CompilerParams(vmem_limit_bytes=mib * 2**20)
 
 
 def stack_rows(top, bottom):
@@ -58,11 +58,12 @@
     return (lane % 8 == lax.broadcasted_iota(jnp.int32, (8, width), 0)).astype(F32)
 
 
-def spread_terms(left_ref, right_ref, right):
+def spread_terms(left_ref, right_ref, gain_ref, right, gain):
     mask = row_mask(W)
     rows = []
     for c in range(C):
         right[c] = jnp.broadcast_to(right_ref[0, c : c + 1, :], (8, W))
+        gain[c] = jnp.broadcast_to(gain_ref[c : c + 1, :], (8, W))
         rows.append(jnp.broadcast_to(left_ref[0, c : c + 1, :], (8, W)) * mask)
     value = jnp.concatenate(rows, axis=0)
     high = value.astype(BF)
@@ -77,9 +78,9 @@
 
 def norm_kernel(
     pair_ref, left_ref, right_ref, lanes_ref, gain_ref, kl_ref, kr_ref, pay_ref, inv_ref,
-    right, terms, wide,
+    right, gain, terms, wide,
 ):
-    left = spread_terms(left_ref, right_ref, right)
+    left = spread_terms(left_ref, right_ref, gain_ref, right, gain)
     for g in range(4):
         terms[g] = jnp.dot(left, lanes_ref[g], preferred_element_type=F32)
     for g in range(4):
@@ -90,14 +91,13 @@
             pair = raw[part] + left_terms[part] + right[...]
             shifted = pair - mean_channels(pair)
             inverse = lax.rsqrt(mean_channels(shifted * shifted) + EPS)
-            scaleds.append(shifted * inverse * gain_ref[...])
+            scaleds.append(shifted * inverse * gain[...])
             invs.append(inverse[0])
         both = jnp.concatenate(invs, axis=0)
         inv_ref[0, g * 16 : g * 16 + 16, :] = both
         wide[:, g * 256 : g * 256 + 256] = stack_rows(*scaleds).astype(BF)
-        first = 256 + (g % 2) * 16
-        for q in range(g // 2, C // 2, 2):
-            pay_ref[0, q, first : first + 16, :] = both.astype(BF)
+        for q in range(g, C // 2, 4):
+            pay_ref[0, q, 256:272, :] = both.astype(BF)
     for k, weight in enumerate((kl_ref, kr_ref)):
         outs = jnp.dot(weight[...], wide[...], preferred_element_type=F32)
         for g in range(4):
@@ -112,7 +112,7 @@
     each_spec(C, W),
     each_spec(C, W),
     whole_spec(4, 2 * W, 2 * W),
-    whole_spec(C, 8, W),
+    whole_spec(C, W),
 ]
 
 
@@ -127,6 +127,7 @@
             jax.ShapeDtypeStruct((T, H, W), F32),
         ],
         scratch_shapes=[
+            pltpu.VMEM((C, 8, W), F32),
             pltpu.VMEM((C, 8, W), F32),
             pltpu.VMEM((4, K8, 2 * W), F32),
             pltpu.VMEM((K8, N), BF),
@@ -174,10 +175,10 @@
 
 def back_kernel(
     pair_ref, left_ref, right_ref, lanes_ref, gain_ref, inv_ref, grad_ref, kg_ref, kb_ref,
-    scaled_ref, out_ref, sum_ref, right,
+    scaled_ref, out_ref, sum_ref, right, gain,
 ):
     step = pl.program_id(0)
-    left = spread_terms(left_ref, right_ref, right)
+    left = spread_terms(left_ref, right_ref, gain_ref, right, gain)
 
     @pl.when(step == 0)
     def _():
@@ -191,7 +192,7 @@
         for part in range(2):
             first = g * 16 + part * 8
             inverse = inv_ref[0, first : first + 8, :][None]
-            scaleds.append((pairs[part] - mean_channels(pairs[part])) * inverse * gain_ref[...])
+            scaleds.append((pairs[part] - mean_channels(pairs[part])) * inverse * gain[...])
         scaled_ref[0, :, rows, :] = join_rows(*scaleds).astype(BF)
         opened = unstack_rows(
             jnp.dot(kg_ref[...], stack_rows(*scaleds).astype(BF), preferred_element_type=F32)
@@ -220,7 +221,7 @@
             pltpu.HBM((T, C, H, W), BF),
             jax.ShapeDtypeStruct((C, H, W), F32),
         ],
-        scratch_shapes=[pltpu.VMEM((C, 8, W), F32)],
+        scratch_shapes=[pltpu.VMEM((C, 8, W), F32), pltpu.VMEM((C, 8, W), F32)],
         compiler_params=params(),
         cost_estimate=pl.CostEstimate(flops=4 * 2**31, bytes_accessed=16 * 2**20, transcendentals=2**21),
         name="back_project",
@@ -453,6 +454,23 @@
     )(core.reshape(1), left, right, grad, inv)
 
 
+def add_kernel(left_ref, right_ref, out_ref):
+    out_ref[...] = (left_ref[...].astype(F32) + right_ref[...].astype(F32)).astype(BF)
+
+
+def run_add(left, right):
+    spec = pl.BlockSpec((64, H // 2, W), lambda i: (i, 0, 0))
+    return pl.pallas_call(
+        add_kernel,
+        grid=(2,),
+        in_specs=[spec, spec],
+        out_specs=spec,
+        out_shape=pltpu.HBM((128, H // 2, W), BF),
+        compiler_params=params(40),
+        name="add_halves",
+    )(left, right)
+
+
 def close_kernel(
     recv_ref, mean_ref, inv_ref, scaled_ref, pick_ref, weight_ref, valid_ref, base_ref, out_ref
 ):
@@ -490,7 +508,7 @@
         ],
         out_specs=both(C, W),
         out_shape=jax.ShapeDtypeStruct((2, T, C, W), BF),
-        compiler_params=params(),
+        compiler_params=params(58),
         name="close_sums",
     )(recv, mean, inv, scaled, pick, weights, valid, base)
 
@@ -558,8 +576,7 @@
     sent_feat = jnp.broadcast_to(template_feat.reshape(1, 4, 16, W), (32, 4, 16, W))
     pool = exchange(sent_feat.reshape(128, 16, W))
     gain = norm_gain.astype(F32)
-    gain_wide = jnp.broadcast_to(gain[:, None, None], (C, 8, W))
-    pool, gain_wide = lax.optimization_barrier((pool, gain_wide))
+    gain_wide = jnp.broadcast_to(gain[:, None], (C, W))
     column_ids = lambda m, at: lax.dynamic_index_in_dim(m, at, axis=1, keepdims=False)
     row_ids = column_ids(block_map, row_block)
     member_ids = [column_ids(block_map, col ^ k) for k in range(4)]
@@ -626,8 +643,9 @@
             (factors, scaled, back, pair_sum, mixed, closing, opening, weights, own_valid, place)
         )
     )
-    my_inv = factors[:, 256:]
-    inv_all = in_order(core, my_inv, swap_cores(my_inv), 1)
+    inv_part = factors[:, None, 256:]
+    inv_part = in_order(member // 2, inv_part, from_member(inv_part, 2), 1)[:, :, None]
+    inv_all = in_order(core, inv_part, swap_cores(inv_part), 2).reshape(128, H, W)
     prod = exchange(run_product(factors)).reshape(T, C, H, W)
     left, right, inv_matrix = run_square(factors, inv_all)
     prod, left, right, inv_matrix = lax.optimization_barrier((prod, left, right, inv_matrix))
@@ -641,7 +659,7 @@
         )
     )
     kept, given, col_sums, row_sums = run_factor(core, left, right, grads, inv_matrix)
-    mean_half = (kept.astype(F32) + swap_cores(given).astype(F32)).astype(BF)
+    mean_half = run_add(kept, swap_cores(given))
     col_sums, row_sums, mean_half = lax.optimization_barrier((col_sums, row_sums, mean_half))
     recv = exchange(mean_half).reshape(T, 16, 2, H // 2, W)
 

time: 381 us -> 396 us (1.039)
  waiting for transfers between devices: 182 us -> 194 us
  starting transfers between devices: 48.6 us -> 52.9 us
    ppermute x11 -> x12, waiting for transfers between devices: 13.3 us -> 67.4 us  [from_member(): return lax.ppermute(value, 'col', [(i, i ^ k) for i in range(8)])]
    all_to_all x5, waiting for transfers between devices: 169 us -> 126 us  [exchange(): return lax.all_to_all(value, AXES, split_axis=0, concat_axis=0, tiled=True)]
    ppermute x11 -> x12, starting transfers between devices: 11.5 us -> 12.6 us  [from_member(): return lax.ppermute(value, 'col', [(i, i ^ k) for i in range(8)])]
  transfers between devices with their start and end apart: 16 -> 17, of which waited for: 13 -> 13; matrix products, arithmetic and copies ran while one was open for 6% -> 6% of each run, Pallas kernels for 12% -> 12%
where the time goes in v6:
time: 396 us; the launch traced here: 395 us
  waiting for transfers between devices  194 us (49%)
  Pallas kernels  97.5 us (25%)
  starting transfers between devices  52.9 us (13%)
  blocking collectives  17.7 us (4%)
  local copies, waits for them, and re-layouts  15.4 us (4%)
  matrix products  8.73 us (2%)
  other arithmetic  7.4 us (2%)
    all_to_all x5, waiting for transfers between devices, exchange(): return lax.all_to_all(value, AXES, split_axis=0, concat_axis=0, tiled=True)  126 us
    ppermute x12, waiting for transfers between devices, from_member(): return lax.ppermute(value, 'col', [(i, i ^ k) for i in range(8)])  67.4 us
    all_to_all x5, starting transfers between devices, exchange(): return lax.all_to_all(value, AXES, split_axis=0, concat_axis=0, tiled=True)  40.3 us
    pallas_call x1, Pallas kernels, run_gate(): pl.pallas_call(gate_kernel, grid=(T,), in_specs=[each_spec(C, H, W), each...  22.5 us
    all_to_all x1, blocking collectives, exchange(): return lax.all_to_all(value, AXES, split_axis=0, concat_axis=0, tiled=True)  17.7 us
    pallas_call x1, Pallas kernels, run_factor(): pl.pallas_call(factor_kernel, grid=(2,), in_specs=[pl.BlockSpec(memory_sp...  16.3 us
    pallas_call x1, Pallas kernels, run_back(): pl.pallas_call(back_kernel, grid=(T,), in_specs=[*TERM_SPECS, each_spec(H...  16.1 us
    ppermute x12, starting transfers between devices, from_member(): return lax.ppermute(value, 'col', [(i, i ^ k) for i in range(8)])  12.6 us
  transfers between devices with their start and end apart: 17, of which 13 were waited for; matrix products, arithmetic and copies ran while one was open for 6% of the time, Pallas kernels for 12%

profile of v6, /device:TPU:1, one launch (start us, length us, event | category | flops | bytes accessed | tf_op | source)
XLA Modules:
  0.0 394.6 jit_solution(15838176943906374042)
XLA Ops:
  0.7 1.6 broadcast_in_dim.35
  2.3 11.5 %all-to-all-start = ((bf16[128,16,128]{2,1,0:T(8,128)(2,1)}), bf16[128,16,128]{2,1,0:T(8,128)(2,1)S(1)}, u32[]{:S(2)}, u32[]{:S(2)}) async-start(bf16[128,16,128]{2,1,0:T(8,128)(2,1)} %bitcast.1), calls=%async_computation | async-start | bytes 1048576 | tf_op jit(solution)/shard_map/all_to_all | solution.py:525
  19.4 2.1 select_convert_fusion
  21.9 1.6 slice_bitcast_fusion
  23.5 3.8 all-to-all-done
  29.0 1.5 collective-permute-start.2
  35.1 11.3 %pair_norm.1 = (bf16[4,32,272,128]{3,2,1,0:T(8,128)(2,1)}, f32[4,64,128]{2,1,0:T(8,128)}) custom-call(bf16[4,64,64,128]{3,2,1,0:T(8,128)(2,1)} %pair_ref.3, f32[4,64,128]{2,1,0:T(8,128)} %fusion.5.left_ref, f32[4,64,128]{2,1,0:T(8,128)} %fusion.4.right_ref, bf16[4,256,256]{2,1,0:T(8,128)(2,1)} %constant.170.clone.lanes_ref, ...), custom_call_target="tpu_custom_call" | custom-call | tf_op jit(solution)/shard_map/pair_norm/pallas_call | solution.py:120
  46.4 6.3 %all-to-all-start.1 = ((bf16[128,272,128]{2,1,0:T(8,128)(2,1)}), bf16[128,272,128]{2,1,0:T(8,128)(2,1)}, u32[]{:S(2)}, u32[]{:S(2)}) async-start(bf16[128,272,128]{2,1,0:T(8,128)(2,1)} %bitcast.164), calls=%async_computation.1 | async-start | bytes 17825792 | tf_op jit(solution)/shard_map/all_to_all | solution.py:525
  55.2 16.1 %back_project.1 = (bf16[4,64,64,128]{3,2,1,0:T(8,128)(2,1)}, bf16[4,64,64,128]{3,2,1,0:T(8,128)(2,1)}, f32[64,64,128]{2,1,0:T(8,128)}) custom-call(bf16[4,64,64,128]{3,2,1,0:T(8,128)(2,1)} %pair_ref.3, f32[4,64,128]{2,1,0:T(8,128)} %fusion.5.left_ref, f32[4,64,128]{2,1,0:T(8,128)} %fusion.4.right_ref, bf16[4,256,256]{2,1,0:T(8,128)(2,1)} %constant.170.clone.lanes_ref, ...), custom_call_target="tpu_custom_call" | custom-call | flops 8589934592 | bytes 16777216 | tf_op jit(solution)/shard_map/back_project/pallas_call | solution.py:212
  71.2 86.9 %all-to-all-done.1.left_ref.right_ref = bf16[128,272,128]{2,1,0:T(8,128)(2,1)} async-done(((bf16[128,272,128]{2,1,0:T(8,128)(2,1)}), bf16[128,272,128]{2,1,0:T(8,128)(2,1)}, u32[]{:S(2)}, u32[]{:S(2)}) %all-to-all-start.1) | async-done | bytes 8912928 | tf_op jit(solution)/shard_map/all_to_all | solution.py:525
  158.1 8.4 %triangle_product.1 = bf16[128,128,128]{2,1,0:T(8,128)(2,1)} custom-call(bf16[128,272,128]{2,1,0:T(8,128)(2,1)} %all-to-all-done.1.left_ref.right_ref, bf16[128,272,128]{2,1,0:T(8,128)(2,1)} %all-to-all-done.1.left_ref.right_ref), custom_call_target="tpu_custom_call" | custom-call | tf_op jit(solution)/shard_map/triangle_product/pallas_call | solution.py:165
  166.5 8.8 %all-to-all-start.2 = ((bf16[128,128,128]{2,1,0:T(8,128)(2,1)}), bf16[128,128,128]{2,1,0:T(8,128)(2,1)}, u32[]{:S(2)}, u32[]{:S(2)}) async-start(bf16[128,128,128]{2,1,0:T(8,128)(2,1)} %triangle_product.1), calls=%async_computation.2 | async-start | bytes 8388608 | tf_op jit(solution)/shard_map/all_to_all | solution.py:525
  176.5 1.6 collective-permute-start.3
  178.1 54.5 %collective-permute-done.3 = bf16[128,1,16,128]{3,2,0,1:T(8,128)(2,1)S(1)} collective-permute-done((bf16[128,1,16,128]{3,2,0,1:T(8,128)(2,1)S(1)}, bf16[128,1,16,128]{3,2,0,1:T(8,128)(2,1)S(1)}, u32[]{:S(2)}, u32[]{:S(2)}) %collective-permute-start.3) | collective-permute-done | bytes 524320 | tf_op jit(solution)/shard_map/ppermute | solution.py:517
  234.8 2.3 collective-permute-done.4
  237.4 2.0 copy.62
  239.4 8.1 %to_matrices.1 = (bf16[2,1024,1024]{2,1,0:T(8,128)(2,1)}, bf16[2,1024,1024]{2,1,0:T(8,128)(2,1)}, bf16[1024,1024]{1,0:T(8,128)(2,1)}) custom-call(bf16[128,272,128]{2,1,0:T(8,128)(2,1)} %all-to-all-done.1.left_ref.right_ref, bf16[128,272,128]{2,1,0:T(8,128)(2,1)} %all-to-all-done.1.left_ref.right_ref, bf16[128,64,128]{2,1,0:T(8,128)(2,1)} %bitcast.165), custom_call_target="tpu_custom_call" | custom-call | flops 1048576 | bytes 20971520 | tf_op jit(solution)/shard_map/to_matrices/pallas_call | solution.py:365
  247.5 7.9 %product_grad.1 = bf16[4,64,64,128]{3,2,1,0:T(8,128)(2,1)} custom-call(bf16[4,64,64,128]{3,2,1,0:T(8,128)(2,1)} %bitcast.40.prod_ref, bf16[4,64,64,128]{3,2,1,0:T(8,128)(2,1)} %get-tuple-element.60.back_ref), custom_call_target="tpu_custom_call" | custom-call | flops 33554432 | bytes 12582912 | tf_op jit(solution)/shard_map/product_grad/pallas_call | solution.py:246
  255.5 9.9 %all-to-all-start.3 = ((bf16[128,128,128]{2,1,0:T(8,128)(2,1)}), bf16[128,128,128]{2,1,0:T(8,128)(2,1)}, u32[]{:S(2)}, u32[]{:S(2)}) async-start(bf16[128,128,128]{2,1,0:T(8,128)(2,1)} %bitcast.163), calls=%async_computation.3 | async-start | bytes 8388608 | tf_op jit(solution)/shard_map/all_to_all | solution.py:525
  266.1 22.5 %gate_and_embed.1 = (bf16[64,64,128]{2,1,0:T(8,128)(2,1)}, f32[4,64,128]{2,1,0:T(8,128)}, f32[4,64,128]{2,1,0:T(8,128)}, f32[4,64,128]{2,1,0:T(8,128)}, f32[64,128]{1,0:T(8,128)}, /*index=5*/f32[64,128]{1,0:T(8,128)}) custom-call(bf16[4,64,64,128]{3,2,1,0:T(8,128)(2,1)} %bitcast.40.prod_ref, bf16[4,64,64,128]{3,2,1,0:T(8,128)(2,1)} %get-tuple-element.61.scaled_ref, ...), custom_call_target="tpu_custom_call" | custom-call | flops 8589934592 | bytes 12582912 | tf_op jit(solution)/shard_map/gate_and_embed/pallas_call | solution.py:326
  288.6 29.5 %all-to-all-done.3.grad_ref = bf16[128,128,128]{2,1,0:T(8,128)(2,1)} async-done(((bf16[128,128,128]{2,1,0:T(8,128)(2,1)}), bf16[128,128,128]{2,1,0:T(8,128)(2,1)}, u32[]{:S(2)}, u32[]{:S(2)}) %all-to-all-start.3) | async-done | bytes 4194336 | tf_op jit(solution)/shard_map/all_to_all | solution.py:525
  318.2 16.3 %factor_grads.1 = (bf16[128,32,128]{2,1,0:T(8,128)(2,1)}, bf16[128,32,128]{2,1,0:T(8,128)(2,1)}, f32[2,2,8,1024]{3,2,1,0:T(8,128)}, f32[2,2,1024,128]{3,2,1,0:T(8,128)}) custom-call(s32[1]{0:T(128)} %bitcast.46.core_ref, bf16[2,1024,1024]{2,1,0:T(8,128)(2,1)} %get-tuple-element.71.left_ref, bf16[2,1024,1024]{2,1,0:T(8,128)(2,1)} %get-tuple-element.72.right_ref, ...), custom_call_target="tpu_custom_call" | custom-call | tf_op jit(solution)/shard_map/factor_grads/pallas_call | solution.py:429
  335.3 2.5 collective-permute-done.5.right_ref
  340.1 3.8 all-to-all-start.4
  349.6 1.3 collective-permute-start.8
  350.9 2.1 fusion.3.base_ref
  353.0 1.3 collective-permute-done.7
  354.3 2.5 collective-permute-done.8
  356.8 6.1 %all-to-all-done.4 = bf16[128,32,128]{2,1,0:T(8,128)(2,1)S(1)} async-done(((bf16[128,32,128]{2,1,0:T(8,128)(2,1)}), bf16[128,32,128]{2,1,0:T(8,128)(2,1)S(1)}, u32[]{:S(2)}, u32[]{:S(2)}) %all-to-all-start.4) | async-done | bytes 1048608 | tf_op jit(solution)/shard_map/all_to_all | solution.py:525
  363.9 5.8 %close_sums.1 = bf16[2,4,64,128]{3,2,1,0:T(8,128)(2,1)} custom-call(bf16[4,16,2,32,128]{4,3,2,1,0:T(8,128)(2,1)} %bitcast.166, f32[4,64,128]{2,1,0:T(8,128)} %get-tuple-element.95.mean_ref, f32[4,64,128]{2,1,0:T(8,128)} %get-tuple-element.51.inv_ref, bf16[4,64,64,128]{3,2,1,0:T(8,128)(2,1)} %get-tuple-element.61.scaled_ref, ...), custom_call_target="tpu_custom_call" | custom-call | tf_op jit(solution)/shard_map/close_sums/pallas_call | solution.py:502
  372.0 1.6 collective-permute-start.11
  376.2 17.7 %all_to_all.30 = bf16[128,16,128]{2,1,0:T(8,128)(2,1)S(1)} all-to-all(bf16[128,16,128]{2,1,0:T(8,128)(2,1)S(1)} %bitcast.168), channel_id=1, replica_groups=mesh['row'=16,'col'=8] {'row','col'}, dimensions={0} | all-to-all | bytes 1048576 | tf_op jit(solution)/shard_map/all_to_all | solution.py:525
  (115 shorter events, 34.0 us)
Async XLA Ops:
  0.6 20.8 %copy-start.7 = (s32[4,8]{1,0:T(4,128)S(1)}, s32[4,8]{1,0:T(4,128)}, u32[]{:S(2)}) copy-start(s32[4,8]{1,0:T(4,128)} %param.18) | copy-start | bytes 388
  0.6 20.8 %copy-start.10 = (s32[4,8]{1,0:T(4,128)S(1)}, s32[4,8]{1,0:T(4,128)}, u32[]{:S(2)}) copy-start(s32[4,8]{1,0:T(4,128)} %param.19) | copy-start | bytes 388
  0.7 21.2 %copy-start.11 = (s32[4,1024]{1,0:T(4,128)S(1)}, s32[4,1024]{1,0:T(4,128)}, u32[]{:S(2)}) copy-start(s32[4,1024]{1,0:T(4,128)} %param.20) | copy-start | bytes 49156
  2.3 25.0 %all-to-all-start = ((bf16[128,16,128]{2,1,0:T(8,128)(2,1)}), bf16[128,16,128]{2,1,0:T(8,128)(2,1)S(1)}, u32[]{:S(2)}, u32[]{:S(2)}) async-start(bf16[128,16,128]{2,1,0:T(8,128)(2,1)} %bitcast.1), calls=%async_computation | async-start | bytes 1048576 | tf_op jit(solution)/shard_map/all_to_all | solution.py:525
  21.5 12.9 %copy-start.12 = (bf16[64]{0:T(256)(128)(2,1)S(1)}, bf16[64]{0:T(256)(128)(2,1)}, u32[]{:S(2)}) copy-start(bf16[64]{0:T(256)(128)(2,1)} %param.23) | copy-start | bytes 388
  27.6 2.9 collective-permute-start
  28.8 2.8 collective-permute-start.1
  29.0 3.7 collective-permute-start.2
  46.4 6.4 %copy-start.4 = (bf16[64,64]{1,0:T(8,128)(2,1)S(1)}, bf16[64,64]{1,0:T(8,128)(2,1)}, u32[]{:S(2)}) copy-start(bf16[64,64]{1,0:T(8,128)(2,1)} %param.24) | copy-start | bytes 24580
  46.4 6.5 %copy-start.5 = (bf16[64,64]{1,0:T(8,128)(2,1)S(1)}, bf16[64,64]{1,0:T(8,128)(2,1)}, u32[]{:S(2)}) copy-start(bf16[64,64]{1,0:T(8,128)(2,1)} %param.25) | copy-start | bytes 24580
  46.4 6.6 %copy-start.6 = (bf16[64,64]{1,0:T(8,128)(2,1)S(1)}, bf16[64,64]{1,0:T(8,128)(2,1)}, u32[]{:S(2)}) copy-start(bf16[64,64]{1,0:T(8,128)(2,1)} %param.26) | copy-start | bytes 24580
  46.4 111.7 %all-to-all-start.1 = ((bf16[128,272,128]{2,1,0:T(8,128)(2,1)}), bf16[128,272,128]{2,1,0:T(8,128)(2,1)}, u32[]{:S(2)}, u32[]{:S(2)}) async-start(bf16[128,272,128]{2,1,0:T(8,128)(2,1)} %bitcast.164), calls=%async_computation.1 | async-start | bytes 17825792 | tf_op jit(solution)/shard_map/all_to_all | solution.py:525
  166.5 81.0 %all-to-all-start.2 = ((bf16[128,128,128]{2,1,0:T(8,128)(2,1)}), bf16[128,128,128]{2,1,0:T(8,128)(2,1)}, u32[]{:S(2)}, u32[]{:S(2)}) async-start(bf16[128,128,128]{2,1,0:T(8,128)(2,1)} %triangle_product.1), calls=%async_computation.2 | async-start | bytes 8388608 | tf_op jit(solution)/shard_map/all_to_all | solution.py:525
  176.5 56.2 %collective-permute-start.3 = (bf16[128,1,16,128]{3,2,0,1:T(8,128)(2,1)S(1)}, bf16[128,1,16,128]{3,2,0,1:T(8,128)(2,1)S(1)}, u32[]{:S(2)}, u32[]{:S(2)}) collective-permute-start(bf16[128,1,16,128]{3,2,0,1:T(8,128)(2,1)S(1)} %slice_bitcast_fusion.5), channel_id=1, source_target_pairs={{0,2},{1,3},{2,0},{3,1},{4,6},{5,7},{6,4},{7,5},{8,10},{9,11},{10,... | collective-permute-start | bytes 1572872 | tf_op jit(solution)/shard_map/ppermute | solution.py:517
  233.9 3.2 collective-permute-start.4
  255.5 9.9 %copy-start.3 = (bf16[4,256,128]{2,1,0:T(8,128)(2,1)S(1)}, bf16[4,256,128]{2,1,0:T(8,128)(2,1)}, u32[]{:S(2)}) copy-start(bf16[4,256,128]{2,1,0:T(8,128)(2,1)} %constant.171.clone) | copy-start | bytes 786436
  255.5 62.7 %all-to-all-start.3 = ((bf16[128,128,128]{2,1,0:T(8,128)(2,1)}), bf16[128,128,128]{2,1,0:T(8,128)(2,1)}, u32[]{:S(2)}, u32[]{:S(2)}) async-start(bf16[128,128,128]{2,1,0:T(8,128)(2,1)} %bitcast.163), calls=%async_computation.3 | async-start | bytes 8388608 | tf_op jit(solution)/shard_map/all_to_all | solution.py:525
  318.2 25.7 %copy-start.9 = (f32[64,128]{1,0:T(8,128)S(1)}, f32[64,128]{1,0:T(8,128)}, u32[]{:S(2)}) copy-start(f32[64,128]{1,0:T(8,128)} %get-tuple-element.84) | copy-start | bytes 98308
  334.4 3.3 collective-permute-start.5
  335.3 15.6 %copy-start.8 = (f32[2,4,128]{2,1,0:T(4,128)}, f32[2,4,128]{2,1,0:T(4,128)S(1)}, u32[]{:S(2)}) copy-start(f32[2,4,128]{2,1,0:T(4,128)S(1)} %pad_maximum_fusion.2) | copy-start | bytes 12292
  337.8 1.2 copy-start
  339.0 6.8 %copy-start.2 = (f32[2,2,1024,128]{3,2,1,0:T(8,128)S(1)}, f32[2,2,1024,128]{3,2,1,0:T(8,128)}, u32[]{:S(2)}) copy-start(f32[2,2,1024,128]{3,2,1,0:T(8,128)} %get-tuple-element.87) | copy-start | bytes 6291460
  340.1 22.8 %all-to-all-start.4 = ((bf16[128,32,128]{2,1,0:T(8,128)(2,1)}), bf16[128,32,128]{2,1,0:T(8,128)(2,1)S(1)}, u32[]{:S(2)}, u32[]{:S(2)}) async-start(bf16[128,32,128]{2,1,0:T(8,128)(2,1)} %add_halves.1), calls=%async_computation.4 | async-start | bytes 2097152 | tf_op jit(solution)/shard_map/all_to_all | solution.py:525
  347.7 5.3 %collective-permute-start.6 = (bf16[8,16,128]{2,1,0:T(8,128)(2,1)S(1)}, bf16[8,16,128]{2,1,0:T(8,128)(2,1)S(1)}, u32[]{:S(2)}, u32[]{:S(2)}) collective-permute-start(bf16[8,16,128]{2,1,0:T(8,128)(2,1)S(1)} %get-tuple-element.123), channel_id=1, source_target_pairs={{0,1},{1,0},{2,3},{3,2},{4,5},{5,4},{6,7},{7,6},{8,9},{9,8},{10,11... | collective-permute-start | bytes 98312 | tf_op jit(solution)/shard_map/ppermute | solution.py:517
  349.0 5.4 %collective-permute-start.7 = (bf16[8,16,128]{2,1,0:T(8,128)(2,1)S(1)}, bf16[8,16,128]{2,1,0:T(8,128)(2,1)S(1)}, u32[]{:S(2)}, u32[]{:S(2)}) collective-permute-start(bf16[8,16,128]{2,1,0:T(8,128)(2,1)S(1)} %get-tuple-element.122), channel_id=1, source_target_pairs={{0,2},{1,3},{2,0},{3,1},{4,6},{5,7},{6,4},{7,5},{8,10},{9,11},{10,... | collective-permute-start | bytes 98312 | tf_op jit(solution)/shard_map/ppermute | solution.py:517
  349.6 7.3 %collective-permute-start.8 = (bf16[8,16,128]{2,1,0:T(8,128)(2,1)S(1)}, bf16[8,16,128]{2,1,0:T(8,128)(2,1)S(1)}, u32[]{:S(2)}, u32[]{:S(2)}) collective-permute-start(bf16[8,16,128]{2,1,0:T(8,128)(2,1)S(1)} %get-tuple-element.121), channel_id=1, source_target_pairs={{0,3},{1,2},{2,1},{3,0},{4,7},{5,6},{6,5},{7,4},{8,11},{9,10},{10,... | collective-permute-start | bytes 98312 | tf_op jit(solution)/shard_map/ppermute | solution.py:517
  362.9 1.0 copy-start.1
  370.6 3.1 collective-permute-start.9
  371.9 2.8 collective-permute-start.10
  372.0 3.7 collective-permute-start.11

commit v7 on v6

--- a/solution.py
+++ b/solution.py
@@ -349,29 +349,37 @@
     )(prod, scaled, grad, pair_sum, inv, kg, ko, pick)
 
 
-def square_kernel(left_ref, right_ref, inv_ref, left, right, inv):
-    step = pl.program_id(0)
+def square_kernel(left_ref, right_ref, left, right):
     spread(left_ref, left.at[0])
     spread(right_ref, right.at[0])
 
-    @pl.when(step == 0)
-    def _():
-        spread(inv_ref, inv)
-
-
-def run_square(factors, inv):
+
+def run_square(factors):
     spec = lambda first: pl.BlockSpec((128, H, W), lambda s: (0, first + s, 0))
     out = pl.BlockSpec((1, N, N), lambda s: (s, 0, 0))
     return pl.pallas_call(
         square_kernel,
         grid=(2,),
-        in_specs=[spec(0), spec(2), pl.BlockSpec((128, H, W), lambda s: (0, 0, 0))],
-        out_specs=[out, out, pl.BlockSpec((N, N), lambda s: (0, 0))],
-        out_shape=[pltpu.HBM((2, N, N), BF), pltpu.HBM((2, N, N), BF), pltpu.HBM((N, N), BF)],
+        in_specs=[spec(0), spec(2)],
+        out_specs=[out, out],
+        out_shape=[pltpu.HBM((2, N, N), BF), pltpu.HBM((2, N, N), BF)],
         compiler_params=params(),
-        cost_estimate=pl.CostEstimate(flops=2**20, bytes_accessed=20 * 2**20, transcendentals=0),
+        cost_estimate=pl.CostEstimate(flops=2**20, bytes_accessed=16 * 2**20, transcendentals=0),
         name="to_matrices",
-    )(factors, factors, inv)
+    )(factors, factors)
+
+
+def run_matrix(blocks):
+    return pl.pallas_call(
+        spread,
+        grid=(1,),
+        in_specs=[whole_spec(128, H, W)],
+        out_specs=whole_spec(N, N),
+        out_shape=pltpu.HBM((N, N), BF),
+        compiler_params=params(),
+        cost_estimate=pl.CostEstimate(flops=2**20, bytes_accessed=4 * 2**20, transcendentals=0),
+        name="to_matrix",
+    )(blocks)
 
 
 def factor_kernel(
@@ -643,19 +651,33 @@
             (factors, scaled, back, pair_sum, mixed, closing, opening, weights, own_valid, place)
         )
     )
-    inv_part = factors[:, None, 256:]
-    inv_part = in_order(member // 2, inv_part, from_member(inv_part, 2), 1)[:, :, None]
+    first, rest = factors[:64, None, 256:], factors[64:, None, 256:]
+    first_other = from_member(first, 2)
+    product, first_other = lax.optimization_barrier((run_product(factors), first_other))
+    prod = exchange(product).reshape(T, C, H, W)
+    left, right = run_square(factors)
+    prod, left, right, first, rest = lax.optimization_barrier((prod, left, right, first, rest))
+    rest_other = from_member(rest, 2)
+    grad_prod = run_grad(prod, back)
+    grad_prod, first, rest, rest_other = lax.optimization_barrier(
+        (grad_prod, first, rest, rest_other)
+    )
+    grads = exchange(grad_prod.reshape(128, 2 * H, W))
+    inv_part = jnp.concatenate(
+        [
+            in_order(member // 2, first, first_other, 1),
+            in_order(member // 2, rest, rest_other, 1),
+        ],
+        axis=0,
+    )[:, :, None]
     inv_all = in_order(core, inv_part, swap_cores(inv_part), 2).reshape(128, H, W)
-    prod = exchange(run_product(factors)).reshape(T, C, H, W)
-    left, right, inv_matrix = run_square(factors, inv_all)
-    prod, left, right, inv_matrix = lax.optimization_barrier((prod, left, right, inv_matrix))
-    grads = exchange(run_grad(prod, back).reshape(128, 2 * H, W))
+    inv_matrix = run_matrix(inv_all)
     embedding, gate_mean, gate_rows, gate_cols, out_rows, out_cols = run_gate(
         prod, scaled, embed_grad, pair_sum, inv, kg, ko, sums_pick
     )
-    grads, embedding, gate_mean, gate_rows, gate_cols, out_rows, out_cols = (
+    grads, embedding, gate_mean, gate_rows, gate_cols, out_rows, out_cols, inv_matrix = (
         lax.optimization_barrier(
-            (grads, embedding, gate_mean, gate_rows, gate_cols, out_rows, out_cols)
+            (grads, embedding, gate_mean, gate_rows, gate_cols, out_rows, out_cols, inv_matrix)
         )
     )
     kept, given, col_sums, row_sums = run_factor(core, left, right, grads, inv_matrix)

time: 396 us -> 375 us (0.947)
  waiting for transfers between devices: 194 us -> 175 us
    ppermute x12 -> x13, waiting for transfers between devices: 67.4 us -> 10.6 us  [from_member(): return lax.ppermute(value, 'col', [(i, i ^ k) for i in range(8)])]
    all_to_all x5, waiting for transfers between devices: 126 us -> 165 us  [exchange(): return lax.all_to_all(value, AXES, split_axis=0, concat_axis=0, tiled=True)]
    pallas_call x1 -> x2, Pallas kernels: 8.09 us -> 9.77 us  [the longest x1 6.39 us: run_square(): pl.pallas_call(square_kernel, grid=(2,), in_specs=[spec(0), spec(2)], out...]
    ppermute x12 -> x13, starting transfers between devices: 12.6 us -> 11.5 us  [from_member(): return lax.ppermute(value, 'col', [(i, i ^ k) for i in range(8)])]
  transfers between devices with their start and end apart: 17 -> 18, of which waited for: 13 -> 12; matrix products, arithmetic and copies ran while one was open for 6% -> 6% of each run, Pallas kernels for 12% -> 17%
where the time goes in v7:
time: 375 us; the launch traced here: 374 us
  waiting for transfers between devices  175 us (47%)
  Pallas kernels  99.2 us (26%)
  starting transfers between devices  49.2 us (13%)
  blocking collectives  17.7 us (5%)
  local copies, waits for them, and re-layouts  15.4 us (4%)
  matrix products  8.74 us (2%)
  other arithmetic  7.3 us (2%)
    all_to_all x5, waiting for transfers between devices, exchange(): return lax.all_to_all(value, AXES, split_axis=0, concat_axis=0, tiled=True)  165 us
    all_to_all x5, starting transfers between devices, exchange(): return lax.all_to_all(value, AXES, split_axis=0, concat_axis=0, tiled=True)  37.7 us
    pallas_call x1, Pallas kernels, run_gate(): pl.pallas_call(gate_kernel, grid=(T,), in_specs=[each_spec(C, H, W), each...  22.5 us
    all_to_all x1, blocking collectives, exchange(): return lax.all_to_all(value, AXES, split_axis=0, concat_axis=0, tiled=True)  17.7 us
    pallas_call x1, Pallas kernels, run_factor(): pl.pallas_call(factor_kernel, grid=(2,), in_specs=[pl.BlockSpec(memory_sp...  16.3 us
    pallas_call x1, Pallas kernels, run_back(): pl.pallas_call(back_kernel, grid=(T,), in_specs=[*TERM_SPECS, each_spec(H...  16.1 us
    ppermute x13, starting transfers between devices, from_member(): return lax.ppermute(value, 'col', [(i, i ^ k) for i in range(8)])  11.5 us
    pallas_call x1, Pallas kernels, run_norm(): pl.pallas_call(norm_kernel, grid=(T,), in_specs=[*TERM_SPECS, whole_spec(...  11.3 us
  transfers between devices with their start and end apart: 18, of which 12 were waited for; matrix products, arithmetic and copies ran while one was open for 6% of the time, Pallas kernels for 17%

profile of v7, /device:TPU:1, one launch (start us, length us, event | category | flops | bytes accessed | tf_op | source)
XLA Modules:
  0.0 374.0 jit_solution(11197460087981676519)
XLA Ops:
  0.7 1.6 broadcast_in_dim.37
  2.3 11.5 %all-to-all-start = ((bf16[128,16,128]{2,1,0:T(8,128)(2,1)}), bf16[128,16,128]{2,1,0:T(8,128)(2,1)S(1)}, u32[]{:S(2)}, u32[]{:S(2)}) async-start(bf16[128,16,128]{2,1,0:T(8,128)(2,1)} %bitcast.1), calls=%async_computation | async-start | bytes 1048576 | tf_op jit(solution)/shard_map/all_to_all | solution.py:533
  19.4 2.1 select_convert_fusion
  21.9 1.6 slice_bitcast_fusion
  23.5 3.8 %all-to-all-done = bf16[128,16,128]{2,1,0:T(8,128)(2,1)S(1)} async-done(((bf16[128,16,128]{2,1,0:T(8,128)(2,1)}), bf16[128,16,128]{2,1,0:T(8,128)(2,1)S(1)}, u32[]{:S(2)}, u32[]{:S(2)}) %all-to-all-start) | async-done | bytes 524320 | tf_op jit(solution)/shard_map/all_to_all | solution.py:533
  29.0 1.5 collective-permute-start.2
  35.1 11.3 %pair_norm.1 = (bf16[4,32,272,128]{3,2,1,0:T(8,128)(2,1)}, f32[4,64,128]{2,1,0:T(8,128)}) custom-call(bf16[4,64,64,128]{3,2,1,0:T(8,128)(2,1)} %pair_ref.3, f32[4,64,128]{2,1,0:T(8,128)} %fusion.5.left_ref, f32[4,64,128]{2,1,0:T(8,128)} %fusion.4.right_ref, bf16[4,256,256]{2,1,0:T(8,128)(2,1)} %constant.172.clone.lanes_ref, ...), custom_call_target="tpu_custom_call" | custom-call | tf_op jit(solution)/shard_map/pair_norm/pallas_call | solution.py:120
  46.4 6.3 %all-to-all-start.1 = ((bf16[128,272,128]{2,1,0:T(8,128)(2,1)}), bf16[128,272,128]{2,1,0:T(8,128)(2,1)}, u32[]{:S(2)}, u32[]{:S(2)}) async-start(bf16[128,272,128]{2,1,0:T(8,128)(2,1)} %bitcast.162), calls=%async_computation.1 | async-start | bytes 17825792 | tf_op jit(solution)/shard_map/all_to_all | solution.py:533
  55.1 16.1 %back_project.1 = (bf16[4,64,64,128]{3,2,1,0:T(8,128)(2,1)}, bf16[4,64,64,128]{3,2,1,0:T(8,128)(2,1)}, f32[64,64,128]{2,1,0:T(8,128)}) custom-call(bf16[4,64,64,128]{3,2,1,0:T(8,128)(2,1)} %pair_ref.3, f32[4,64,128]{2,1,0:T(8,128)} %fusion.5.left_ref, f32[4,64,128]{2,1,0:T(8,128)} %fusion.4.right_ref, bf16[4,256,256]{2,1,0:T(8,128)(2,1)} %constant.172.clone.lanes_ref, ...), custom_call_target="tpu_custom_call" | custom-call | flops 8589934592 | bytes 16777216 | tf_op jit(solution)/shard_map/back_project/pallas_call | solution.py:212
  71.2 86.9 %all-to-all-done.1.left_ref.right_ref = bf16[128,272,128]{2,1,0:T(8,128)(2,1)} async-done(((bf16[128,272,128]{2,1,0:T(8,128)(2,1)}), bf16[128,272,128]{2,1,0:T(8,128)(2,1)}, u32[]{:S(2)}, u32[]{:S(2)}) %all-to-all-start.1) | async-done | bytes 8912928 | tf_op jit(solution)/shard_map/all_to_all | solution.py:533
  159.3 8.4 %triangle_product.1 = bf16[128,128,128]{2,1,0:T(8,128)(2,1)} custom-call(bf16[128,272,128]{2,1,0:T(8,128)(2,1)} %all-to-all-done.1.left_ref.right_ref, bf16[128,272,128]{2,1,0:T(8,128)(2,1)} %all-to-all-done.1.left_ref.right_ref), custom_call_target="tpu_custom_call" | custom-call | tf_op jit(solution)/shard_map/triangle_product/pallas_call | solution.py:165
  167.7 10.2 %all-to-all-start.2 = ((bf16[128,128,128]{2,1,0:T(8,128)(2,1)}), bf16[128,128,128]{2,1,0:T(8,128)(2,1)}, u32[]{:S(2)}, u32[]{:S(2)}) async-start(bf16[128,128,128]{2,1,0:T(8,128)(2,1)} %triangle_product.1), calls=%async_computation.2 | async-start | bytes 8388608 | tf_op jit(solution)/shard_map/all_to_all | solution.py:533
  178.0 6.4 %to_matrices.1 = (bf16[2,1024,1024]{2,1,0:T(8,128)(2,1)}, bf16[2,1024,1024]{2,1,0:T(8,128)(2,1)}) custom-call(bf16[128,272,128]{2,1,0:T(8,128)(2,1)} %all-to-all-done.1.left_ref.right_ref, bf16[128,272,128]{2,1,0:T(8,128)(2,1)} %all-to-all-done.1.left_ref.right_ref), custom_call_target="tpu_custom_call" | custom-call | flops 1048576 | bytes 16777216 | tf_op jit(solution)/shard_map/to_matrices/pallas_call | solution.py:360
  184.4 46.4 %all-to-all-done.2 = bf16[128,128,128]{2,1,0:T(8,128)(2,1)} async-done(((bf16[128,128,128]{2,1,0:T(8,128)(2,1)}), bf16[128,128,128]{2,1,0:T(8,128)(2,1)}, u32[]{:S(2)}, u32[]{:S(2)}) %all-to-all-start.2) | async-done | bytes 4194336 | tf_op jit(solution)/shard_map/all_to_all | solution.py:533
  230.8 7.9 %product_grad.1 = bf16[4,64,64,128]{3,2,1,0:T(8,128)(2,1)} custom-call(bf16[4,64,64,128]{3,2,1,0:T(8,128)(2,1)} %bitcast.41.prod_ref, bf16[4,64,64,128]{3,2,1,0:T(8,128)(2,1)} %get-tuple-element.67.back_ref), custom_call_target="tpu_custom_call" | custom-call | flops 33554432 | bytes 12582912 | tf_op jit(solution)/shard_map/product_grad/pallas_call | solution.py:246
  238.7 5.9 %all-to-all-start.3 = ((bf16[128,128,128]{2,1,0:T(8,128)(2,1)}), bf16[128,128,128]{2,1,0:T(8,128)(2,1)}, u32[]{:S(2)}, u32[]{:S(2)}) async-start(bf16[128,128,128]{2,1,0:T(8,128)(2,1)} %bitcast.161), calls=%async_computation.3 | async-start | bytes 8388608 | tf_op jit(solution)/shard_map/all_to_all | solution.py:533
  244.8 1.4 collective-permute-start.5
  246.1 1.7 broadcast_select_fusion.6.pick_ref
  247.8 22.5 %gate_and_embed.1 = (bf16[64,64,128]{2,1,0:T(8,128)(2,1)}, f32[4,64,128]{2,1,0:T(8,128)}, f32[4,64,128]{2,1,0:T(8,128)}, f32[4,64,128]{2,1,0:T(8,128)}, f32[64,128]{1,0:T(8,128)}, /*index=5*/f32[64,128]{1,0:T(8,128)}) custom-call(bf16[4,64,64,128]{3,2,1,0:T(8,128)(2,1)} %bitcast.41.prod_ref, bf16[4,64,64,128]{3,2,1,0:T(8,128)(2,1)} %get-tuple-element.71.scaled_ref, ...), custom_call_target="tpu_custom_call" | custom-call | flops 8589934592 | bytes 12582912 | tf_op jit(solution)/shard_map/gate_and_embed/pallas_call | solution.py:326
  270.7 2.1 copy.62
  272.8 3.4 to_matrix.1.inv_ref
  276.2 21.3 %all-to-all-done.3.grad_ref = bf16[128,128,128]{2,1,0:T(8,128)(2,1)} async-done(((bf16[128,128,128]{2,1,0:T(8,128)(2,1)}), bf16[128,128,128]{2,1,0:T(8,128)(2,1)}, u32[]{:S(2)}, u32[]{:S(2)}) %all-to-all-start.3) | async-done | bytes 4194336 | tf_op jit(solution)/shard_map/all_to_all | solution.py:533
  297.5 16.3 %factor_grads.1 = (bf16[128,32,128]{2,1,0:T(8,128)(2,1)}, bf16[128,32,128]{2,1,0:T(8,128)(2,1)}, f32[2,2,8,1024]{3,2,1,0:T(8,128)}, f32[2,2,1024,128]{3,2,1,0:T(8,128)}) custom-call(s32[1]{0:T(128)} %bitcast.47.core_ref, bf16[2,1024,1024]{2,1,0:T(8,128)(2,1)} %get-tuple-element.85.left_ref, bf16[2,1024,1024]{2,1,0:T(8,128)(2,1)} %get-tuple-element.86.right_ref, ...), custom_call_target="tpu_custom_call" | custom-call | tf_op jit(solution)/shard_map/factor_grads/pallas_call | solution.py:437
  314.7 2.5 collective-permute-done.6.right_ref
  319.5 3.8 %all-to-all-start.4 = ((bf16[128,32,128]{2,1,0:T(8,128)(2,1)}), bf16[128,32,128]{2,1,0:T(8,128)(2,1)S(1)}, u32[]{:S(2)}, u32[]{:S(2)}) async-start(bf16[128,32,128]{2,1,0:T(8,128)(2,1)} %add_halves.1), calls=%async_computation.4 | async-start | bytes 2097152 | tf_op jit(solution)/shard_map/all_to_all | solution.py:533
  327.1 1.5 collective-permute-start.7
  330.3 2.1 fusion.3.base_ref
  333.7 2.5 collective-permute-done.9
  336.2 6.1 %all-to-all-done.4 = bf16[128,32,128]{2,1,0:T(8,128)(2,1)S(1)} async-done(((bf16[128,32,128]{2,1,0:T(8,128)(2,1)}), bf16[128,32,128]{2,1,0:T(8,128)(2,1)S(1)}, u32[]{:S(2)}, u32[]{:S(2)}) %all-to-all-start.4) | async-done | bytes 1048608 | tf_op jit(solution)/shard_map/all_to_all | solution.py:533
  343.3 5.8 %close_sums.1 = bf16[2,4,64,128]{3,2,1,0:T(8,128)(2,1)} custom-call(bf16[4,16,2,32,128]{4,3,2,1,0:T(8,128)(2,1)} %bitcast.164, f32[4,64,128]{2,1,0:T(8,128)} %get-tuple-element.109.mean_ref, f32[4,64,128]{2,1,0:T(8,128)} %get-tuple-element.58.inv_ref, bf16[4,64,64,128]{3,2,1,0:T(8,128)(2,1)} %get-tuple-element.71.scaled_ref, ...), custom_call_target="tpu_custom_call" | custom-call | tf_op jit(solution)/shard_map/close_sums/pallas_call | solution.py:510
  351.4 1.6 collective-permute-start.12
  355.6 17.7 %all_to_all.30 = bf16[128,16,128]{2,1,0:T(8,128)(2,1)S(1)} all-to-all(bf16[128,16,128]{2,1,0:T(8,128)(2,1)S(1)} %bitcast.166), channel_id=1, replica_groups=mesh['row'=16,'col'=8] {'row','col'}, dimensions={0} | all-to-all | bytes 1048576 | tf_op jit(solution)/shard_map/all_to_all | solution.py:533
  (117 shorter events, 32.5 us)
Async XLA Ops:
  0.6 20.8 %copy-start.6 = (s32[4,8]{1,0:T(4,128)S(1)}, s32[4,8]{1,0:T(4,128)}, u32[]{:S(2)}) copy-start(s32[4,8]{1,0:T(4,128)} %param.18) | copy-start | bytes 388
  0.6 20.8 %copy-start.9 = (s32[4,8]{1,0:T(4,128)S(1)}, s32[4,8]{1,0:T(4,128)}, u32[]{:S(2)}) copy-start(s32[4,8]{1,0:T(4,128)} %param.19) | copy-start | bytes 388
  0.7 21.2 %copy-start.10 = (s32[4,1024]{1,0:T(4,128)S(1)}, s32[4,1024]{1,0:T(4,128)}, u32[]{:S(2)}) copy-start(s32[4,1024]{1,0:T(4,128)} %param.20) | copy-start | bytes 49156
  2.3 25.0 %all-to-all-start = ((bf16[128,16,128]{2,1,0:T(8,128)(2,1)}), bf16[128,16,128]{2,1,0:T(8,128)(2,1)S(1)}, u32[]{:S(2)}, u32[]{:S(2)}) async-start(bf16[128,16,128]{2,1,0:T(8,128)(2,1)} %bitcast.1), calls=%async_computation | async-start | bytes 1048576 | tf_op jit(solution)/shard_map/all_to_all | solution.py:533
  21.5 12.9 %copy-start.11 = (bf16[64]{0:T(256)(128)(2,1)S(1)}, bf16[64]{0:T(256)(128)(2,1)}, u32[]{:S(2)}) copy-start(bf16[64]{0:T(256)(128)(2,1)} %param.23) | copy-start | bytes 388
  27.6 2.9 collective-permute-start
  28.8 2.8 collective-permute-start.1
  29.0 3.7 collective-permute-start.2
  46.4 6.4 %copy-start.3 = (bf16[64,64]{1,0:T(8,128)(2,1)S(1)}, bf16[64,64]{1,0:T(8,128)(2,1)}, u32[]{:S(2)}) copy-start(bf16[64,64]{1,0:T(8,128)(2,1)} %param.24) | copy-start | bytes 24580
  46.4 6.5 %copy-start.4 = (bf16[64,64]{1,0:T(8,128)(2,1)S(1)}, bf16[64,64]{1,0:T(8,128)(2,1)}, u32[]{:S(2)}) copy-start(bf16[64,64]{1,0:T(8,128)(2,1)} %param.25) | copy-start | bytes 24580
  46.4 6.5 %copy-start.5 = (bf16[64,64]{1,0:T(8,128)(2,1)S(1)}, bf16[64,64]{1,0:T(8,128)(2,1)}, u32[]{:S(2)}) copy-start(bf16[64,64]{1,0:T(8,128)(2,1)} %param.26) | copy-start | bytes 24580
  46.4 111.7 %all-to-all-start.1 = ((bf16[128,272,128]{2,1,0:T(8,128)(2,1)}), bf16[128,272,128]{2,1,0:T(8,128)(2,1)}, u32[]{:S(2)}, u32[]{:S(2)}) async-start(bf16[128,272,128]{2,1,0:T(8,128)(2,1)} %bitcast.162), calls=%async_computation.1 | async-start | bytes 17825792 | tf_op jit(solution)/shard_map/all_to_all | solution.py:533
  159.2 8.5 %collective-permute-start.3 = (bf16[64,1,16,128]{3,2,0,1:T(8,128)(2,1)S(1)}, bf16[64,1,16,128]{3,2,0,1:T(8,128)(2,1)S(1)}, u32[]{:S(2)}, u32[]{:S(2)}) collective-permute-start(bf16[64,1,16,128]{3,2,0,1:T(8,128)(2,1)S(1)} %get-tuple-element.79), channel_id=1, source_target_pairs={{0,2},{1,3},{2,0},{3,1},{4,6},{5,7},{6,4},{7,5},{8,10},{9,11},{10,... | collective-permute-start | bytes 786440 | tf_op jit(solution)/shard_map/ppermute | solution.py:525
  167.7 63.0 %all-to-all-start.2 = ((bf16[128,128,128]{2,1,0:T(8,128)(2,1)}), bf16[128,128,128]{2,1,0:T(8,128)(2,1)}, u32[]{:S(2)}, u32[]{:S(2)}) async-start(bf16[128,128,128]{2,1,0:T(8,128)(2,1)} %triangle_product.1), calls=%async_computation.2 | async-start | bytes 8388608 | tf_op jit(solution)/shard_map/all_to_all | solution.py:533
  230.8 7.9 %collective-permute-start.4 = (bf16[64,1,16,128]{3,2,0,1:T(8,128)(2,1)S(1)}, bf16[64,1,16,128]{3,2,0,1:T(8,128)(2,1)S(1)}, u32[]{:S(2)}, u32[]{:S(2)}) collective-permute-start(bf16[64,1,16,128]{3,2,0,1:T(8,128)(2,1)S(1)} %get-tuple-element.81), channel_id=1, source_target_pairs={{0,2},{1,3},{2,0},{3,1},{4,6},{5,7},{6,4},{7,5},{8,10},{9,11},{10,... | collective-permute-start | bytes 786440 | tf_op jit(solution)/shard_map/ppermute | solution.py:525
  238.7 58.8 %all-to-all-start.3 = ((bf16[128,128,128]{2,1,0:T(8,128)(2,1)}), bf16[128,128,128]{2,1,0:T(8,128)(2,1)}, u32[]{:S(2)}, u32[]{:S(2)}) async-start(bf16[128,128,128]{2,1,0:T(8,128)(2,1)} %bitcast.161), calls=%async_computation.3 | async-start | bytes 8388608 | tf_op jit(solution)/shard_map/all_to_all | solution.py:533
  244.8 25.6 %collective-permute-start.5 = (bf16[128,2,1,16,128]{4,3,0,1,2:T(8,128)(2,1)S(1)}, bf16[128,2,1,16,128]{4,3,0,1,2:T(8,128)(2,1)S(1)}, u32[]{:S(2)}, u32[]{:S(2)}) collective-permute-start(bf16[128,2,1,16,128]{4,3,0,1,2:T(8,128)(2,1)S(1)} %maximum_bitcast_fusion), channel_id=1, source_target_pairs={{0,1},{1,0},{2,3},{3,2},{4,5},{5,4},{6,7},{7,6},{8,9},{9,8},{10,11... | collective-permute-start | bytes 3145736 | tf_op jit(solution)/shard_map/ppermute | solution.py:525
  297.5 25.8 %copy-start.8 = (f32[64,128]{1,0:T(8,128)S(1)}, f32[64,128]{1,0:T(8,128)}, u32[]{:S(2)}) copy-start(f32[64,128]{1,0:T(8,128)} %get-tuple-element.98) | copy-start | bytes 98308
  313.8 3.3 collective-permute-start.6
  314.7 15.6 %copy-start.7 = (f32[2,4,128]{2,1,0:T(4,128)}, f32[2,4,128]{2,1,0:T(4,128)S(1)}, u32[]{:S(2)}) copy-start(f32[2,4,128]{2,1,0:T(4,128)S(1)} %pad_maximum_fusion.2) | copy-start | bytes 12292
  317.2 1.2 copy-start
  318.4 6.8 %copy-start.2 = (f32[2,2,1024,128]{3,2,1,0:T(8,128)S(1)}, f32[2,2,1024,128]{3,2,1,0:T(8,128)}, u32[]{:S(2)}) copy-start(f32[2,2,1024,128]{3,2,1,0:T(8,128)} %get-tuple-element.101) | copy-start | bytes 6291460
  319.5 22.8 %all-to-all-start.4 = ((bf16[128,32,128]{2,1,0:T(8,128)(2,1)}), bf16[128,32,128]{2,1,0:T(8,128)(2,1)S(1)}, u32[]{:S(2)}, u32[]{:S(2)}) async-start(bf16[128,32,128]{2,1,0:T(8,128)(2,1)} %add_halves.1), calls=%async_computation.4 | async-start | bytes 2097152 | tf_op jit(solution)/shard_map/all_to_all | solution.py:533
  327.1 5.3 %collective-permute-start.7 = (bf16[8,16,128]{2,1,0:T(8,128)(2,1)S(1)}, bf16[8,16,128]{2,1,0:T(8,128)(2,1)S(1)}, u32[]{:S(2)}, u32[]{:S(2)}) collective-permute-start(bf16[8,16,128]{2,1,0:T(8,128)(2,1)S(1)} %get-tuple-element.141), channel_id=1, source_target_pairs={{0,1},{1,0},{2,3},{3,2},{4,5},{5,4},{6,7},{7,6},{8,9},{9,8},{10,11... | collective-permute-start | bytes 98312 | tf_op jit(solution)/shard_map/ppermute | solution.py:525
  328.6 5.2 %collective-permute-start.8 = (bf16[8,16,128]{2,1,0:T(8,128)(2,1)S(1)}, bf16[8,16,128]{2,1,0:T(8,128)(2,1)S(1)}, u32[]{:S(2)}, u32[]{:S(2)}) collective-permute-start(bf16[8,16,128]{2,1,0:T(8,128)(2,1)S(1)} %get-tuple-element.140), channel_id=1, source_target_pairs={{0,2},{1,3},{2,0},{3,1},{4,6},{5,7},{6,4},{7,5},{8,10},{9,11},{10,... | collective-permute-start | bytes 98312 | tf_op jit(solution)/shard_map/ppermute | solution.py:525
  329.0 7.3 %collective-permute-start.9 = (bf16[8,16,128]{2,1,0:T(8,128)(2,1)S(1)}, bf16[8,16,128]{2,1,0:T(8,128)(2,1)S(1)}, u32[]{:S(2)}, u32[]{:S(2)}) collective-permute-start(bf16[8,16,128]{2,1,0:T(8,128)(2,1)S(1)} %get-tuple-element.139), channel_id=1, source_target_pairs={{0,3},{1,2},{2,1},{3,0},{4,7},{5,6},{6,5},{7,4},{8,11},{9,10},{10,... | collective-permute-start | bytes 98312 | tf_op jit(solution)/shard_map/ppermute | solution.py:525
  342.3 1.0 copy-start.1
  350.0 3.1 collective-permute-start.10
  351.3 2.8 collective-permute-start.11
  351.4 3.7 collective-permute-start.12

commit v8 on v7

--- a/solution.py
+++ b/solution.py
@@ -58,13 +58,16 @@
     return (lane % 8 == lax.broadcasted_iota(jnp.int32, (8, width), 0)).astype(F32)
 
 
-def spread_terms(left_ref, right_ref, gain_ref, right, gain):
+def spread_terms(feats_row_ref, feats_col_ref, embeds_ref, valid_ref, gain_ref, right, gain, both):
+    for side, feats in enumerate((feats_row_ref, feats_col_ref)):
+        terms = jnp.dot(embeds_ref[side], feats[0], preferred_element_type=F32)
+        both[side] = terms * valid_ref[side, 0]
     mask = row_mask(W)
     rows = []
     for c in range(C):
-        right[c] = jnp.broadcast_to(right_ref[0, c : c + 1, :], (8, W))
+        right[c] = jnp.broadcast_to(both[1, c : c + 1, :], (8, W))
         gain[c] = jnp.broadcast_to(gain_ref[c : c + 1, :], (8, W))
-        rows.append(jnp.broadcast_to(left_ref[0, c : c + 1, :], (8, W)) * mask)
+        rows.append(jnp.broadcast_to(both[0, c : c + 1, :], (8, W)) * mask)
     value = jnp.concatenate(rows, axis=0)
     high = value.astype(BF)
     return jnp.concatenate([high, (value - high.astype(F32)).astype(BF)], axis=1)
@@ -77,10 +80,12 @@
 
 
 def norm_kernel(
-    pair_ref, left_ref, right_ref, lanes_ref, gain_ref, kl_ref, kr_ref, pay_ref, inv_ref,
-    right, gain, terms, wide,
+    pair_ref, feats_row_ref, feats_col_ref, embeds_ref, valid_ref, lanes_ref, gain_ref,
+    kl_ref, kr_ref, pay_ref, inv_ref, right, gain, both, terms, wide,
 ):
-    left = spread_terms(left_ref, right_ref, gain_ref, right, gain)
+    left = spread_terms(
+        feats_row_ref, feats_col_ref, embeds_ref, valid_ref, gain_ref, right, gain, both
+    )
     for g in range(4):
         terms[g] = jnp.dot(left, lanes_ref[g], preferred_element_type=F32)
     for g in range(4):
@@ -93,11 +98,11 @@
             inverse = lax.rsqrt(mean_channels(shifted * shifted) + EPS)
             scaleds.append(shifted * inverse * gain[...])
             invs.append(inverse[0])
-        both = jnp.concatenate(invs, axis=0)
-        inv_ref[0, g * 16 : g * 16 + 16, :] = both
+        inverses = jnp.concatenate(invs, axis=0)
+        inv_ref[0, g * 16 : g * 16 + 16, :] = inverses
         wide[:, g * 256 : g * 256 + 256] = stack_rows(*scaleds).astype(BF)
         for q in range(g, C // 2, 4):
-            pay_ref[0, q, 256:272, :] = both.astype(BF)
+            pay_ref[0, q, 256:272, :] = inverses.astype(BF)
     for k, weight in enumerate((kl_ref, kr_ref)):
         outs = jnp.dot(weight[...], wide[...], preferred_element_type=F32)
         for g in range(4):
@@ -109,14 +114,16 @@
 
 TERM_SPECS = [
     each_spec(C, H, W),
+    pl.BlockSpec((1, C, W), lambda t: (t + T, 0, 0)),
     each_spec(C, W),
-    each_spec(C, W),
+    whole_spec(2, C, C),
+    pl.BlockSpec((2, 1, 1, W), lambda t: (0, t, 0, 0)),
     whole_spec(4, 2 * W, 2 * W),
     whole_spec(C, W),
 ]
 
 
-def run_norm(pair, left, right, lanes, gain, kl, kr):
+def run_norm(pair, feats, embeds, valid, lanes, gain, kl, kr):
     return pl.pallas_call(
         norm_kernel,
         grid=(T,),
@@ -129,12 +136,13 @@
         scratch_shapes=[
             pltpu.VMEM((C, 8, W), F32),
             pltpu.VMEM((C, 8, W), F32),
+            pltpu.VMEM((2, C, W), F32),
             pltpu.VMEM((4, K8, 2 * W), F32),
             pltpu.VMEM((K8, N), BF),
         ],
         compiler_params=params(),
         name="pair_norm",
-    )(pair, left, right, lanes, gain, kl, kr)
+    )(pair, feats, feats, embeds, valid, lanes, gain, kl, kr)
 
 
 def spread(blocks_ref, full_ref):
@@ -174,11 +182,13 @@
 
 
 def back_kernel(
-    pair_ref, left_ref, right_ref, lanes_ref, gain_ref, inv_ref, grad_ref, kg_ref, kb_ref,
-    scaled_ref, out_ref, sum_ref, right, gain,
+    pair_ref, feats_row_ref, feats_col_ref, embeds_ref, valid_ref, lanes_ref, gain_ref,
+    inv_ref, grad_ref, kg_ref, kb_ref, scaled_ref, out_ref, sum_ref, right, gain, both,
 ):
     step = pl.program_id(0)
-    left = spread_terms(left_ref, right_ref, gain_ref, right, gain)
+    left = spread_terms(
+        feats_row_ref, feats_col_ref, embeds_ref, valid_ref, gain_ref, right, gain, both
+    )
 
     @pl.when(step == 0)
     def _():
@@ -208,7 +218,7 @@
         out_ref[0, :, rows, :] = join_rows(*outs).astype(BF)
 
 
-def run_back(pair, left, right, lanes, gain, inv, grad, kg, kb):
+def run_back(pair, feats, embeds, valid, lanes, gain, inv, grad, kg, kb):
     return pl.pallas_call(
         back_kernel,
         grid=(T,),
@@ -221,11 +231,15 @@
             pltpu.HBM((T, C, H, W), BF),
             jax.ShapeDtypeStruct((C, H, W), F32),
         ],
-        scratch_shapes=[pltpu.VMEM((C, 8, W), F32), pltpu.VMEM((C, 8, W), F32)],
+        scratch_shapes=[
+            pltpu.VMEM((C, 8, W), F32),
+            pltpu.VMEM((C, 8, W), F32),
+            pltpu.VMEM((2, C, W), F32),
+        ],
         compiler_params=params(),
         cost_estimate=pl.CostEstimate(flops=4 * 2**31, bytes_accessed=16 * 2**20, transcendentals=2**21),
         name="back_project",
-    )(pair, left, right, lanes, gain, inv, grad, kg, kb)
+    )(pair, feats, feats, embeds, valid, lanes, gain, inv, grad, kg, kb)
 
 
 def product_norm(product):
@@ -480,7 +494,7 @@
 
 
 def close_kernel(
-    recv_ref, mean_ref, inv_ref, scaled_ref, pick_ref, weight_ref, valid_ref, base_ref, out_ref
+    recv_ref, mean_ref, inv_ref, scaled_ref, pick_ref, weight_ref, valid_ref, base_ref, *out_refs
 ):
     got = recv_ref[0].astype(F32)
     total = got[0]
@@ -502,7 +516,9 @@
         )
     for side, sums in enumerate((fold_rows(row_sums), jnp.sum(col_sums, axis=1))):
         value = jnp.dot(weight_ref[side], sums, precision=HIGHEST, preferred_element_type=F32)
-        out_ref[side, 0] = (base_ref[side, 0] + value * valid_ref[side, 0]).astype(BF)
+        value = (base_ref[side, 0] + value * valid_ref[side, 0]).astype(BF)
+        for k, out_ref in enumerate(out_refs):
+            out_ref[side, 0] = value[k * 16 : k * 16 + 16]
 
 
 def run_close(recv, mean, inv, scaled, pick, weights, valid, base):
@@ -514,8 +530,8 @@
             each_spec(16, 2, H // 2, W), each_spec(H, W), each_spec(H, W), each_spec(C, H, W),
             whole_spec(4, 2 * W, W), whole_spec(2, C, C), both(1, W), both(C, W),
         ],
-        out_specs=both(C, W),
-        out_shape=jax.ShapeDtypeStruct((2, T, C, W), BF),
+        out_specs=[both(16, W)] * 4,
+        out_shape=[jax.ShapeDtypeStruct((2, T, 16, W), BF)] * 4,
         compiler_params=params(58),
         name="close_sums",
     )(recv, mean, inv, scaled, pick, weights, valid, base)
@@ -607,10 +623,8 @@
 
     col_valid = marks(col).astype(F32)
     row_valid = (marks(row_block) & (offsets // H == half)[None, :]).astype(F32)
-    left_terms = jnp.einsum("fc,tfi->tci", embeds[0], feats[4:], preferred_element_type=F32)
-    left_terms = left_terms * row_valid[:, None, :]
-    right_terms = jnp.einsum("fc,tfj->tcj", embeds[1], feats[:4], preferred_element_type=F32)
-    right_terms = right_terms * col_valid[:, None, :]
+    valid = jnp.stack([row_valid, col_valid])[:, :, None, :]
+    turned = jnp.swapaxes(embeds, 1, 2)
     kl, kr, kg, ko, kb = expand(
         jnp.stack([left_proj.T, right_proj.T, gate_proj.T, out_proj.T, out_proj])
     )
@@ -619,7 +633,7 @@
     terms_pick = jnp.asarray(np.tile(lanes.transpose(0, 2, 1), (1, 2, 1)), BF)
     sums_pick = jnp.where((offsets // H == half)[None, None, :], jnp.asarray(lanes, BF), 0)
 
-    terms = (template_pair, left_terms, right_terms, terms_pick, gain_wide)
+    terms = (template_pair, feats, turned, valid, terms_pick, gain_wide)
     sent, inv = run_norm(*terms, kl, kr)
     def center(weights):
         scaled_weights = gain[:, None] * weights.astype(F32)
@@ -685,7 +699,6 @@
     col_sums, row_sums, mean_half = lax.optimization_barrier((col_sums, row_sums, mean_half))
     recv = exchange(mean_half).reshape(T, 16, 2, H // 2, W)
 
-    valid = jnp.stack([row_valid, col_valid])[:, :, None, :]
     base = jnp.einsum(
         "efc,etcp->etfp", mixed[2], jnp.stack([gate_rows, gate_cols]), precision=HIGHEST
     )
@@ -704,7 +717,8 @@
     own_parts = quarters(grad_own)
     recv, base, *own_parts = lax.optimization_barrier((recv, base, *own_parts))
     closed = run_close(recv, gate_mean, inv, scaled, sums_pick, closing, valid, base)
-    parts = quarters(closed.reshape(2 * T, C, W))
+    closed = [part.reshape(2 * T, 16, W) for part in closed]
+    parts = [closed[0]] + [from_member(closed[k], k) for k in range(1, 4)]
     entries = jnp.concatenate([*own_parts, *parts], axis=0)
     placed = jnp.einsum(
         "be,ex->bx", place, entries.reshape(64, 16 * W), preferred_element_type=F32

time: 375 us -> 377 us (level)
  waiting for transfers between devices: 175 us -> 170 us
    all_to_all x5, waiting for transfers between devices: 165 us -> 160 us  [exchange(): return lax.all_to_all(value, AXES, split_axis=0, concat_axis=0, tiled=True)]
  transfers between devices with their start and end apart: 18 -> 18, of which waited for: 12 -> 12; matrix products, arithmetic and copies ran while one was open for 6% -> 7% of each run, Pallas kernels for 17% -> 17%
where the time goes in v8:
time: 377 us; the launch traced here: 375 us
  waiting for transfers between devices  170 us (45%)
  Pallas kernels  100 us (27%)
  starting transfers between devices  52.4 us (14%)
  local copies, waits for them, and re-layouts  17.7 us (5%)
  blocking collectives  17.7 us (5%)
  other arithmetic  9.3 us (2%)
  matrix products  6.38 us (2%)
    all_to_all x5, waiting for transfers between devices, exchange(): return lax.all_to_all(value, AXES, split_axis=0, concat_axis=0, tiled=True)  160 us
    all_to_all x5, starting transfers between devices, exchange(): return lax.all_to_all(value, AXES, split_axis=0, concat_axis=0, tiled=True)  40.9 us
    pallas_call x1, Pallas kernels, run_gate(): pl.pallas_call(gate_kernel, grid=(T,), in_specs=[each_spec(C, H, W), each...  22.5 us
    all_to_all x1, blocking collectives, exchange(): return lax.all_to_all(value, AXES, split_axis=0, concat_axis=0, tiled=True)  17.7 us
    pallas_call x1, Pallas kernels, run_back(): pl.pallas_call(back_kernel, grid=(T,), in_specs=[*TERM_SPECS, each_spec(H...  16.6 us
    pallas_call x1, Pallas kernels, run_factor(): pl.pallas_call(factor_kernel, grid=(2,), in_specs=[pl.BlockSpec(memory_sp...  16.3 us
    pallas_call x1, Pallas kernels, run_norm(): pl.pallas_call(norm_kernel, grid=(T,), in_specs=[*TERM_SPECS, whole_spec(...  11.8 us
    ppermute x13, starting transfers between devices, from_member(): return lax.ppermute(value, 'col', [(i, i ^ k) for i in range(8)])  11.4 us
  transfers between devices with their start and end apart: 18, of which 12 were waited for; matrix products, arithmetic and copies ran while one was open for 7% of the time, Pallas kernels for 17%

profile of v8, /device:TPU:1, one launch (start us, length us, event | category | flops | bytes accessed | tf_op | source)
XLA Modules:
  0.0 375.3 jit_solution(9545168486662622202)
XLA Ops:
  0.6 1.6 broadcast_in_dim.37
  2.3 11.5 %all-to-all-start = ((bf16[128,16,128]{2,1,0:T(8,128)(2,1)}), bf16[128,16,128]{2,1,0:T(8,128)(2,1)S(1)}, u32[]{:S(2)}, u32[]{:S(2)}) async-start(bf16[128,16,128]{2,1,0:T(8,128)(2,1)} %bitcast.1), calls=%async_computation | async-start | bytes 1048576 | tf_op jit(solution)/shard_map/all_to_all | solution.py:549
  22.9 2.1 select_convert_fusion
  25.0 1.5 slice_bitcast_fusion
  29.0 1.5 collective-permute-start.2
  33.3 11.8 %pair_norm.1 = (bf16[4,32,272,128]{3,2,1,0:T(8,128)(2,1)}, f32[4,64,128]{2,1,0:T(8,128)}) custom-call(bf16[4,64,64,128]{3,2,1,0:T(8,128)(2,1)} %pair_ref.3, bf16[8,64,128]{2,1,0:T(8,128)(2,1)} %copy-done.3, bf16[8,64,128]{2,1,0:T(8,128)(2,1)} %copy-done.3, bf16[2,64,64]{2,1,0:T(8,128)(2,1)} %copy.34.embeds_ref, f32[2,4,1,128]{3,2,1,0:T(1,128)} %bitcast.191, ...), custom_call_target="tpu_custom_call" | custom-call | tf_op jit(solution)/shard_map/pair_norm/pallas_call | solution.py:127
  45.1 9.5 %all-to-all-start.1 = ((bf16[128,272,128]{2,1,0:T(8,128)(2,1)}), bf16[128,272,128]{2,1,0:T(8,128)(2,1)}, u32[]{:S(2)}, u32[]{:S(2)}) async-start(bf16[128,272,128]{2,1,0:T(8,128)(2,1)} %bitcast.180), calls=%async_computation.1 | async-start | bytes 17825792 | tf_op jit(solution)/shard_map/all_to_all | solution.py:549
  58.2 16.6 %back_project.1 = (bf16[4,64,64,128]{3,2,1,0:T(8,128)(2,1)}, bf16[4,64,64,128]{3,2,1,0:T(8,128)(2,1)}, f32[64,64,128]{2,1,0:T(8,128)}) custom-call(bf16[4,64,64,128]{3,2,1,0:T(8,128)(2,1)} %pair_ref.3, bf16[8,64,128]{2,1,0:T(8,128)(2,1)} %copy-done.3, bf16[8,64,128]{2,1,0:T(8,128)(2,1)} %copy-done.3, bf16[2,64,64]{2,1,0:T(8,128)(2,1)} %copy.34.embeds_ref, ...), custom_call_target="tpu_custom_call" | custom-call | flops 8589934592 | bytes 16777216 | tf_op jit(solution)/shard_map/back_project/pallas_call | solution.py:222
  74.8 85.2 %all-to-all-done.1.left_ref.right_ref = bf16[128,272,128]{2,1,0:T(8,128)(2,1)} async-done(((bf16[128,272,128]{2,1,0:T(8,128)(2,1)}), bf16[128,272,128]{2,1,0:T(8,128)(2,1)}, u32[]{:S(2)}, u32[]{:S(2)}) %all-to-all-start.1) | async-done | bytes 8912928 | tf_op jit(solution)/shard_map/all_to_all | solution.py:549
  161.2 8.4 %triangle_product.1 = bf16[128,128,128]{2,1,0:T(8,128)(2,1)} custom-call(bf16[128,272,128]{2,1,0:T(8,128)(2,1)} %all-to-all-done.1.left_ref.right_ref, bf16[128,272,128]{2,1,0:T(8,128)(2,1)} %all-to-all-done.1.left_ref.right_ref), custom_call_target="tpu_custom_call" | custom-call | tf_op jit(solution)/shard_map/triangle_product/pallas_call | solution.py:173
  169.6 10.2 %all-to-all-start.2 = ((bf16[128,128,128]{2,1,0:T(8,128)(2,1)}), bf16[128,128,128]{2,1,0:T(8,128)(2,1)}, u32[]{:S(2)}, u32[]{:S(2)}) async-start(bf16[128,128,128]{2,1,0:T(8,128)(2,1)} %triangle_product.1), calls=%async_computation.2 | async-start | bytes 8388608 | tf_op jit(solution)/shard_map/all_to_all | solution.py:549
  179.9 6.4 %to_matrices.1 = (bf16[2,1024,1024]{2,1,0:T(8,128)(2,1)}, bf16[2,1024,1024]{2,1,0:T(8,128)(2,1)}) custom-call(bf16[128,272,128]{2,1,0:T(8,128)(2,1)} %all-to-all-done.1.left_ref.right_ref, bf16[128,272,128]{2,1,0:T(8,128)(2,1)} %all-to-all-done.1.left_ref.right_ref), custom_call_target="tpu_custom_call" | custom-call | flops 1048576 | bytes 16777216 | tf_op jit(solution)/shard_map/to_matrices/pallas_call | solution.py:374
  186.3 46.4 %all-to-all-done.2 = bf16[128,128,128]{2,1,0:T(8,128)(2,1)} async-done(((bf16[128,128,128]{2,1,0:T(8,128)(2,1)}), bf16[128,128,128]{2,1,0:T(8,128)(2,1)}, u32[]{:S(2)}, u32[]{:S(2)}) %all-to-all-start.2) | async-done | bytes 4194336 | tf_op jit(solution)/shard_map/all_to_all | solution.py:549
  232.7 7.9 %product_grad.1 = bf16[4,64,64,128]{3,2,1,0:T(8,128)(2,1)} custom-call(bf16[4,64,64,128]{3,2,1,0:T(8,128)(2,1)} %bitcast.36.prod_ref, bf16[4,64,64,128]{3,2,1,0:T(8,128)(2,1)} %get-tuple-element.71.back_ref), custom_call_target="tpu_custom_call" | custom-call | flops 33554432 | bytes 12582912 | tf_op jit(solution)/shard_map/product_grad/pallas_call | solution.py:260
  240.6 5.9 %all-to-all-start.3 = ((bf16[128,128,128]{2,1,0:T(8,128)(2,1)}), bf16[128,128,128]{2,1,0:T(8,128)(2,1)}, u32[]{:S(2)}, u32[]{:S(2)}) async-start(bf16[128,128,128]{2,1,0:T(8,128)(2,1)} %bitcast.179), calls=%async_computation.3 | async-start | bytes 8388608 | tf_op jit(solution)/shard_map/all_to_all | solution.py:549
  246.7 1.4 collective-permute-start.5
  248.0 1.7 broadcast_select_fusion.6.pick_ref
  249.7 22.5 %gate_and_embed.1 = (bf16[64,64,128]{2,1,0:T(8,128)(2,1)}, f32[4,64,128]{2,1,0:T(8,128)}, f32[4,64,128]{2,1,0:T(8,128)}, f32[4,64,128]{2,1,0:T(8,128)}, f32[64,128]{1,0:T(8,128)}, /*index=5*/f32[64,128]{1,0:T(8,128)}) custom-call(bf16[4,64,64,128]{3,2,1,0:T(8,128)(2,1)} %bitcast.36.prod_ref, bf16[4,64,64,128]{3,2,1,0:T(8,128)(2,1)} %get-tuple-element.75.scaled_ref, ...), custom_call_target="tpu_custom_call" | custom-call | flops 8589934592 | bytes 12582912 | tf_op jit(solution)/shard_map/gate_and_embed/pallas_call | solution.py:340
  272.6 2.0 copy.39
  274.7 3.4 to_matrix.1.inv_ref
  278.1 21.4 %all-to-all-done.3.grad_ref = bf16[128,128,128]{2,1,0:T(8,128)(2,1)} async-done(((bf16[128,128,128]{2,1,0:T(8,128)(2,1)}), bf16[128,128,128]{2,1,0:T(8,128)(2,1)}, u32[]{:S(2)}, u32[]{:S(2)}) %all-to-all-start.3) | async-done | bytes 4194336 | tf_op jit(solution)/shard_map/all_to_all | solution.py:549
  299.4 16.3 %factor_grads.1 = (bf16[128,32,128]{2,1,0:T(8,128)(2,1)}, bf16[128,32,128]{2,1,0:T(8,128)(2,1)}, f32[2,2,8,1024]{3,2,1,0:T(8,128)}, f32[2,2,1024,128]{3,2,1,0:T(8,128)}) custom-call(s32[1]{0:T(128)} %bitcast.42.core_ref, bf16[2,1024,1024]{2,1,0:T(8,128)(2,1)} %get-tuple-element.89.left_ref, bf16[2,1024,1024]{2,1,0:T(8,128)(2,1)} %get-tuple-element.90.right_ref, ...), custom_call_target="tpu_custom_call" | custom-call | tf_op jit(solution)/shard_map/factor_grads/pallas_call | solution.py:451
  316.6 2.5 collective-permute-done.6.right_ref
  321.4 3.8 %all-to-all-start.4 = ((bf16[128,32,128]{2,1,0:T(8,128)(2,1)}), bf16[128,32,128]{2,1,0:T(8,128)(2,1)S(1)}, u32[]{:S(2)}, u32[]{:S(2)}) async-start(bf16[128,32,128]{2,1,0:T(8,128)(2,1)} %add_halves.1), calls=%async_computation.4 | async-start | bytes 2097152 | tf_op jit(solution)/shard_map/all_to_all | solution.py:549
  328.4 1.5 collective-permute-start.7
  331.6 2.1 fusion.3.base_ref
  333.7 1.9 collective-permute-done.8
  335.6 2.5 collective-permute-done.9
  338.1 6.1 %all-to-all-done.4 = bf16[128,32,128]{2,1,0:T(8,128)(2,1)S(1)} async-done(((bf16[128,32,128]{2,1,0:T(8,128)(2,1)}), bf16[128,32,128]{2,1,0:T(8,128)(2,1)S(1)}, u32[]{:S(2)}, u32[]{:S(2)}) %all-to-all-start.4) | async-done | bytes 1048608 | tf_op jit(solution)/shard_map/all_to_all | solution.py:549
  345.2 5.9 %close_sums.1 = (bf16[2,4,16,128]{3,2,1,0:T(8,128)(2,1)}, bf16[2,4,16,128]{3,2,1,0:T(8,128)(2,1)}, bf16[2,4,16,128]{3,2,1,0:T(8,128)(2,1)}, bf16[2,4,16,128]{3,2,1,0:T(8,128)(2,1)}) custom-call(bf16[4,16,2,32,128]{4,3,2,1,0:T(8,128)(2,1)} %bitcast.182, f32[4,64,128]{2,1,0:T(8,128)} %get-tuple-element.113.mean_ref, f32[4,64,128]{2,1,0:T(8,128)} %get-tuple-element.62.inv_ref, ...), custom_call_target="tpu_custom_call" | custom-call | tf_op jit(solution)/shard_map/close_sums/pallas_call | solution.py:526
  352.6 1.6 collective-permute-start.12
  356.9 17.7 %all_to_all.30 = bf16[128,16,128]{2,1,0:T(8,128)(2,1)S(1)} all-to-all(bf16[128,16,128]{2,1,0:T(8,128)(2,1)S(1)} %bitcast.184), channel_id=1, replica_groups=mesh['row'=16,'col'=8] {'row','col'}, dimensions={0} | all-to-all | bytes 1048576 | tf_op jit(solution)/shard_map/all_to_all | solution.py:549
  (106 shorter events, 33.2 us)
Async XLA Ops:
  2.3 25.0 %all-to-all-start = ((bf16[128,16,128]{2,1,0:T(8,128)(2,1)}), bf16[128,16,128]{2,1,0:T(8,128)(2,1)S(1)}, u32[]{:S(2)}, u32[]{:S(2)}) async-start(bf16[128,16,128]{2,1,0:T(8,128)(2,1)} %bitcast.1), calls=%async_computation | async-start | bytes 1048576 | tf_op jit(solution)/shard_map/all_to_all | solution.py:549
  25.0 7.6 %copy-start.6 = (bf16[64]{0:T(256)(128)(2,1)S(1)}, bf16[64]{0:T(256)(128)(2,1)}, u32[]{:S(2)}) copy-start(bf16[64]{0:T(256)(128)(2,1)} %param.23) | copy-start | bytes 388
  27.6 2.9 collective-permute-start
  28.7 2.8 collective-permute-start.1
  29.0 3.7 collective-permute-start.2
  32.6 0.7 copy-start.3
  45.1 114.9 %all-to-all-start.1 = ((bf16[128,272,128]{2,1,0:T(8,128)(2,1)}), bf16[128,272,128]{2,1,0:T(8,128)(2,1)}, u32[]{:S(2)}, u32[]{:S(2)}) async-start(bf16[128,272,128]{2,1,0:T(8,128)(2,1)} %bitcast.180), calls=%async_computation.1 | async-start | bytes 17825792 | tf_op jit(solution)/shard_map/all_to_all | solution.py:549
  161.1 8.5 %collective-permute-start.3 = (bf16[64,1,16,128]{3,2,0,1:T(8,128)(2,1)S(1)}, bf16[64,1,16,128]{3,2,0,1:T(8,128)(2,1)S(1)}, u32[]{:S(2)}, u32[]{:S(2)}) collective-permute-start(bf16[64,1,16,128]{3,2,0,1:T(8,128)(2,1)S(1)} %get-tuple-element.83), channel_id=1, source_target_pairs={{0,2},{1,3},{2,0},{3,1},{4,6},{5,7},{6,4},{7,5},{8,10},{9,11},{10,... | collective-permute-start | bytes 786440 | tf_op jit(solution)/shard_map/ppermute | solution.py:541
  169.6 63.1 %all-to-all-start.2 = ((bf16[128,128,128]{2,1,0:T(8,128)(2,1)}), bf16[128,128,128]{2,1,0:T(8,128)(2,1)}, u32[]{:S(2)}, u32[]{:S(2)}) async-start(bf16[128,128,128]{2,1,0:T(8,128)(2,1)} %triangle_product.1), calls=%async_computation.2 | async-start | bytes 8388608 | tf_op jit(solution)/shard_map/all_to_all | solution.py:549
  232.7 7.9 %collective-permute-start.4 = (bf16[64,1,16,128]{3,2,0,1:T(8,128)(2,1)S(1)}, bf16[64,1,16,128]{3,2,0,1:T(8,128)(2,1)S(1)}, u32[]{:S(2)}, u32[]{:S(2)}) collective-permute-start(bf16[64,1,16,128]{3,2,0,1:T(8,128)(2,1)S(1)} %get-tuple-element.85), channel_id=1, source_target_pairs={{0,2},{1,3},{2,0},{3,1},{4,6},{5,7},{6,4},{7,5},{8,10},{9,11},{10,... | collective-permute-start | bytes 786440 | tf_op jit(solution)/shard_map/ppermute | solution.py:541
  240.6 58.8 %all-to-all-start.3 = ((bf16[128,128,128]{2,1,0:T(8,128)(2,1)}), bf16[128,128,128]{2,1,0:T(8,128)(2,1)}, u32[]{:S(2)}, u32[]{:S(2)}) async-start(bf16[128,128,128]{2,1,0:T(8,128)(2,1)} %bitcast.179), calls=%async_computation.3 | async-start | bytes 8388608 | tf_op jit(solution)/shard_map/all_to_all | solution.py:549
  246.7 25.6 %collective-permute-start.5 = (bf16[128,2,1,16,128]{4,3,0,1,2:T(8,128)(2,1)S(1)}, bf16[128,2,1,16,128]{4,3,0,1,2:T(8,128)(2,1)S(1)}, u32[]{:S(2)}, u32[]{:S(2)}) collective-permute-start(bf16[128,2,1,16,128]{4,3,0,1,2:T(8,128)(2,1)S(1)} %maximum_bitcast_fusion), channel_id=1, source_target_pairs={{0,1},{1,0},{2,3},{3,2},{4,5},{5,4},{6,7},{7,6},{8,9},{9,8},{10,11... | collective-permute-start | bytes 3145736 | tf_op jit(solution)/shard_map/ppermute | solution.py:541
  299.4 25.8 %copy-start.5 = (f32[64,128]{1,0:T(8,128)S(1)}, f32[64,128]{1,0:T(8,128)}, u32[]{:S(2)}) copy-start(f32[64,128]{1,0:T(8,128)} %get-tuple-element.102) | copy-start | bytes 98308
  315.8 3.3 collective-permute-start.6
  319.1 1.2 copy-start
  320.3 6.8 %copy-start.2 = (f32[2,2,1024,128]{3,2,1,0:T(8,128)S(1)}, f32[2,2,1024,128]{3,2,1,0:T(8,128)}, u32[]{:S(2)}) copy-start(f32[2,2,1024,128]{3,2,1,0:T(8,128)} %get-tuple-element.105) | copy-start | bytes 6291460
  320.3 11.3 %copy-start.4 = (f32[2,4,128]{2,1,0:T(4,128)S(1)}, f32[2,4,128]{2,1,0:T(4,128)}, u32[]{:S(2)}) copy-start(f32[2,4,128]{2,1,0:T(4,128)} %add_convert_fusion) | copy-start | bytes 12292
  321.4 22.8 %all-to-all-start.4 = ((bf16[128,32,128]{2,1,0:T(8,128)(2,1)}), bf16[128,32,128]{2,1,0:T(8,128)(2,1)S(1)}, u32[]{:S(2)}, u32[]{:S(2)}) async-start(bf16[128,32,128]{2,1,0:T(8,128)(2,1)} %add_halves.1), calls=%async_computation.4 | async-start | bytes 2097152 | tf_op jit(solution)/shard_map/all_to_all | solution.py:549
  328.4 5.3 %collective-permute-start.7 = (bf16[8,16,128]{2,0,1:T(8,128)(2,1)S(1)}, bf16[8,16,128]{2,0,1:T(8,128)(2,1)S(1)}, u32[]{:S(2)}, u32[]{:S(2)}) collective-permute-start(bf16[8,16,128]{2,0,1:T(8,128)(2,1)S(1)} %get-tuple-element.145), channel_id=1, source_target_pairs={{0,1},{1,0},{2,3},{3,2},{4,5},{5,4},{6,7},{7,6},{8,9},{9,8},{10,11... | collective-permute-start | bytes 98312 | tf_op jit(solution)/shard_map/ppermute | solution.py:541
  329.9 5.7 %collective-permute-start.8 = (bf16[8,16,128]{2,0,1:T(8,128)(2,1)S(1)}, bf16[8,16,128]{2,0,1:T(8,128)(2,1)S(1)}, u32[]{:S(2)}, u32[]{:S(2)}) collective-permute-start(bf16[8,16,128]{2,0,1:T(8,128)(2,1)S(1)} %get-tuple-element.144), channel_id=1, source_target_pairs={{0,2},{1,3},{2,0},{3,1},{4,6},{5,7},{6,4},{7,5},{8,10},{9,11},{10,... | collective-permute-start | bytes 98312 | tf_op jit(solution)/shard_map/ppermute | solution.py:541
  330.2 7.9 %collective-permute-start.9 = (bf16[8,16,128]{2,0,1:T(8,128)(2,1)S(1)}, bf16[8,16,128]{2,0,1:T(8,128)(2,1)S(1)}, u32[]{:S(2)}, u32[]{:S(2)}) collective-permute-start(bf16[8,16,128]{2,0,1:T(8,128)(2,1)S(1)} %get-tuple-element.143), channel_id=1, source_target_pairs={{0,3},{1,2},{2,1},{3,0},{4,7},{5,6},{6,5},{7,4},{8,11},{9,10},{10,... | collective-permute-start | bytes 98312 | tf_op jit(solution)/shard_map/ppermute | solution.py:541
  344.3 1.0 copy-start.1
  351.1 3.8 %collective-permute-start.10 = (bf16[8,16,128]{2,1,0:T(8,128)(2,1)}, bf16[8,16,128]{2,1,0:T(8,128)(2,1)S(1)}, u32[]{:S(2)}, u32[]{:S(2)}) collective-permute-start(bf16[8,16,128]{2,1,0:T(8,128)(2,1)} %bitcast.211), channel_id=1, source_target_pairs={{0,1},{1,0},{2,3},{3,2},{4,5},{5,4},{6,7},{7,6},{8,9},{9,8},{10,11... | collective-permute-start | bytes 98312 | tf_op jit(solution)/shard_map/ppermute | solution.py:541
  352.4 3.0 collective-permute-start.11
  352.6 3.9 %collective-permute-start.12 = (bf16[8,16,128]{2,1,0:T(8,128)(2,1)}, bf16[8,16,128]{2,1,0:T(8,128)(2,1)S(1)}, u32[]{:S(2)}, u32[]{:S(2)}) collective-permute-start(bf16[8,16,128]{2,1,0:T(8,128)(2,1)} %bitcast.209), channel_id=1, source_target_pairs={{0,3},{1,2},{2,1},{3,0},{4,7},{5,6},{6,5},{7,4},{8,11},{9,10},{10,... | collective-permute-start | bytes 98312 | tf_op jit(solution)/shard_map/ppermute | solution.py:541

commit v9 on v8

--- a/solution.py
+++ b/solution.py
@@ -63,10 +63,13 @@
         terms = jnp.dot(embeds_ref[side], feats[0], preferred_element_type=F32)
         both[side] = terms * valid_ref[side, 0]
     mask = row_mask(W)
+    same = lax.broadcasted_iota(jnp.int32, (C, C), 0) == lax.broadcasted_iota(jnp.int32, (C, C), 1)
+    diagonal = jnp.where(same, jnp.broadcast_to(gain_ref[...].astype(F32), (C, C)), 0.0)
+    both[2] = jnp.dot(diagonal.astype(BF), jnp.ones((C, W), BF), preferred_element_type=F32)
     rows = []
     for c in range(C):
         right[c] = jnp.broadcast_to(both[1, c : c + 1, :], (8, W))
-        gain[c] = jnp.broadcast_to(gain_ref[c : c + 1, :], (8, W))
+        gain[c] = jnp.broadcast_to(both[2, c : c + 1, :], (8, W))
         rows.append(jnp.broadcast_to(both[0, c : c + 1, :], (8, W)) * mask)
     value = jnp.concatenate(rows, axis=0)
     high = value.astype(BF)
@@ -119,7 +122,7 @@
     whole_spec(2, C, C),
     pl.BlockSpec((2, 1, 1, W), lambda t: (0, t, 0, 0)),
     whole_spec(4, 2 * W, 2 * W),
-    whole_spec(C, W),
+    whole_spec(1, C),
 ]
 
 
@@ -136,7 +139,7 @@
         scratch_shapes=[
             pltpu.VMEM((C, 8, W), F32),
             pltpu.VMEM((C, 8, W), F32),
-            pltpu.VMEM((2, C, W), F32),
+            pltpu.VMEM((3, C, W), F32),
             pltpu.VMEM((4, K8, 2 * W), F32),
             pltpu.VMEM((K8, N), BF),
         ],
@@ -234,7 +237,7 @@
         scratch_shapes=[
             pltpu.VMEM((C, 8, W), F32),
             pltpu.VMEM((C, 8, W), F32),
-            pltpu.VMEM((2, C, W), F32),
+            pltpu.VMEM((3, C, W), F32),
         ],
         compiler_params=params(),
         cost_estimate=pl.CostEstimate(flops=4 * 2**31, bytes_accessed=16 * 2**20, transcendentals=2**21),
@@ -600,7 +603,6 @@
     sent_feat = jnp.broadcast_to(template_feat.reshape(1, 4, 16, W), (32, 4, 16, W))
     pool = exchange(sent_feat.reshape(128, 16, W))
     gain = norm_gain.astype(F32)
-    gain_wide = jnp.broadcast_to(gain[:, None], (C, W))
     column_ids = lambda m, at: lax.dynamic_index_in_dim(m, at, axis=1, keepdims=False)
     row_ids = column_ids(block_map, row_block)
     member_ids = [column_ids(block_map, col ^ k) for k in range(4)]
@@ -625,16 +627,16 @@
     row_valid = (marks(row_block) & (offsets // H == half)[None, :]).astype(F32)
     valid = jnp.stack([row_valid, col_valid])[:, :, None, :]
     turned = jnp.swapaxes(embeds, 1, 2)
-    kl, kr, kg, ko, kb = expand(
-        jnp.stack([left_proj.T, right_proj.T, gate_proj.T, out_proj.T, out_proj])
-    )
+    kl, kr = expand(jnp.stack([left_proj.T, right_proj.T]))
     group = 2 * np.arange(4)[:, None, None] + (np.arange(2 * W) // W)[None, :, None]
     lanes = np.arange(W)[None, None, :] % H // 8 == group
     terms_pick = jnp.asarray(np.tile(lanes.transpose(0, 2, 1), (1, 2, 1)), BF)
     sums_pick = jnp.where((offsets // H == half)[None, None, :], jnp.asarray(lanes, BF), 0)
 
-    terms = (template_pair, feats, turned, valid, terms_pick, gain_wide)
+    terms = (template_pair, feats, turned, valid, terms_pick, norm_gain.reshape(1, C))
     sent, inv = run_norm(*terms, kl, kr)
+    sent, gate_late, out_late = lax.optimization_barrier((sent, gate_proj, out_proj))
+    kg, ko, kb = expand(jnp.stack([gate_late.T, out_late.T, out_late]))
     def center(weights):
         scaled_weights = gain[:, None] * weights.astype(F32)
         return scaled_weights - jnp.mean(scaled_weights, axis=0, keepdims=True)

time: 377 us -> 373 us (0.989)
  starting transfers between devices: 52.4 us -> 48.1 us
  waiting for transfers between devices: 170 us -> 174 us
    all_to_all x5, starting transfers between devices: 40.9 us -> 36.7 us  [exchange(): return lax.all_to_all(value, AXES, split_axis=0, concat_axis=0, tiled=True)]
  transfers between devices with their start and end apart: 18 -> 18, of which waited for: 12 -> 12; matrix products, arithmetic and copies ran while one was open for 7% -> 6% of each run, Pallas kernels for 17% -> 18%
where the time goes in v9:
time: 373 us; the launch traced here: 371 us
  waiting for transfers between devices  174 us (47%)
  Pallas kernels  100 us (27%)
  starting transfers between devices  48.1 us (13%)
  blocking collectives  17.7 us (5%)
  local copies, waits for them, and re-layouts  14.8 us (4%)
  other arithmetic  8.6 us (2%)
  matrix products  6.62 us (2%)
    all_to_all x5, waiting for transfers between devices, exchange(): return lax.all_to_all(value, AXES, split_axis=0, concat_axis=0, tiled=True)  163 us
    all_to_all x5, starting transfers between devices, exchange(): return lax.all_to_all(value, AXES, split_axis=0, concat_axis=0, tiled=True)  36.7 us
    pallas_call x1, Pallas kernels, run_gate(): pl.pallas_call(gate_kernel, grid=(T,), in_specs=[each_spec(C, H, W), each...  22.5 us
    all_to_all x1, blocking collectives, exchange(): return lax.all_to_all(value, AXES, split_axis=0, concat_axis=0, tiled=True)  17.7 us
    pallas_call x1, Pallas kernels, run_back(): pl.pallas_call(back_kernel, grid=(T,), in_specs=[*TERM_SPECS, each_spec(H...  16.7 us
    pallas_call x1, Pallas kernels, run_factor(): pl.pallas_call(factor_kernel, grid=(2,), in_specs=[pl.BlockSpec(memory_sp...  16.3 us
    pallas_call x1, Pallas kernels, run_norm(): pl.pallas_call(norm_kernel, grid=(T,), in_specs=[*TERM_SPECS, whole_spec(...  11.8 us
    ppermute x13, starting transfers between devices, from_member(): return lax.ppermute(value, 'col', [(i, i ^ k) for i in range(8)])  11.5 us
  transfers between devices with their start and end apart: 18, of which 12 were waited for; matrix products, arithmetic and copies ran while one was open for 6% of the time, Pallas kernels for 18%

profile of v9, /device:TPU:1, one launch (start us, length us, event | category | flops | bytes accessed | tf_op | source)
XLA Modules:
  0.0 371.3 jit_solution(11853607942844702116)
XLA Ops:
  0.6 1.6 broadcast_in_dim.43
  2.3 11.5 %all-to-all-start = ((bf16[128,16,128]{2,1,0:T(8,128)(2,1)}), bf16[128,16,128]{2,1,0:T(8,128)(2,1)S(1)}, u32[]{:S(2)}, u32[]{:S(2)}) async-start(bf16[128,16,128]{2,1,0:T(8,128)(2,1)} %bitcast.1), calls=%async_computation | async-start | bytes 1048576 | tf_op jit(solution)/shard_map/all_to_all | solution.py:552
  18.3 1.5 select_convert_fusion.1
  20.8 6.4 %all-to-all-done = bf16[128,16,128]{2,1,0:T(8,128)(2,1)S(1)} async-done(((bf16[128,16,128]{2,1,0:T(8,128)(2,1)}), bf16[128,16,128]{2,1,0:T(8,128)(2,1)S(1)}, u32[]{:S(2)}, u32[]{:S(2)}) %all-to-all-start) | async-done | bytes 524320 | tf_op jit(solution)/shard_map/all_to_all | solution.py:552
  29.0 1.5 collective-permute-start.2
  33.3 11.8 %pair_norm.1 = (bf16[4,32,272,128]{3,2,1,0:T(8,128)(2,1)}, f32[4,64,128]{2,1,0:T(8,128)}) custom-call(bf16[4,64,64,128]{3,2,1,0:T(8,128)(2,1)} %pair_ref.3, bf16[8,64,128]{2,1,0:T(8,128)(2,1)} %copy-done.3, bf16[8,64,128]{2,1,0:T(8,128)(2,1)} %copy-done.3, bf16[2,64,64]{2,1,0:T(8,128)(2,1)} %copy.29.embeds_ref, f32[2,4,1,128]{3,2,1,0:T(1,128)} %bitcast.192, ...), custom_call_target="tpu_custom_call" | custom-call | tf_op jit(solution)/shard_map/pair_norm/pallas_call | solution.py:130
  45.2 5.1 %all-to-all-start.1 = ((bf16[128,272,128]{2,1,0:T(8,128)(2,1)}), bf16[128,272,128]{2,1,0:T(8,128)(2,1)}, u32[]{:S(2)}, u32[]{:S(2)}) async-start(bf16[128,272,128]{2,1,0:T(8,128)(2,1)} %bitcast.181), calls=%async_computation.1 | async-start | bytes 17825792 | tf_op jit(solution)/shard_map/all_to_all | solution.py:552
  56.4 16.7 %back_project.1 = (bf16[4,64,64,128]{3,2,1,0:T(8,128)(2,1)}, bf16[4,64,64,128]{3,2,1,0:T(8,128)(2,1)}, f32[64,64,128]{2,1,0:T(8,128)}) custom-call(bf16[4,64,64,128]{3,2,1,0:T(8,128)(2,1)} %pair_ref.3, bf16[8,64,128]{2,1,0:T(8,128)(2,1)} %copy-done.3, bf16[8,64,128]{2,1,0:T(8,128)(2,1)} %copy-done.3, bf16[2,64,64]{2,1,0:T(8,128)(2,1)} %copy.29.embeds_ref, ...), custom_call_target="tpu_custom_call" | custom-call | flops 8589934592 | bytes 16777216 | tf_op jit(solution)/shard_map/back_project/pallas_call | solution.py:225
  73.1 82.8 %all-to-all-done.1.left_ref.right_ref = bf16[128,272,128]{2,1,0:T(8,128)(2,1)} async-done(((bf16[128,272,128]{2,1,0:T(8,128)(2,1)}), bf16[128,272,128]{2,1,0:T(8,128)(2,1)}, u32[]{:S(2)}, u32[]{:S(2)}) %all-to-all-start.1) | async-done | bytes 8912928 | tf_op jit(solution)/shard_map/all_to_all | solution.py:552
  157.0 8.4 %triangle_product.1 = bf16[128,128,128]{2,1,0:T(8,128)(2,1)} custom-call(bf16[128,272,128]{2,1,0:T(8,128)(2,1)} %all-to-all-done.1.left_ref.right_ref, bf16[128,272,128]{2,1,0:T(8,128)(2,1)} %all-to-all-done.1.left_ref.right_ref), custom_call_target="tpu_custom_call" | custom-call | tf_op jit(solution)/shard_map/triangle_product/pallas_call | solution.py:176
  165.5 10.2 %all-to-all-start.2 = ((bf16[128,128,128]{2,1,0:T(8,128)(2,1)}), bf16[128,128,128]{2,1,0:T(8,128)(2,1)}, u32[]{:S(2)}, u32[]{:S(2)}) async-start(bf16[128,128,128]{2,1,0:T(8,128)(2,1)} %triangle_product.1), calls=%async_computation.2 | async-start | bytes 8388608 | tf_op jit(solution)/shard_map/all_to_all | solution.py:552
  175.7 6.4 %to_matrices.1 = (bf16[2,1024,1024]{2,1,0:T(8,128)(2,1)}, bf16[2,1024,1024]{2,1,0:T(8,128)(2,1)}) custom-call(bf16[128,272,128]{2,1,0:T(8,128)(2,1)} %all-to-all-done.1.left_ref.right_ref, bf16[128,272,128]{2,1,0:T(8,128)(2,1)} %all-to-all-done.1.left_ref.right_ref), custom_call_target="tpu_custom_call" | custom-call | flops 1048576 | bytes 16777216 | tf_op jit(solution)/shard_map/to_matrices/pallas_call | solution.py:377
  182.1 46.4 %all-to-all-done.2 = bf16[128,128,128]{2,1,0:T(8,128)(2,1)} async-done(((bf16[128,128,128]{2,1,0:T(8,128)(2,1)}), bf16[128,128,128]{2,1,0:T(8,128)(2,1)}, u32[]{:S(2)}, u32[]{:S(2)}) %all-to-all-start.2) | async-done | bytes 4194336 | tf_op jit(solution)/shard_map/all_to_all | solution.py:552
  228.5 7.9 %product_grad.1 = bf16[4,64,64,128]{3,2,1,0:T(8,128)(2,1)} custom-call(bf16[4,64,64,128]{3,2,1,0:T(8,128)(2,1)} %bitcast.38.prod_ref, bf16[4,64,64,128]{3,2,1,0:T(8,128)(2,1)} %get-tuple-element.77.back_ref), custom_call_target="tpu_custom_call" | custom-call | flops 33554432 | bytes 12582912 | tf_op jit(solution)/shard_map/product_grad/pallas_call | solution.py:263
  236.4 5.9 %all-to-all-start.3 = ((bf16[128,128,128]{2,1,0:T(8,128)(2,1)}), bf16[128,128,128]{2,1,0:T(8,128)(2,1)}, u32[]{:S(2)}, u32[]{:S(2)}) async-start(bf16[128,128,128]{2,1,0:T(8,128)(2,1)} %bitcast.180), calls=%async_computation.3 | async-start | bytes 8388608 | tf_op jit(solution)/shard_map/all_to_all | solution.py:552
  242.5 1.4 collective-permute-start.5
  243.9 1.7 broadcast_select_fusion.6.pick_ref
  245.6 22.5 %gate_and_embed.1 = (bf16[64,64,128]{2,1,0:T(8,128)(2,1)}, f32[4,64,128]{2,1,0:T(8,128)}, f32[4,64,128]{2,1,0:T(8,128)}, f32[4,64,128]{2,1,0:T(8,128)}, f32[64,128]{1,0:T(8,128)}, /*index=5*/f32[64,128]{1,0:T(8,128)}) custom-call(bf16[4,64,64,128]{3,2,1,0:T(8,128)(2,1)} %bitcast.38.prod_ref, bf16[4,64,64,128]{3,2,1,0:T(8,128)(2,1)} %get-tuple-element.81.scaled_ref, ...), custom_call_target="tpu_custom_call" | custom-call | flops 8589934592 | bytes 12582912 | tf_op jit(solution)/shard_map/gate_and_embed/pallas_call | solution.py:343
  268.5 2.1 copy.36
  270.6 3.4 to_matrix.1.inv_ref
  273.9 21.3 %all-to-all-done.3.grad_ref = bf16[128,128,128]{2,1,0:T(8,128)(2,1)} async-done(((bf16[128,128,128]{2,1,0:T(8,128)(2,1)}), bf16[128,128,128]{2,1,0:T(8,128)(2,1)}, u32[]{:S(2)}, u32[]{:S(2)}) %all-to-all-start.3) | async-done | bytes 4194336 | tf_op jit(solution)/shard_map/all_to_all | solution.py:552
  295.3 16.3 %factor_grads.1 = (bf16[128,32,128]{2,1,0:T(8,128)(2,1)}, bf16[128,32,128]{2,1,0:T(8,128)(2,1)}, f32[2,2,8,1024]{3,2,1,0:T(8,128)}, f32[2,2,1024,128]{3,2,1,0:T(8,128)}) custom-call(s32[1]{0:T(128)} %bitcast.44.core_ref, bf16[2,1024,1024]{2,1,0:T(8,128)(2,1)} %get-tuple-element.95.left_ref, bf16[2,1024,1024]{2,1,0:T(8,128)(2,1)} %get-tuple-element.96.right_ref, ...), custom_call_target="tpu_custom_call" | custom-call | tf_op jit(solution)/shard_map/factor_grads/pallas_call | solution.py:454
  312.4 2.5 collective-permute-done.6.right_ref
  317.3 3.9 %all-to-all-start.4 = ((bf16[128,32,128]{2,1,0:T(8,128)(2,1)}), bf16[128,32,128]{2,1,0:T(8,128)(2,1)S(1)}, u32[]{:S(2)}, u32[]{:S(2)}) async-start(bf16[128,32,128]{2,1,0:T(8,128)(2,1)} %add_halves.1), calls=%async_computation.4 | async-start | bytes 2097152 | tf_op jit(solution)/shard_map/all_to_all | solution.py:552
  324.3 1.5 collective-permute-start.7
  327.6 2.1 fusion.2.base_ref
  329.7 1.9 collective-permute-done.8
  331.6 2.5 collective-permute-done.9
  334.1 6.1 %all-to-all-done.4 = bf16[128,32,128]{2,1,0:T(8,128)(2,1)S(1)} async-done(((bf16[128,32,128]{2,1,0:T(8,128)(2,1)}), bf16[128,32,128]{2,1,0:T(8,128)(2,1)S(1)}, u32[]{:S(2)}, u32[]{:S(2)}) %all-to-all-start.4) | async-done | bytes 1048608 | tf_op jit(solution)/shard_map/all_to_all | solution.py:552
  341.2 5.9 %close_sums.1 = (bf16[2,4,16,128]{3,2,1,0:T(8,128)(2,1)}, bf16[2,4,16,128]{3,2,1,0:T(8,128)(2,1)}, bf16[2,4,16,128]{3,2,1,0:T(8,128)(2,1)}, bf16[2,4,16,128]{3,2,1,0:T(8,128)(2,1)}) custom-call(bf16[4,16,2,32,128]{4,3,2,1,0:T(8,128)(2,1)} %bitcast.183, f32[4,64,128]{2,1,0:T(8,128)} %get-tuple-element.119.mean_ref, f32[4,64,128]{2,1,0:T(8,128)} %get-tuple-element.66.inv_ref, ...), custom_call_target="tpu_custom_call" | custom-call | tf_op jit(solution)/shard_map/close_sums/pallas_call | solution.py:529
  348.6 1.6 collective-permute-start.12
  352.9 17.7 %all_to_all.30 = bf16[128,16,128]{2,1,0:T(8,128)(2,1)S(1)} all-to-all(bf16[128,16,128]{2,1,0:T(8,128)(2,1)S(1)} %bitcast.185), channel_id=1, replica_groups=mesh['row'=16,'col'=8] {'row','col'}, dimensions={0} | all-to-all | bytes 1048576 | tf_op jit(solution)/shard_map/all_to_all | solution.py:552
  (113 shorter events, 31.3 us)
Async XLA Ops:
  2.3 25.0 %all-to-all-start = ((bf16[128,16,128]{2,1,0:T(8,128)(2,1)}), bf16[128,16,128]{2,1,0:T(8,128)(2,1)S(1)}, u32[]{:S(2)}, u32[]{:S(2)}) async-start(bf16[128,16,128]{2,1,0:T(8,128)(2,1)} %bitcast.1), calls=%async_computation | async-start | bytes 1048576 | tf_op jit(solution)/shard_map/all_to_all | solution.py:552
  27.6 2.9 collective-permute-start
  28.7 2.8 collective-permute-start.1
  29.0 3.7 collective-permute-start.2
  32.6 0.7 copy-start.3
  45.1 5.2 %copy-start.10 = (bf16[64]{0:T(256)(128)(2,1)S(1)}, bf16[64]{0:T(256)(128)(2,1)}, u32[]{:S(2)}) copy-start(bf16[64]{0:T(256)(128)(2,1)} %param.24) | copy-start | bytes 388
  45.1 5.2 %copy-start.7 = (bf16[64,64]{1,0:T(8,128)(2,1)S(1)}, bf16[64,64]{1,0:T(8,128)(2,1)}, u32[]{:S(2)}) copy-start(bf16[64,64]{1,0:T(8,128)(2,1)} %param.25) | copy-start | bytes 24580
  45.1 5.3 %copy-start.8 = (bf16[64,64]{1,0:T(8,128)(2,1)S(1)}, bf16[64,64]{1,0:T(8,128)(2,1)}, u32[]{:S(2)}) copy-start(bf16[64,64]{1,0:T(8,128)(2,1)} %param.26) | copy-start | bytes 24580
  45.1 5.4 %copy-start.4 = (bf16[64,64]{1,0:T(8,128)(2,1)S(1)}, bf16[64,64]{1,0:T(8,128)(2,1)}, u32[]{:S(2)}) copy-start(bf16[64,64]{1,0:T(8,128)(2,1)} %param.27) | copy-start | bytes 24580
  45.1 9.2 %copy-start.9 = (bf16[64,64]{1,0:T(8,128)(2,1)S(1)}, bf16[64,64]{1,0:T(8,128)(2,1)}, u32[]{:S(2)}) copy-start(bf16[64,64]{1,0:T(8,128)(2,1)} %param.28) | copy-start | bytes 24580
  45.2 9.3 %copy-start.11 = (bf16[512,64,1]{0,1,2:T(8,128)(2,1)S(1)}, bf16[512,64,1]{0,1,2:T(8,128)(2,1)}, u32[]{:S(2)}) copy-start(bf16[512,64,1]{0,1,2:T(8,128)(2,1)} %constant.178) | copy-start | bytes 196612
  45.2 110.7 %all-to-all-start.1 = ((bf16[128,272,128]{2,1,0:T(8,128)(2,1)}), bf16[128,272,128]{2,1,0:T(8,128)(2,1)}, u32[]{:S(2)}, u32[]{:S(2)}) async-start(bf16[128,272,128]{2,1,0:T(8,128)(2,1)} %bitcast.181), calls=%async_computation.1 | async-start | bytes 17825792 | tf_op jit(solution)/shard_map/all_to_all | solution.py:552
  156.9 8.5 %collective-permute-start.3 = (bf16[64,1,16,128]{3,2,0,1:T(8,128)(2,1)S(1)}, bf16[64,1,16,128]{3,2,0,1:T(8,128)(2,1)S(1)}, u32[]{:S(2)}, u32[]{:S(2)}) collective-permute-start(bf16[64,1,16,128]{3,2,0,1:T(8,128)(2,1)S(1)} %get-tuple-element.89), channel_id=1, source_target_pairs={{0,2},{1,3},{2,0},{3,1},{4,6},{5,7},{6,4},{7,5},{8,10},{9,11},{10,... | collective-permute-start | bytes 786440 | tf_op jit(solution)/shard_map/ppermute | solution.py:544
  165.5 63.1 %all-to-all-start.2 = ((bf16[128,128,128]{2,1,0:T(8,128)(2,1)}), bf16[128,128,128]{2,1,0:T(8,128)(2,1)}, u32[]{:S(2)}, u32[]{:S(2)}) async-start(bf16[128,128,128]{2,1,0:T(8,128)(2,1)} %triangle_product.1), calls=%async_computation.2 | async-start | bytes 8388608 | tf_op jit(solution)/shard_map/all_to_all | solution.py:552
  228.5 7.9 %collective-permute-start.4 = (bf16[64,1,16,128]{3,2,0,1:T(8,128)(2,1)S(1)}, bf16[64,1,16,128]{3,2,0,1:T(8,128)(2,1)S(1)}, u32[]{:S(2)}, u32[]{:S(2)}) collective-permute-start(bf16[64,1,16,128]{3,2,0,1:T(8,128)(2,1)S(1)} %get-tuple-element.91), channel_id=1, source_target_pairs={{0,2},{1,3},{2,0},{3,1},{4,6},{5,7},{6,4},{7,5},{8,10},{9,11},{10,... | collective-permute-start | bytes 786440 | tf_op jit(solution)/shard_map/ppermute | solution.py:544
  236.4 58.8 %all-to-all-start.3 = ((bf16[128,128,128]{2,1,0:T(8,128)(2,1)}), bf16[128,128,128]{2,1,0:T(8,128)(2,1)}, u32[]{:S(2)}, u32[]{:S(2)}) async-start(bf16[128,128,128]{2,1,0:T(8,128)(2,1)} %bitcast.180), calls=%async_computation.3 | async-start | bytes 8388608 | tf_op jit(solution)/shard_map/all_to_all | solution.py:552
  242.5 25.6 %collective-permute-start.5 = (bf16[128,2,1,16,128]{4,3,0,1,2:T(8,128)(2,1)S(1)}, bf16[128,2,1,16,128]{4,3,0,1,2:T(8,128)(2,1)S(1)}, u32[]{:S(2)}, u32[]{:S(2)}) collective-permute-start(bf16[128,2,1,16,128]{4,3,0,1,2:T(8,128)(2,1)S(1)} %maximum_bitcast_fusion), channel_id=1, source_target_pairs={{0,1},{1,0},{2,3},{3,2},{4,5},{5,4},{6,7},{7,6},{8,9},{9,8},{10,11... | collective-permute-start | bytes 3145736 | tf_op jit(solution)/shard_map/ppermute | solution.py:544
  295.3 25.9 %copy-start.6 = (f32[64,128]{1,0:T(8,128)S(1)}, f32[64,128]{1,0:T(8,128)}, u32[]{:S(2)}) copy-start(f32[64,128]{1,0:T(8,128)} %get-tuple-element.108) | copy-start | bytes 98308
  311.6 3.3 collective-permute-start.6
  314.9 1.2 copy-start
  316.2 7.0 %copy-start.2 = (f32[2,2,1024,128]{3,2,1,0:T(8,128)S(1)}, f32[2,2,1024,128]{3,2,1,0:T(8,128)}, u32[]{:S(2)}) copy-start(f32[2,2,1024,128]{3,2,1,0:T(8,128)} %get-tuple-element.111) | copy-start | bytes 6291460
  317.3 10.3 %copy-start.5 = (f32[2,4,128]{2,1,0:T(4,128)S(1)}, f32[2,4,128]{2,1,0:T(4,128)}, u32[]{:S(2)}) copy-start(f32[2,4,128]{2,1,0:T(4,128)} %add_convert_fusion) | copy-start | bytes 12292
  317.3 23.0 %all-to-all-start.4 = ((bf16[128,32,128]{2,1,0:T(8,128)(2,1)}), bf16[128,32,128]{2,1,0:T(8,128)(2,1)S(1)}, u32[]{:S(2)}, u32[]{:S(2)}) async-start(bf16[128,32,128]{2,1,0:T(8,128)(2,1)} %add_halves.1), calls=%async_computation.4 | async-start | bytes 2097152 | tf_op jit(solution)/shard_map/all_to_all | solution.py:552
  324.3 5.3 %collective-permute-start.7 = (bf16[8,16,128]{2,0,1:T(8,128)(2,1)S(1)}, bf16[8,16,128]{2,0,1:T(8,128)(2,1)S(1)}, u32[]{:S(2)}, u32[]{:S(2)}) collective-permute-start(bf16[8,16,128]{2,0,1:T(8,128)(2,1)S(1)} %get-tuple-element.151), channel_id=1, source_target_pairs={{0,1},{1,0},{2,3},{3,2},{4,5},{5,4},{6,7},{7,6},{8,9},{9,8},{10,11... | collective-permute-start | bytes 98312 | tf_op jit(solution)/shard_map/ppermute | solution.py:544
  325.8 5.7 %collective-permute-start.8 = (bf16[8,16,128]{2,0,1:T(8,128)(2,1)S(1)}, bf16[8,16,128]{2,0,1:T(8,128)(2,1)S(1)}, u32[]{:S(2)}, u32[]{:S(2)}) collective-permute-start(bf16[8,16,128]{2,0,1:T(8,128)(2,1)S(1)} %get-tuple-element.150), channel_id=1, source_target_pairs={{0,2},{1,3},{2,0},{3,1},{4,6},{5,7},{6,4},{7,5},{8,10},{9,11},{10,... | collective-permute-start | bytes 98312 | tf_op jit(solution)/shard_map/ppermute | solution.py:544
  326.2 7.9 %collective-permute-start.9 = (bf16[8,16,128]{2,0,1:T(8,128)(2,1)S(1)}, bf16[8,16,128]{2,0,1:T(8,128)(2,1)S(1)}, u32[]{:S(2)}, u32[]{:S(2)}) collective-permute-start(bf16[8,16,128]{2,0,1:T(8,128)(2,1)S(1)} %get-tuple-element.149), channel_id=1, source_target_pairs={{0,3},{1,2},{2,1},{3,0},{4,7},{5,6},{6,5},{7,4},{8,11},{9,10},{10,... | collective-permute-start | bytes 98312 | tf_op jit(solution)/shard_map/ppermute | solution.py:544
  340.2 1.0 copy-start.1
  347.1 3.8 %collective-permute-start.10 = (bf16[8,16,128]{2,1,0:T(8,128)(2,1)}, bf16[8,16,128]{2,1,0:T(8,128)(2,1)S(1)}, u32[]{:S(2)}, u32[]{:S(2)}) collective-permute-start(bf16[8,16,128]{2,1,0:T(8,128)(2,1)} %bitcast.219), channel_id=1, source_target_pairs={{0,1},{1,0},{2,3},{3,2},{4,5},{5,4},{6,7},{7,6},{8,9},{9,8},{10,11... | collective-permute-start | bytes 98312 | tf_op jit(solution)/shard_map/ppermute | solution.py:544
  348.4 3.0 collective-permute-start.11
  348.6 3.9 %collective-permute-start.12 = (bf16[8,16,128]{2,1,0:T(8,128)(2,1)}, bf16[8,16,128]{2,1,0:T(8,128)(2,1)S(1)}, u32[]{:S(2)}, u32[]{:S(2)}) collective-permute-start(bf16[8,16,128]{2,1,0:T(8,128)(2,1)} %bitcast.217), channel_id=1, source_target_pairs={{0,3},{1,2},{2,1},{3,0},{4,7},{5,6},{6,5},{7,4},{8,11},{9,10},{10,... | collective-permute-start | bytes 98312 | tf_op jit(solution)/shard_map/ppermute | solution.py:544

commit v10 on v9

--- a/solution.py
+++ b/solution.py
@@ -667,9 +667,12 @@
             (factors, scaled, back, pair_sum, mixed, closing, opening, weights, own_valid, place)
         )
     )
-    first, rest = factors[:64, None, 256:], factors[64:, None, 256:]
+    first = factors[:64, None, 256:]
     first_other = from_member(first, 2)
-    product, first_other = lax.optimization_barrier((run_product(factors), first_other))
+    product, first_other, factors = lax.optimization_barrier(
+        (run_product(factors), first_other, factors)
+    )
+    rest = factors[64:, None, 256:]
     prod = exchange(product).reshape(T, C, H, W)
     left, right = run_square(factors)
     prod, left, right, first, rest = lax.optimization_barrier((prod, left, right, first, rest))

time: 373 us -> 372 us (level)
  no operation moved by 1% of the time
where the time goes in v10:
time: 372 us; the launch traced here: 371 us
  waiting for transfers between devices  173 us (47%)
  Pallas kernels  100 us (27%)
  starting transfers between devices  48.1 us (13%)
  blocking collectives  17.7 us (5%)
  local copies, waits for them, and re-layouts  15.7 us (4%)
  other arithmetic  8.61 us (2%)
  matrix products  6.63 us (2%)
    all_to_all x5, waiting for transfers between devices, exchange(): return lax.all_to_all(value, AXES, split_axis=0, concat_axis=0, tiled=True)  162 us
    all_to_all x5, starting transfers between devices, exchange(): return lax.all_to_all(value, AXES, split_axis=0, concat_axis=0, tiled=True)  36.7 us
    pallas_call x1, Pallas kernels, run_gate(): pl.pallas_call(gate_kernel, grid=(T,), in_specs=[each_spec(C, H, W), each...  22.5 us
    all_to_all x1, blocking collectives, exchange(): return lax.all_to_all(value, AXES, split_axis=0, concat_axis=0, tiled=True)  17.7 us
    pallas_call x1, Pallas kernels, run_back(): pl.pallas_call(back_kernel, grid=(T,), in_specs=[*TERM_SPECS, each_spec(H...  16.7 us
    pallas_call x1, Pallas kernels, run_factor(): pl.pallas_call(factor_kernel, grid=(2,), in_specs=[pl.BlockSpec(memory_sp...  16.3 us
    pallas_call x1, Pallas kernels, run_norm(): pl.pallas_call(norm_kernel, grid=(T,), in_specs=[*TERM_SPECS, whole_spec(...  11.8 us
    ppermute x13, starting transfers between devices, from_member(): return lax.ppermute(value, 'col', [(i, i ^ k) for i in range(8)])  11.4 us
  transfers between devices with their start and end apart: 18, of which 12 were waited for; matrix products, arithmetic and copies ran while one was open for 6% of the time, Pallas kernels for 18%

profile of v10, /device:TPU:1, one launch (start us, length us, event | category | flops | bytes accessed | tf_op | source)
XLA Modules:
  0.0 371.2 jit_solution(5642255818108285942)
XLA Ops:
  0.6 1.6 broadcast_in_dim.43
  2.3 11.5 %all-to-all-start = ((bf16[128,16,128]{2,1,0:T(8,128)(2,1)}), bf16[128,16,128]{2,1,0:T(8,128)(2,1)S(1)}, u32[]{:S(2)}, u32[]{:S(2)}) async-start(bf16[128,16,128]{2,1,0:T(8,128)(2,1)} %bitcast.1), calls=%async_computation | async-start | bytes 1048576 | tf_op jit(solution)/shard_map/all_to_all | solution.py:552
  18.3 1.5 select_convert_fusion.1
  20.8 6.4 %all-to-all-done = bf16[128,16,128]{2,1,0:T(8,128)(2,1)S(1)} async-done(((bf16[128,16,128]{2,1,0:T(8,128)(2,1)}), bf16[128,16,128]{2,1,0:T(8,128)(2,1)S(1)}, u32[]{:S(2)}, u32[]{:S(2)}) %all-to-all-start) | async-done | bytes 524320 | tf_op jit(solution)/shard_map/all_to_all | solution.py:552
  29.0 1.5 collective-permute-start.2
  33.3 11.8 %pair_norm.1 = (bf16[4,32,272,128]{3,2,1,0:T(8,128)(2,1)}, f32[4,64,128]{2,1,0:T(8,128)}) custom-call(bf16[4,64,64,128]{3,2,1,0:T(8,128)(2,1)} %pair_ref.3, bf16[8,64,128]{2,1,0:T(8,128)(2,1)} %copy-done.3, bf16[8,64,128]{2,1,0:T(8,128)(2,1)} %copy-done.3, bf16[2,64,64]{2,1,0:T(8,128)(2,1)} %copy.29.embeds_ref, f32[2,4,1,128]{3,2,1,0:T(1,128)} %bitcast.192, ...), custom_call_target="tpu_custom_call" | custom-call | tf_op jit(solution)/shard_map/pair_norm/pallas_call | solution.py:130
  45.2 5.1 %all-to-all-start.1 = ((bf16[128,272,128]{2,1,0:T(8,128)(2,1)}), bf16[128,272,128]{2,1,0:T(8,128)(2,1)}, u32[]{:S(2)}, u32[]{:S(2)}) async-start(bf16[128,272,128]{2,1,0:T(8,128)(2,1)} %bitcast.181), calls=%async_computation.1 | async-start | bytes 17825792 | tf_op jit(solution)/shard_map/all_to_all | solution.py:552
  56.4 16.7 %back_project.1 = (bf16[4,64,64,128]{3,2,1,0:T(8,128)(2,1)}, bf16[4,64,64,128]{3,2,1,0:T(8,128)(2,1)}, f32[64,64,128]{2,1,0:T(8,128)}) custom-call(bf16[4,64,64,128]{3,2,1,0:T(8,128)(2,1)} %pair_ref.3, bf16[8,64,128]{2,1,0:T(8,128)(2,1)} %copy-done.3, bf16[8,64,128]{2,1,0:T(8,128)(2,1)} %copy-done.3, bf16[2,64,64]{2,1,0:T(8,128)(2,1)} %copy.29.embeds_ref, ...), custom_call_target="tpu_custom_call" | custom-call | flops 8589934592 | bytes 16777216 | tf_op jit(solution)/shard_map/back_project/pallas_call | solution.py:225
  73.1 82.8 %all-to-all-done.1.left_ref.right_ref = bf16[128,272,128]{2,1,0:T(8,128)(2,1)} async-done(((bf16[128,272,128]{2,1,0:T(8,128)(2,1)}), bf16[128,272,128]{2,1,0:T(8,128)(2,1)}, u32[]{:S(2)}, u32[]{:S(2)}) %all-to-all-start.1) | async-done | bytes 8912928 | tf_op jit(solution)/shard_map/all_to_all | solution.py:552
  156.9 8.4 %triangle_product.1 = bf16[128,128,128]{2,1,0:T(8,128)(2,1)} custom-call(bf16[128,272,128]{2,1,0:T(8,128)(2,1)} %all-to-all-done.1.left_ref.right_ref, bf16[128,272,128]{2,1,0:T(8,128)(2,1)} %all-to-all-done.1.left_ref.right_ref), custom_call_target="tpu_custom_call" | custom-call | tf_op jit(solution)/shard_map/triangle_product/pallas_call | solution.py:176
  165.3 10.2 %all-to-all-start.2 = ((bf16[128,128,128]{2,1,0:T(8,128)(2,1)}), bf16[128,128,128]{2,1,0:T(8,128)(2,1)}, u32[]{:S(2)}, u32[]{:S(2)}) async-start(bf16[128,128,128]{2,1,0:T(8,128)(2,1)} %triangle_product.1), calls=%async_computation.2 | async-start | bytes 8388608 | tf_op jit(solution)/shard_map/all_to_all | solution.py:552
  175.6 6.4 %to_matrices.1 = (bf16[2,1024,1024]{2,1,0:T(8,128)(2,1)}, bf16[2,1024,1024]{2,1,0:T(8,128)(2,1)}) custom-call(bf16[128,272,128]{2,1,0:T(8,128)(2,1)} %all-to-all-done.1.left_ref.right_ref, bf16[128,272,128]{2,1,0:T(8,128)(2,1)} %all-to-all-done.1.left_ref.right_ref), custom_call_target="tpu_custom_call" | custom-call | flops 1048576 | bytes 16777216 | tf_op jit(solution)/shard_map/to_matrices/pallas_call | solution.py:377
  182.9 45.5 %all-to-all-done.2 = bf16[128,128,128]{2,1,0:T(8,128)(2,1)} async-done(((bf16[128,128,128]{2,1,0:T(8,128)(2,1)}), bf16[128,128,128]{2,1,0:T(8,128)(2,1)}, u32[]{:S(2)}, u32[]{:S(2)}) %all-to-all-start.2) | async-done | bytes 4194336 | tf_op jit(solution)/shard_map/all_to_all | solution.py:552
  228.4 7.9 %product_grad.1 = bf16[4,64,64,128]{3,2,1,0:T(8,128)(2,1)} custom-call(bf16[4,64,64,128]{3,2,1,0:T(8,128)(2,1)} %bitcast.38.prod_ref, bf16[4,64,64,128]{3,2,1,0:T(8,128)(2,1)} %get-tuple-element.79.back_ref), custom_call_target="tpu_custom_call" | custom-call | flops 33554432 | bytes 12582912 | tf_op jit(solution)/shard_map/product_grad/pallas_call | solution.py:263
  236.3 5.9 %all-to-all-start.3 = ((bf16[128,128,128]{2,1,0:T(8,128)(2,1)}), bf16[128,128,128]{2,1,0:T(8,128)(2,1)}, u32[]{:S(2)}, u32[]{:S(2)}) async-start(bf16[128,128,128]{2,1,0:T(8,128)(2,1)} %bitcast.180), calls=%async_computation.3 | async-start | bytes 8388608 | tf_op jit(solution)/shard_map/all_to_all | solution.py:552
  242.4 1.4 collective-permute-start.5
  243.8 1.7 broadcast_select_fusion.6.pick_ref
  245.5 22.5 %gate_and_embed.1 = (bf16[64,64,128]{2,1,0:T(8,128)(2,1)}, f32[4,64,128]{2,1,0:T(8,128)}, f32[4,64,128]{2,1,0:T(8,128)}, f32[4,64,128]{2,1,0:T(8,128)}, f32[64,128]{1,0:T(8,128)}, /*index=5*/f32[64,128]{1,0:T(8,128)}) custom-call(bf16[4,64,64,128]{3,2,1,0:T(8,128)(2,1)} %bitcast.38.prod_ref, bf16[4,64,64,128]{3,2,1,0:T(8,128)(2,1)} %get-tuple-element.83.scaled_ref, ...), custom_call_target="tpu_custom_call" | custom-call | flops 8589934592 | bytes 12582912 | tf_op jit(solution)/shard_map/gate_and_embed/pallas_call | solution.py:343
  268.4 2.1 copy.36
  270.4 3.4 to_matrix.1.inv_ref
  273.8 21.3 %all-to-all-done.3.grad_ref = bf16[128,128,128]{2,1,0:T(8,128)(2,1)} async-done(((bf16[128,128,128]{2,1,0:T(8,128)(2,1)}), bf16[128,128,128]{2,1,0:T(8,128)(2,1)}, u32[]{:S(2)}, u32[]{:S(2)}) %all-to-all-start.3) | async-done | bytes 4194336 | tf_op jit(solution)/shard_map/all_to_all | solution.py:552
  295.2 16.3 %factor_grads.1 = (bf16[128,32,128]{2,1,0:T(8,128)(2,1)}, bf16[128,32,128]{2,1,0:T(8,128)(2,1)}, f32[2,2,8,1024]{3,2,1,0:T(8,128)}, f32[2,2,1024,128]{3,2,1,0:T(8,128)}) custom-call(s32[1]{0:T(128)} %bitcast.44.core_ref, bf16[2,1024,1024]{2,1,0:T(8,128)(2,1)} %get-tuple-element.97.left_ref, bf16[2,1024,1024]{2,1,0:T(8,128)(2,1)} %get-tuple-element.98.right_ref, ...), custom_call_target="tpu_custom_call" | custom-call | tf_op jit(solution)/shard_map/factor_grads/pallas_call | solution.py:454
  312.3 2.5 collective-permute-done.6.right_ref
  317.1 3.9 %all-to-all-start.4 = ((bf16[128,32,128]{2,1,0:T(8,128)(2,1)}), bf16[128,32,128]{2,1,0:T(8,128)(2,1)S(1)}, u32[]{:S(2)}, u32[]{:S(2)}) async-start(bf16[128,32,128]{2,1,0:T(8,128)(2,1)} %add_halves.1), calls=%async_computation.4 | async-start | bytes 2097152 | tf_op jit(solution)/shard_map/all_to_all | solution.py:552
  324.2 1.5 collective-permute-start.7
  327.4 2.1 fusion.2.base_ref
  329.5 1.9 collective-permute-done.8
  331.4 2.5 collective-permute-done.9
  334.0 6.1 %all-to-all-done.4 = bf16[128,32,128]{2,1,0:T(8,128)(2,1)S(1)} async-done(((bf16[128,32,128]{2,1,0:T(8,128)(2,1)}), bf16[128,32,128]{2,1,0:T(8,128)(2,1)S(1)}, u32[]{:S(2)}, u32[]{:S(2)}) %all-to-all-start.4) | async-done | bytes 1048608 | tf_op jit(solution)/shard_map/all_to_all | solution.py:552
  341.0 5.9 %close_sums.1 = (bf16[2,4,16,128]{3,2,1,0:T(8,128)(2,1)}, bf16[2,4,16,128]{3,2,1,0:T(8,128)(2,1)}, bf16[2,4,16,128]{3,2,1,0:T(8,128)(2,1)}, bf16[2,4,16,128]{3,2,1,0:T(8,128)(2,1)}) custom-call(bf16[4,16,2,32,128]{4,3,2,1,0:T(8,128)(2,1)} %bitcast.183, f32[4,64,128]{2,1,0:T(8,128)} %get-tuple-element.121.mean_ref, f32[4,64,128]{2,1,0:T(8,128)} %get-tuple-element.67.inv_ref, ...), custom_call_target="tpu_custom_call" | custom-call | tf_op jit(solution)/shard_map/close_sums/pallas_call | solution.py:529
  348.4 1.6 collective-permute-start.12
  352.7 17.7 %all_to_all.30 = bf16[128,16,128]{2,1,0:T(8,128)(2,1)S(1)} all-to-all(bf16[128,16,128]{2,1,0:T(8,128)(2,1)S(1)} %bitcast.185), channel_id=1, replica_groups=mesh['row'=16,'col'=8] {'row','col'}, dimensions={0} | all-to-all | bytes 1048576 | tf_op jit(solution)/shard_map/all_to_all | solution.py:552
  (114 shorter events, 32.2 us)
Async XLA Ops:
  2.3 25.0 %all-to-all-start = ((bf16[128,16,128]{2,1,0:T(8,128)(2,1)}), bf16[128,16,128]{2,1,0:T(8,128)(2,1)S(1)}, u32[]{:S(2)}, u32[]{:S(2)}) async-start(bf16[128,16,128]{2,1,0:T(8,128)(2,1)} %bitcast.1), calls=%async_computation | async-start | bytes 1048576 | tf_op jit(solution)/shard_map/all_to_all | solution.py:552
  27.6 2.9 collective-permute-start
  28.7 2.8 collective-permute-start.1
  29.0 3.7 collective-permute-start.2
  32.6 0.6 copy-start.3
  45.1 5.2 %copy-start.10 = (bf16[64]{0:T(256)(128)(2,1)S(1)}, bf16[64]{0:T(256)(128)(2,1)}, u32[]{:S(2)}) copy-start(bf16[64]{0:T(256)(128)(2,1)} %param.24) | copy-start | bytes 388
  45.1 5.2 %copy-start.7 = (bf16[64,64]{1,0:T(8,128)(2,1)S(1)}, bf16[64,64]{1,0:T(8,128)(2,1)}, u32[]{:S(2)}) copy-start(bf16[64,64]{1,0:T(8,128)(2,1)} %param.25) | copy-start | bytes 24580
  45.1 5.3 %copy-start.8 = (bf16[64,64]{1,0:T(8,128)(2,1)S(1)}, bf16[64,64]{1,0:T(8,128)(2,1)}, u32[]{:S(2)}) copy-start(bf16[64,64]{1,0:T(8,128)(2,1)} %param.26) | copy-start | bytes 24580
  45.1 5.4 %copy-start.4 = (bf16[64,64]{1,0:T(8,128)(2,1)S(1)}, bf16[64,64]{1,0:T(8,128)(2,1)}, u32[]{:S(2)}) copy-start(bf16[64,64]{1,0:T(8,128)(2,1)} %param.27) | copy-start | bytes 24580
  45.1 9.2 %copy-start.9 = (bf16[64,64]{1,0:T(8,128)(2,1)S(1)}, bf16[64,64]{1,0:T(8,128)(2,1)}, u32[]{:S(2)}) copy-start(bf16[64,64]{1,0:T(8,128)(2,1)} %param.28) | copy-start | bytes 24580
  45.2 9.3 %copy-start.11 = (bf16[512,64,1]{0,1,2:T(8,128)(2,1)S(1)}, bf16[512,64,1]{0,1,2:T(8,128)(2,1)}, u32[]{:S(2)}) copy-start(bf16[512,64,1]{0,1,2:T(8,128)(2,1)} %constant.178) | copy-start | bytes 196612
  45.2 110.7 %all-to-all-start.1 = ((bf16[128,272,128]{2,1,0:T(8,128)(2,1)}), bf16[128,272,128]{2,1,0:T(8,128)(2,1)}, u32[]{:S(2)}, u32[]{:S(2)}) async-start(bf16[128,272,128]{2,1,0:T(8,128)(2,1)} %bitcast.181), calls=%async_computation.1 | async-start | bytes 17825792 | tf_op jit(solution)/shard_map/all_to_all | solution.py:552
  156.8 8.5 %collective-permute-start.3 = (bf16[64,1,16,128]{3,2,0,1:T(8,128)(2,1)S(1)}, bf16[64,1,16,128]{3,2,0,1:T(8,128)(2,1)S(1)}, u32[]{:S(2)}, u32[]{:S(2)}) collective-permute-start(bf16[64,1,16,128]{3,2,0,1:T(8,128)(2,1)S(1)} %slice_bitcast_fusion.6), channel_id=1, source_target_pairs={{0,2},{1,3},{2,0},{3,1},{4,6},{5,7},{6,4},{7,5},{8,10},{9,11},{10,... | collective-permute-start | bytes 786440 | tf_op jit(solution)/shard_map/ppermute | solution.py:544
  165.3 63.0 %all-to-all-start.2 = ((bf16[128,128,128]{2,1,0:T(8,128)(2,1)}), bf16[128,128,128]{2,1,0:T(8,128)(2,1)}, u32[]{:S(2)}, u32[]{:S(2)}) async-start(bf16[128,128,128]{2,1,0:T(8,128)(2,1)} %triangle_product.1), calls=%async_computation.2 | async-start | bytes 8388608 | tf_op jit(solution)/shard_map/all_to_all | solution.py:552
  228.4 7.9 %collective-permute-start.4 = (bf16[64,1,16,128]{3,2,0,1:T(8,128)(2,1)S(1)}, bf16[64,1,16,128]{3,2,0,1:T(8,128)(2,1)S(1)}, u32[]{:S(2)}, u32[]{:S(2)}) collective-permute-start(bf16[64,1,16,128]{3,2,0,1:T(8,128)(2,1)S(1)} %slice_bitcast_fusion.5), channel_id=1, source_target_pairs={{0,2},{1,3},{2,0},{3,1},{4,6},{5,7},{6,4},{7,5},{8,10},{9,11},{10,... | collective-permute-start | bytes 786440 | tf_op jit(solution)/shard_map/ppermute | solution.py:544
  236.3 58.9 %all-to-all-start.3 = ((bf16[128,128,128]{2,1,0:T(8,128)(2,1)}), bf16[128,128,128]{2,1,0:T(8,128)(2,1)}, u32[]{:S(2)}, u32[]{:S(2)}) async-start(bf16[128,128,128]{2,1,0:T(8,128)(2,1)} %bitcast.180), calls=%async_computation.3 | async-start | bytes 8388608 | tf_op jit(solution)/shard_map/all_to_all | solution.py:552
  242.4 25.6 %collective-permute-start.5 = (bf16[128,2,1,16,128]{4,3,0,1,2:T(8,128)(2,1)S(1)}, bf16[128,2,1,16,128]{4,3,0,1,2:T(8,128)(2,1)S(1)}, u32[]{:S(2)}, u32[]{:S(2)}) collective-permute-start(bf16[128,2,1,16,128]{4,3,0,1,2:T(8,128)(2,1)S(1)} %maximum_bitcast_fusion), channel_id=1, source_target_pairs={{0,1},{1,0},{2,3},{3,2},{4,5},{5,4},{6,7},{7,6},{8,9},{9,8},{10,11... | collective-permute-start | bytes 3145736 | tf_op jit(solution)/shard_map/ppermute | solution.py:544
  295.1 25.9 %copy-start.6 = (f32[64,128]{1,0:T(8,128)S(1)}, f32[64,128]{1,0:T(8,128)}, u32[]{:S(2)}) copy-start(f32[64,128]{1,0:T(8,128)} %get-tuple-element.110) | copy-start | bytes 98308
  311.4 3.3 collective-permute-start.6
  314.8 1.2 copy-start
  316.0 7.0 %copy-start.2 = (f32[2,2,1024,128]{3,2,1,0:T(8,128)S(1)}, f32[2,2,1024,128]{3,2,1,0:T(8,128)}, u32[]{:S(2)}) copy-start(f32[2,2,1024,128]{3,2,1,0:T(8,128)} %get-tuple-element.113) | copy-start | bytes 6291460
  317.1 10.3 %copy-start.5 = (f32[2,4,128]{2,1,0:T(4,128)S(1)}, f32[2,4,128]{2,1,0:T(4,128)}, u32[]{:S(2)}) copy-start(f32[2,4,128]{2,1,0:T(4,128)} %add_convert_fusion) | copy-start | bytes 12292
  317.1 23.0 %all-to-all-start.4 = ((bf16[128,32,128]{2,1,0:T(8,128)(2,1)}), bf16[128,32,128]{2,1,0:T(8,128)(2,1)S(1)}, u32[]{:S(2)}, u32[]{:S(2)}) async-start(bf16[128,32,128]{2,1,0:T(8,128)(2,1)} %add_halves.1), calls=%async_computation.4 | async-start | bytes 2097152 | tf_op jit(solution)/shard_map/all_to_all | solution.py:552
  324.2 5.3 %collective-permute-start.7 = (bf16[8,16,128]{2,0,1:T(8,128)(2,1)S(1)}, bf16[8,16,128]{2,0,1:T(8,128)(2,1)S(1)}, u32[]{:S(2)}, u32[]{:S(2)}) collective-permute-start(bf16[8,16,128]{2,0,1:T(8,128)(2,1)S(1)} %get-tuple-element.151), channel_id=1, source_target_pairs={{0,1},{1,0},{2,3},{3,2},{4,5},{5,4},{6,7},{7,6},{8,9},{9,8},{10,11... | collective-permute-start | bytes 98312 | tf_op jit(solution)/shard_map/ppermute | solution.py:544
  325.7 5.7 %collective-permute-start.8 = (bf16[8,16,128]{2,0,1:T(8,128)(2,1)S(1)}, bf16[8,16,128]{2,0,1:T(8,128)(2,1)S(1)}, u32[]{:S(2)}, u32[]{:S(2)}) collective-permute-start(bf16[8,16,128]{2,0,1:T(8,128)(2,1)S(1)} %get-tuple-element.150), channel_id=1, source_target_pairs={{0,2},{1,3},{2,0},{3,1},{4,6},{5,7},{6,4},{7,5},{8,10},{9,11},{10,... | collective-permute-start | bytes 98312 | tf_op jit(solution)/shard_map/ppermute | solution.py:544
  326.1 7.9 %collective-permute-start.9 = (bf16[8,16,128]{2,0,1:T(8,128)(2,1)S(1)}, bf16[8,16,128]{2,0,1:T(8,128)(2,1)S(1)}, u32[]{:S(2)}, u32[]{:S(2)}) collective-permute-start(bf16[8,16,128]{2,0,1:T(8,128)(2,1)S(1)} %get-tuple-element.149), channel_id=1, source_target_pairs={{0,3},{1,2},{2,1},{3,0},{4,7},{5,6},{6,5},{7,4},{8,11},{9,10},{10,... | collective-permute-start | bytes 98312 | tf_op jit(solution)/shard_map/ppermute | solution.py:544
  340.1 1.0 copy-start.1
  346.9 3.8 %collective-permute-start.10 = (bf16[8,16,128]{2,1,0:T(8,128)(2,1)}, bf16[8,16,128]{2,1,0:T(8,128)(2,1)S(1)}, u32[]{:S(2)}, u32[]{:S(2)}) collective-permute-start(bf16[8,16,128]{2,1,0:T(8,128)(2,1)} %bitcast.219), channel_id=1, source_target_pairs={{0,1},{1,0},{2,3},{3,2},{4,5},{5,4},{6,7},{7,6},{8,9},{9,8},{10,11... | collective-permute-start | bytes 98312 | tf_op jit(solution)/shard_map/ppermute | solution.py:544
  348.3 3.0 collective-permute-start.11
  348.4 3.9 %collective-permute-start.12 = (bf16[8,16,128]{2,1,0:T(8,128)(2,1)}, bf16[8,16,128]{2,1,0:T(8,128)(2,1)S(1)}, u32[]{:S(2)}, u32[]{:S(2)}) collective-permute-start(bf16[8,16,128]{2,1,0:T(8,128)(2,1)} %bitcast.217), channel_id=1, source_target_pairs={{0,3},{1,2},{2,1},{3,0},{4,7},{5,6},{6,5},{7,4},{8,11},{9,10},{10,... | collective-permute-start | bytes 98312 | tf_op jit(solution)/shard_map/ppermute | solution.py:544
